TPU v7x, 128 devices: a whole 4x4x4 slice. The times are simulated.
128 devices in a mesh: gx: 4 (over x), gy: 32 (over y, z, core).
Axes of the slice: x: 4, y: 4, z: 4, core: 2. Of those that a mesh axis runs over, the one named last changes fastest.
Arguments:
- linearized_heat_field: float32 [32, 256, 128], P('gx', 'gy'), may hold values from -6 to 6
- local_rock_factor: float32 [32, 256, 128], P('gx', 'gy'), may hold values from 0.5 to 2
- misfit_heat_derivative: float32 [32, 256, 128], P('gx', 'gy'), may hold values from -6 to 6
- patch_region_map: int32 [32, 256, 1], P('gx', 'gy'), may hold values from 0 to 65535
- region_logarithmic_thermal: float32 [65536], P('gy'), may hold values from -2.5 to 2.5
- region_tally_per_rank: int32 [32], replicated, may hold values from 1 to 4096, 65536 in all
- region_adjacency_table: int32 [65536, 6], P('gy'), may hold values from 0 to 65535
Outputs:
- zone_gradient: float32 [131072], P('gy')
Inputs may be any that keep to these rules, and one draw needn't show every extreme that they name: `region_tally_per_rank`: the counts sum to 65536; some owner holds exactly 4096 zones.
All inputs are finite; a program needn't handle non-finite values.
Results may differ from a plain program's by a relative error of at most 0.00002.
Values sent between devices are 32-bit elements; how exact they have to be, the bound alone decides.
No kernel may reach another device: no remote copies, remote signals or barrier semaphores. Data moves between devices by JAX's collectives and lax.ppermute only.
A program may use at most 64 MiB of HBM per device.

v0:
```python
import jax
import jax.numpy as jnp
from jax import lax
from jax.sharding import PartitionSpec as P

NBRS = 6
ITERS = 3


relaxation = 0.8
smoothing = 0.5
sens_scale = 0.03125


def with_halo(cells, sides, width):
    for axis, dim in sides:
        count = lax.axis_size(axis)
        ends = count - 1
        head = lax.slice_in_dim(cells, 0, width, axis=dim)
        tail = lax.slice_in_dim(cells, cells.shape[dim] - width, cells.shape[dim], axis=dim)
        cells = jnp.concatenate(
            [
                lax.ppermute(tail, axis, [(i, (i + 1) % count) for i in range(ends)]),
                cells,
                lax.ppermute(head, axis, [((i + 1) % count, i) for i in range(ends)]),
            ],
            axis=dim,
        )
    return cells


def hexa_face_offsets(padded):
    return (
        padded[2:, 1:-1, 1:-1],
        padded[:-2, 1:-1, 1:-1],
        padded[1:-1, 2:, 1:-1],
        padded[1:-1, :-2, 1:-1],
        padded[1:-1, 1:-1, 2:],
        padded[1:-1, 1:-1, :-2],
    )


def conduct_parts(local_thermal_factor, padded_conduct):
    faces = tuple(
        ((local_thermal_factor + side) * 0.5 for side in hexa_face_offsets(padded_conduct))
    )
    diagonal = faces[0] + faces[1] + faces[2] + faces[3] + faces[4] + faces[5]
    return (faces, diagonal)


def jacobi_step(dual_solution, dual_padded_field, faces, diagonal, source):
    sides = hexa_face_offsets(dual_padded_field)
    coupled = faces[0] * sides[0]
    for number in range(1, 6):
        coupled = coupled + faces[number] * sides[number]
    applied = diagonal * dual_solution - coupled
    return dual_solution + relaxation * (source - applied) / diagonal


def local_misfit_derivative(
    linearized_heat_field, heat_padded_field, dual_solution, dual_padded_field, local_thermal_factor
):
    full_objective_derivative = jnp.zeros_like(linearized_heat_field)
    for heat_adjacent_values, dual_adjacent_values in zip(
        hexa_face_offsets(heat_padded_field), hexa_face_offsets(dual_padded_field)
    ):
        full_objective_derivative = full_objective_derivative + (
            linearized_heat_field - heat_adjacent_values
        ) * (dual_solution - dual_adjacent_values)
    return -0.5 * full_objective_derivative * local_thermal_factor


def dual_padded_field(field):
    bordered_array = with_halo(field, (("gx", 0), ("gy", 1)), 1)
    return jnp.pad(bordered_array, ((0, 0), (0, 0), (1, 1)))


def slot_of(zone_ids, region_tally_per_rank, capacity):
    owners = region_tally_per_rank.shape[0]
    ends = jnp.cumsum(region_tally_per_rank)
    starts = ends - region_tally_per_rank
    owner = jnp.sum((zone_ids[..., None] >= ends).astype(jnp.int32), axis=-1)
    ranks = jnp.arange(owners, dtype=jnp.int32)
    first = jnp.sum(jnp.where(owner[..., None] == ranks, starts, 0), axis=-1)
    return owner * capacity + zone_ids - first


def body(
    linearized_heat_field,
    local_rock_factor,
    misfit_heat_derivative,
    patch_region_map,
    region_logarithmic_thermal,
    region_tally_per_rank,
    region_adjacency_table,
):
    eastward_span, northward_span, vertical_layer_number = linearized_heat_field.shape
    blocks = patch_region_map.shape[2]
    zone_local = region_logarithmic_thermal.shape[0]
    capacity = 2 * zone_local
    owners = lax.axis_size("gy")
    zone_all = lax.all_gather(region_logarithmic_thermal, "gy", axis=0, tiled=True)
    zone_log = zone_all[patch_region_map]
    local_thermal_factor = (
        local_rock_factor.reshape(
            eastward_span, northward_span, blocks, vertical_layer_number // blocks
        )
        * jnp.exp(zone_log)[..., None]
    ).reshape(eastward_span, northward_span, vertical_layer_number)
    combined_contributions = jnp.stack([linearized_heat_field, local_thermal_factor])
    bordered_array = with_halo(combined_contributions, (("gx", 1), ("gy", 2)), 1)
    bordered_array = jnp.pad(bordered_array, ((0, 0), (0, 0), (0, 0), (1, 1)))
    heat_padded_field = bordered_array[0]
    faces, diagonal = conduct_parts(local_thermal_factor, bordered_array[1])
    dual_solution = misfit_heat_derivative / diagonal
    for sweep in range(ITERS):
        dual_solution = jacobi_step(
            dual_solution, dual_padded_field(dual_solution), faces, diagonal, misfit_heat_derivative
        )
    scaled_contributions = local_misfit_derivative(
        linearized_heat_field,
        heat_padded_field,
        dual_solution,
        dual_padded_field(dual_solution),
        local_thermal_factor,
    )
    block_sums = scaled_contributions.reshape(
        eastward_span, northward_span, blocks, vertical_layer_number // blocks
    ).sum(-1)
    block_slots = slot_of(patch_region_map.reshape(-1), region_tally_per_rank, capacity)
    neighbour_sum = jnp.sum(zone_all[region_adjacency_table], axis=-1)
    smooth_term = smoothing * (NBRS * region_logarithmic_thermal - neighbour_sum)
    smooth_term = jnp.where(lax.axis_index("gx") == 0, smooth_term, jnp.float32(0.0))
    own_zones = lax.axis_index("gy") * zone_local + jnp.arange(zone_local, dtype=jnp.int32)
    own_slots = slot_of(own_zones, region_tally_per_rank, capacity)
    values = jnp.concatenate([sens_scale * block_sums.reshape(-1), smooth_term])
    targets = jnp.concatenate([block_slots, own_slots])
    partial_sums = jax.ops.segment_sum(values, targets, num_segments=owners * capacity)
    column = lax.psum(partial_sums, "gx")
    totals = lax.psum_scatter(column, "gy", scatter_dimension=0, tiled=True)
    ranks = jnp.arange(owners, dtype=jnp.int32)
    held = jnp.sum(jnp.where(ranks == lax.axis_index("gy"), region_tally_per_rank, 0))
    within = jnp.arange(capacity, dtype=jnp.int32)
    return jnp.where(within < held, totals, jnp.float32(0.0))


def solution(mesh):
    placed = (
        P("gx", "gy", None),
        P("gx", "gy", None),
        P("gx", "gy", None),
        P("gx", "gy", None),
        P("gy"),
        P(),
        P("gy", None),
    )
    return jax.shard_map(body, mesh=mesh, in_specs=placed, out_specs=P("gy"), check_vma=False)
```

profile of v0, /device:TPU:1, one launch (start us, length us, event | category | flops | bytes accessed | tf_op | source)
XLA Modules:
  0.0 340.9 jit_solution(9935425160573528134)
XLA Ops:
  6.5 27.7 %all_gather.3 = f32[65536]{0:T(1024)S(1)} all-gather(f32[2048]{0:T(1024)} %param.11), channel_id=1, replica_groups=mesh['gx'=4,'gy'=32] {'gy'}, dimensions={0}, use_global_device_ids=true | all-gather | bytes 270336 | tf_op jit(solution)/shard_map/all_gather | solution.py:102
  34.8 1.3 fusion.72
  36.1 0.8 gather_fusion
  37.8 3.1 collective-permute-start
  40.9 1.3 collective-permute-start.1
  45.3 4.4 %collective-permute-start.2 = (f32[2,10,1,128]{3,2,1,0:T(1,128)S(1)}, f32[2,10,1,128]{3,2,1,0:T(1,128)S(1)}, u32[]{:S(2)}, u32[]{:S(2)}) collective-permute-start(f32[2,10,1,128]{3,2,1,0:T(1,128)S(1)} %get-tuple-element.16), channel_id=1, source_target_pairs={{0,1},{1,2},{2,3},{3,4},{4,5},{5,6},{6,7},{7,8},{8,9},{9,10},{10,1... | collective-permute-start | bytes 30728 | tf_op jit(solution)/shard_map/ppermute | solution.py:23
  49.7 1.9 collective-permute-start.3
  51.7 3.0 collective-permute-done.3
  55.9 1.3 collective-permute-start.4
  57.2 4.0 %collective-permute-start.5 = (f32[1,8,128]{2,1,0:T(8,128)S(1)}, f32[1,8,128]{2,1,0:T(8,128)S(1)}, u32[]{:S(2)}, u32[]{:S(2)}) collective-permute-start(f32[1,8,128]{2,1,0:T(8,128)S(1)} %get-tuple-element.34), channel_id=1, source_target_pairs={{0,32},{32,64},{64,96},{1,33},{33,65},{65,97},{2,34},{34,66},{66,9... | collective-permute-start | bytes 12296 | tf_op jit(solution)/shard_map/ppermute | solution.py:23
  61.9 1.9 collective-permute-start.6
  63.9 3.6 %collective-permute-start.7 = (f32[10,1,128]{2,1,0:T(1,128)S(1)}, f32[10,1,128]{2,1,0:T(1,128)S(1)}, u32[]{:S(2)}, u32[]{:S(2)}) collective-permute-start(f32[10,1,128]{2,1,0:T(1,128)S(1)} %get-tuple-element.26), channel_id=1, source_target_pairs={{0,1},{1,2},{2,3},{3,4},{4,5},{5,6},{6,7},{7,8},{8,9},{9,10},{10,1... | collective-permute-start | bytes 15368 | tf_op jit(solution)/shard_map/ppermute | solution.py:23
  69.2 1.3 collective-permute-start.8
  70.5 4.8 %collective-permute-start.9 = (f32[1,8,128]{2,1,0:T(8,128)}, f32[1,8,128]{2,1,0:T(8,128)}, u32[]{:S(2)}, u32[]{:S(2)}) collective-permute-start(f32[1,8,128]{2,1,0:T(8,128)} %get-tuple-element.32), channel_id=1, source_target_pairs={{0,32},{32,64},{64,96},{1,33},{33,65},{65,97},{2,34},{34,66},{66,9... | collective-permute-start | bytes 12296 | tf_op jit(solution)/shard_map/ppermute | solution.py:23
  75.9 68.0 %gather_fusion.1 = f32[12288]{0:T(1024)S(1)} fusion(f32[65536]{0:T(1024)S(1)} %all_gather.3, s32[12288]{0:T(1024)S(1)} %broadcast_clamp_fusion), kind=kCustom, calls=%fused_computation.1 | custom fusion | bytes 147456 | tf_op jit(solution)/shard_map/gather | solution.py:131
  143.9 1.0 reshape.67
  146.5 1.9 collective-permute-start.10
  148.4 4.5 %collective-permute-start.11 = (f32[10,1,128]{2,1,0:T(1,128)S(1)}, f32[10,1,128]{2,1,0:T(1,128)S(1)}, u32[]{:S(2)}, u32[]{:S(2)}) collective-permute-start(f32[10,1,128]{2,1,0:T(1,128)S(1)} %get-tuple-element.24), channel_id=1, source_target_pairs={{0,1},{1,2},{2,3},{3,4},{4,5},{5,6},{6,7},{7,8},{8,9},{9,10},{10,1... | collective-permute-start | bytes 15368 | tf_op jit(solution)/shard_map/ppermute | solution.py:23
  153.7 0.8 select_maximum_fusion.13
  154.6 0.8 fusion.41
  155.4 1.3 collective-permute-start.12
  156.7 4.0 %collective-permute-start.13 = (f32[1,8,128]{2,1,0:T(8,128)S(1)}, f32[1,8,128]{2,1,0:T(8,128)S(1)}, u32[]{:S(2)}, u32[]{:S(2)}) collective-permute-start(f32[1,8,128]{2,1,0:T(8,128)S(1)} %get-tuple-element.30), channel_id=1, source_target_pairs={{0,32},{32,64},{64,96},{1,33},{33,65},{65,97},{2,34},{34,66},{66,9... | collective-permute-start | bytes 12296 | tf_op jit(solution)/shard_map/ppermute | solution.py:23
  161.4 1.9 collective-permute-start.14
  163.3 5.3 %collective-permute-start.15 = (f32[10,1,128]{2,1,0:T(1,128)S(1)}, f32[10,1,128]{2,1,0:T(1,128)S(1)}, u32[]{:S(2)}, u32[]{:S(2)}) collective-permute-start(f32[10,1,128]{2,1,0:T(1,128)S(1)} %get-tuple-element.22), channel_id=1, source_target_pairs={{0,1},{1,2},{2,3},{3,4},{4,5},{5,6},{6,7},{7,8},{8,9},{9,10},{10,1... | collective-permute-start | bytes 15368 | tf_op jit(solution)/shard_map/ppermute | solution.py:23
  169.7 1.4 collective-permute-start.16
  171.1 4.5 %collective-permute-start.17 = (f32[1,8,128]{2,1,0:T(8,128)S(1)}, f32[1,8,128]{2,1,0:T(8,128)S(1)}, u32[]{:S(2)}, u32[]{:S(2)}) collective-permute-start(f32[1,8,128]{2,1,0:T(8,128)S(1)} %get-tuple-element.28), channel_id=1, source_target_pairs={{0,32},{32,64},{64,96},{1,33},{33,65},{65,97},{2,34},{34,66},{66,9... | collective-permute-start | bytes 12296 | tf_op jit(solution)/shard_map/ppermute | solution.py:23
  176.4 1.9 collective-permute-start.18
  178.3 5.0 %collective-permute-start.19 = (f32[10,1,128]{2,1,0:T(1,128)S(1)}, f32[10,1,128]{2,1,0:T(1,128)S(1)}, u32[]{:S(2)}, u32[]{:S(2)}) collective-permute-start(f32[10,1,128]{2,1,0:T(1,128)S(1)} %get-tuple-element.20), channel_id=1, source_target_pairs={{0,1},{1,2},{2,3},{3,4},{4,5},{5,6},{6,7},{7,8},{8,9},{9,10},{10,1... | collective-permute-start | bytes 15368 | tf_op jit(solution)/shard_map/ppermute | solution.py:23
  185.2 16.9 %scatter_custom_fusion = f32[131072]{0:T(1024)} fusion(s32[2112]{0:T(1024)S(1)} %pad_add_fusion, f32[2112]{0:T(1024)S(1)} %pad_maximum_fusion.32, f32[]{:T(128)} %constant.15.clone.1), kind=kCustom, calls=%fused_computation.14 | custom fusion | flops 2112 | bytes 524292 | tf_op jit(solution)/shard_map/scatter-add | solution.py:138
  204.0 115.1 %all-reduce.8.cloned.1.call-done = f32[131072]{0:T(1024)} async-done(((f32[131072]{0:T(1024)}), f32[131072]{0:T(1024)}) %all-reduce.8.cloned.1.call-update) | async-done | bytes 524304
  319.7 13.1 %psum.8 = f32[4096]{0:T(1024)S(1)} all-reduce(f32[4096]{0:T(1024)S(1)} %dynamic-slice-done), channel_id=1, replica_groups=mesh['gx'=4,'gy'=32] {'gx'}, use_global_device_ids=true, to_apply=%region_9.10 | all-reduce | flops 4096 | bytes 32768 | tf_op jit(solution)/shard_map/psum | solution.py:139
  332.8 1.2 fusion.71
  (139 shorter events, 16.9 us)
Async XLA Ops:
  6.5 312.5 %all-reduce.8.cloned.1.call-start = ((), (), s32[]{:S(2)}) async-start(), calls=%async_computation | async-start | bytes 1048576
  6.5 28.3 %copy-start.29 = (s32[8,8,1]{1,2,0:T(1,128)S(1)}, s32[8,8,1]{1,2,0:T(1,128)}, u32[]{:S(2)}) copy-start(s32[8,8,1]{1,2,0:T(1,128)} %param.10) | copy-start | bytes 772
  37.0 18.6 %copy-start.21 = (f32[8,8]{1,0:T(8,128)}, f32[8,8]{1,0:T(8,128)S(1)}, u32[]{:S(2)}) copy-start(f32[8,8]{1,0:T(8,128)S(1)} %reshape.85) | copy-start | bytes 772
  37.8 7.1 %collective-permute-start = (f32[2,1,8,128]{3,2,1,0:T(8,128)S(1)}, f32[2,1,8,128]{3,2,1,0:T(8,128)S(1)}, u32[]{:S(2)}, u32[]{:S(2)}) collective-permute-start(f32[2,1,8,128]{3,2,1,0:T(8,128)S(1)} %get-tuple-element.18), channel_id=1, source_target_pairs={{0,32},{32,64},{64,96},{1,33},{33,65},{65,97},{2,34},{34,66},{66,9... | collective-permute-start | bytes 24584 | tf_op jit(solution)/shard_map/ppermute | solution.py:23
  40.9 4.4 %collective-permute-start.1 = (f32[2,1,8,128]{3,2,1,0:T(8,128)S(1)}, f32[2,1,8,128]{3,2,1,0:T(8,128)S(1)}, u32[]{:S(2)}, u32[]{:S(2)}) collective-permute-start(f32[2,1,8,128]{3,2,1,0:T(8,128)S(1)} %get-tuple-element.19), channel_id=1, source_target_pairs={{32,0},{64,32},{96,64},{33,1},{65,33},{97,65},{34,2},{66,34},{98,6... | collective-permute-start | bytes 24584 | tf_op jit(solution)/shard_map/ppermute | solution.py:25
  44.2 17.0 %copy-start.27 = (s32[32]{0:T(128)}, s32[32]{0:T(128)S(1)}, u32[]{:S(2)}) copy-start(s32[32]{0:T(128)S(1)} %reduce.4) | copy-start | bytes 388
  44.9 22.6 %copy-start.31 = (s32[32]{0:T(128)}, s32[32]{0:T(128)S(1)}, u32[]{:S(2)}) copy-start(s32[32]{0:T(128)S(1)} %get-tuple-element.37) | copy-start | bytes 388
  45.3 6.3 %collective-permute-start.2 = (f32[2,10,1,128]{3,2,1,0:T(1,128)S(1)}, f32[2,10,1,128]{3,2,1,0:T(1,128)S(1)}, u32[]{:S(2)}, u32[]{:S(2)}) collective-permute-start(f32[2,10,1,128]{3,2,1,0:T(1,128)S(1)} %get-tuple-element.16), channel_id=1, source_target_pairs={{0,1},{1,2},{2,3},{3,4},{4,5},{5,6},{6,7},{7,8},{8,9},{9,10},{10,1... | collective-permute-start | bytes 30728 | tf_op jit(solution)/shard_map/ppermute | solution.py:23
  49.7 5.0 %collective-permute-start.3 = (f32[2,10,1,128]{3,2,1,0:T(1,128)S(1)}, f32[2,10,1,128]{3,2,1,0:T(1,128)S(1)}, u32[]{:S(2)}, u32[]{:S(2)}) collective-permute-start(f32[2,10,1,128]{3,2,1,0:T(1,128)S(1)} %get-tuple-element.17), channel_id=1, source_target_pairs={{1,0},{2,1},{3,2},{4,3},{5,4},{6,5},{7,6},{8,7},{9,8},{10,9},{11,1... | collective-permute-start | bytes 30728 | tf_op jit(solution)/shard_map/ppermute | solution.py:25
  55.8 12.6 %copy-start.7 = (f32[8,8,128]{2,1,0:T(8,128)}, f32[8,8,128]{2,1,0:T(8,128)S(1)}, u32[]{:S(2)}) copy-start(f32[8,8,128]{2,1,0:T(8,128)S(1)} %get-tuple-element.8) | copy-start | bytes 98308
  55.8 12.6 %copy-start.9 = (f32[8,8,128]{2,1,0:T(8,128)}, f32[8,8,128]{2,1,0:T(8,128)S(1)}, u32[]{:S(2)}) copy-start(f32[8,8,128]{2,1,0:T(8,128)S(1)} %get-tuple-element.9) | copy-start | bytes 98308
  55.9 12.6 %copy-start.11 = (f32[8,8,128]{2,1,0:T(8,128)}, f32[8,8,128]{2,1,0:T(8,128)S(1)}, u32[]{:S(2)}) copy-start(f32[8,8,128]{2,1,0:T(8,128)S(1)} %get-tuple-element.10) | copy-start | bytes 98308
  55.9 12.6 %copy-start.13 = (f32[8,8,128]{2,1,0:T(8,128)}, f32[8,8,128]{2,1,0:T(8,128)S(1)}, u32[]{:S(2)}) copy-start(f32[8,8,128]{2,1,0:T(8,128)S(1)} %get-tuple-element.11) | copy-start | bytes 98308
  55.9 12.6 %copy-start.15 = (f32[8,8,128]{2,1,0:T(8,128)}, f32[8,8,128]{2,1,0:T(8,128)S(1)}, u32[]{:S(2)}) copy-start(f32[8,8,128]{2,1,0:T(8,128)S(1)} %get-tuple-element.12) | copy-start | bytes 98308
  55.9 5.4 %collective-permute-start.4 = (f32[1,8,128]{2,1,0:T(8,128)S(1)}, f32[1,8,128]{2,1,0:T(8,128)S(1)}, u32[]{:S(2)}, u32[]{:S(2)}) collective-permute-start(f32[1,8,128]{2,1,0:T(8,128)S(1)} %get-tuple-element.35), channel_id=1, source_target_pairs={{32,0},{64,32},{96,64},{33,1},{65,33},{97,65},{34,2},{66,34},{98,6... | collective-permute-start | bytes 12296 | tf_op jit(solution)/shard_map/ppermute | solution.py:25
  57.2 4.7 %collective-permute-start.5 = (f32[1,8,128]{2,1,0:T(8,128)S(1)}, f32[1,8,128]{2,1,0:T(8,128)S(1)}, u32[]{:S(2)}, u32[]{:S(2)}) collective-permute-start(f32[1,8,128]{2,1,0:T(8,128)S(1)} %get-tuple-element.34), channel_id=1, source_target_pairs={{0,32},{32,64},{64,96},{1,33},{33,65},{65,97},{2,34},{34,66},{66,9... | collective-permute-start | bytes 12296 | tf_op jit(solution)/shard_map/ppermute | solution.py:23
  61.9 5.7 %collective-permute-start.6 = (f32[10,1,128]{2,1,0:T(1,128)S(1)}, f32[10,1,128]{2,1,0:T(1,128)S(1)}, u32[]{:S(2)}, u32[]{:S(2)}) collective-permute-start(f32[10,1,128]{2,1,0:T(1,128)S(1)} %get-tuple-element.27), channel_id=1, source_target_pairs={{1,0},{2,1},{3,2},{4,3},{5,4},{6,5},{7,6},{8,7},{9,8},{10,9},{11,1... | collective-permute-start | bytes 15368 | tf_op jit(solution)/shard_map/ppermute | solution.py:25
  63.9 4.4 %collective-permute-start.7 = (f32[10,1,128]{2,1,0:T(1,128)S(1)}, f32[10,1,128]{2,1,0:T(1,128)S(1)}, u32[]{:S(2)}, u32[]{:S(2)}) collective-permute-start(f32[10,1,128]{2,1,0:T(1,128)S(1)} %get-tuple-element.26), channel_id=1, source_target_pairs={{0,1},{1,2},{2,3},{3,4},{4,5},{5,6},{6,7},{7,8},{8,9},{9,10},{10,1... | collective-permute-start | bytes 15368 | tf_op jit(solution)/shard_map/ppermute | solution.py:23
  69.2 76.2 %collective-permute-start.8 = (f32[1,8,128]{2,1,0:T(8,128)}, f32[1,8,128]{2,1,0:T(8,128)}, u32[]{:S(2)}, u32[]{:S(2)}) collective-permute-start(f32[1,8,128]{2,1,0:T(8,128)} %get-tuple-element.33), channel_id=1, source_target_pairs={{32,0},{64,32},{96,64},{33,1},{65,33},{97,65},{34,2},{66,34},{98,6... | collective-permute-start | bytes 12296 | tf_op jit(solution)/shard_map/ppermute | solution.py:25
  70.5 74.9 %collective-permute-start.9 = (f32[1,8,128]{2,1,0:T(8,128)}, f32[1,8,128]{2,1,0:T(8,128)}, u32[]{:S(2)}, u32[]{:S(2)}) collective-permute-start(f32[1,8,128]{2,1,0:T(8,128)} %get-tuple-element.32), channel_id=1, source_target_pairs={{0,32},{32,64},{64,96},{1,33},{33,65},{65,97},{2,34},{34,66},{66,9... | collective-permute-start | bytes 12296 | tf_op jit(solution)/shard_map/ppermute | solution.py:23
  146.5 6.6 %collective-permute-start.10 = (f32[10,1,128]{2,1,0:T(1,128)S(1)}, f32[10,1,128]{2,1,0:T(1,128)S(1)}, u32[]{:S(2)}, u32[]{:S(2)}) collective-permute-start(f32[10,1,128]{2,1,0:T(1,128)S(1)} %get-tuple-element.25), channel_id=1, source_target_pairs={{1,0},{2,1},{3,2},{4,3},{5,4},{6,5},{7,6},{8,7},{9,8},{10,9},{11,1... | collective-permute-start | bytes 15368 | tf_op jit(solution)/shard_map/ppermute | solution.py:25
  148.4 5.2 %collective-permute-start.11 = (f32[10,1,128]{2,1,0:T(1,128)S(1)}, f32[10,1,128]{2,1,0:T(1,128)S(1)}, u32[]{:S(2)}, u32[]{:S(2)}) collective-permute-start(f32[10,1,128]{2,1,0:T(1,128)S(1)} %get-tuple-element.24), channel_id=1, source_target_pairs={{0,1},{1,2},{2,3},{3,4},{4,5},{5,6},{6,7},{7,8},{8,9},{9,10},{10,1... | collective-permute-start | bytes 15368 | tf_op jit(solution)/shard_map/ppermute | solution.py:23
  155.4 5.4 %collective-permute-start.12 = (f32[1,8,128]{2,1,0:T(8,128)S(1)}, f32[1,8,128]{2,1,0:T(8,128)S(1)}, u32[]{:S(2)}, u32[]{:S(2)}) collective-permute-start(f32[1,8,128]{2,1,0:T(8,128)S(1)} %get-tuple-element.31), channel_id=1, source_target_pairs={{32,0},{64,32},{96,64},{33,1},{65,33},{97,65},{34,2},{66,34},{98,6... | collective-permute-start | bytes 12296 | tf_op jit(solution)/shard_map/ppermute | solution.py:25
  156.7 4.7 %collective-permute-start.13 = (f32[1,8,128]{2,1,0:T(8,128)S(1)}, f32[1,8,128]{2,1,0:T(8,128)S(1)}, u32[]{:S(2)}, u32[]{:S(2)}) collective-permute-start(f32[1,8,128]{2,1,0:T(8,128)S(1)} %get-tuple-element.30), channel_id=1, source_target_pairs={{0,32},{32,64},{64,96},{1,33},{33,65},{65,97},{2,34},{34,66},{66,9... | collective-permute-start | bytes 12296 | tf_op jit(solution)/shard_map/ppermute | solution.py:23
  161.4 7.4 %collective-permute-start.14 = (f32[10,1,128]{2,1,0:T(1,128)S(1)}, f32[10,1,128]{2,1,0:T(1,128)S(1)}, u32[]{:S(2)}, u32[]{:S(2)}) collective-permute-start(f32[10,1,128]{2,1,0:T(1,128)S(1)} %get-tuple-element.23), channel_id=1, source_target_pairs={{1,0},{2,1},{3,2},{4,3},{5,4},{6,5},{7,6},{8,7},{9,8},{10,9},{11,1... | collective-permute-start | bytes 15368 | tf_op jit(solution)/shard_map/ppermute | solution.py:25
  163.3 6.1 %collective-permute-start.15 = (f32[10,1,128]{2,1,0:T(1,128)S(1)}, f32[10,1,128]{2,1,0:T(1,128)S(1)}, u32[]{:S(2)}, u32[]{:S(2)}) collective-permute-start(f32[10,1,128]{2,1,0:T(1,128)S(1)} %get-tuple-element.22), channel_id=1, source_target_pairs={{0,1},{1,2},{2,3},{3,4},{4,5},{5,6},{6,7},{7,8},{8,9},{9,10},{10,1... | collective-permute-start | bytes 15368 | tf_op jit(solution)/shard_map/ppermute | solution.py:23
  169.6 13.8 %copy-start.25 = (s32[2048]{0:T(1024)S(1)}, s32[2048]{0:T(1024)}, u32[]{:S(2)}) copy-start(s32[2048]{0:T(1024)} %add_subtract_fusion) | copy-start | bytes 24580
  169.7 14.6 %copy-start = (f32[10,10,130]{2,1,0:T(8,128)S(1)}, f32[10,10,130]{2,1,0:T(8,128)}, u32[]{:S(2)}) copy-start(f32[10,10,130]{2,1,0:T(8,128)} %get-tuple-element.14) | copy-start | bytes 156004
  169.7 6.0 %collective-permute-start.16 = (f32[1,8,128]{2,1,0:T(8,128)S(1)}, f32[1,8,128]{2,1,0:T(8,128)S(1)}, u32[]{:S(2)}, u32[]{:S(2)}) collective-permute-start(f32[1,8,128]{2,1,0:T(8,128)S(1)} %get-tuple-element.29), channel_id=1, source_target_pairs={{32,0},{64,32},{96,64},{33,1},{65,33},{97,65},{34,2},{66,34},{98,6... | collective-permute-start | bytes 12296 | tf_op jit(solution)/shard_map/ppermute | solution.py:25
  171.1 5.3 %collective-permute-start.17 = (f32[1,8,128]{2,1,0:T(8,128)S(1)}, f32[1,8,128]{2,1,0:T(8,128)S(1)}, u32[]{:S(2)}, u32[]{:S(2)}) collective-permute-start(f32[1,8,128]{2,1,0:T(8,128)S(1)} %get-tuple-element.28), channel_id=1, source_target_pairs={{0,32},{32,64},{64,96},{1,33},{33,65},{65,97},{2,34},{34,66},{66,9... | collective-permute-start | bytes 12296 | tf_op jit(solution)/shard_map/ppermute | solution.py:23
  176.4 7.1 %collective-permute-start.18 = (f32[10,1,128]{2,1,0:T(1,128)S(1)}, f32[10,1,128]{2,1,0:T(1,128)S(1)}, u32[]{:S(2)}, u32[]{:S(2)}) collective-permute-start(f32[10,1,128]{2,1,0:T(1,128)S(1)} %get-tuple-element.21), channel_id=1, source_target_pairs={{1,0},{2,1},{3,2},{4,3},{5,4},{6,5},{7,6},{8,7},{9,8},{10,9},{11,1... | collective-permute-start | bytes 15368 | tf_op jit(solution)/shard_map/ppermute | solution.py:25
  178.3 5.8 %collective-permute-start.19 = (f32[10,1,128]{2,1,0:T(1,128)S(1)}, f32[10,1,128]{2,1,0:T(1,128)S(1)}, u32[]{:S(2)}, u32[]{:S(2)}) collective-permute-start(f32[10,1,128]{2,1,0:T(1,128)S(1)} %get-tuple-element.20), channel_id=1, source_target_pairs={{0,1},{1,2},{2,3},{3,4},{4,5},{5,6},{6,7},{7,8},{8,9},{9,10},{10,1... | collective-permute-start | bytes 15368 | tf_op jit(solution)/shard_map/ppermute | solution.py:23
  (24 other events, 69.4 us)
Sparse Core Ops, SparseCore 0:
  202.2 116.7 all-reduce.7
where the time goes:
time: 345 us; the launch traced here: 341 us
  waiting for transfers between devices  123 us (36%)
  local copies, waits for them, and re-layouts  77.4 us (22%)
  starting transfers between devices  59.5 us (17%)
  blocking collectives  40.8 us (12%)
  other arithmetic  25.4 us (7%)
  between operations  14.8 us (4%)
    unnamed x2, waiting for transfers between devices  115 us
    gather x2, local copies, waits for them, and re-layouts, body(): neighbour_sum = jnp.sum(zone_all[region_adjacency_table], axis=-1)  69.1 us
    ppermute x10, starting transfers between devices, with_halo(): lax.ppermute(tail, axis, [(i, (i + 1) % count) for i in range(ends)])  43.3 us
    all_gather x1, blocking collectives, body(): lax.all_gather(region_logarithmic_thermal, 'gy', axis=0, tiled=True)  27.7 us
    scatter-add x1, other arithmetic, body(): jax.ops.segment_sum(values, targets, num_segments=owners * capacity)  16.9 us
    ppermute x10, starting transfers between devices, with_halo(): lax.ppermute(head, axis, [((i + 1) % count, i) for i in range(ends)])  16.2 us
    psum x1, blocking collectives, body(): column = lax.psum(partial_sums, 'gx')  13.1 us
  transfers between devices with their start and end apart: 21, of which 10 were waited for; matrix products, arithmetic and copies ran while one was open for 21% of the time, Pallas kernels for 0%

commit v1 on v0

v1 whole, which is shorter than its diff:
```python
import jax
import jax.numpy as jnp
from jax import lax
from jax.experimental import pallas as pl
from jax.experimental.pallas import tpu as pltpu
from jax.sharding import PartitionSpec as P

NBRS = 6
ITERS = 3
RELAXATION = 0.8
SMOOTHING = 0.5
SENS_SCALE = 0.03125
LANES = 128
F32 = jnp.float32
BF16 = jnp.bfloat16
I32 = jnp.int32

VMEM = pl.BlockSpec(memory_space=pltpu.VMEM)
SMEM = pl.BlockSpec(memory_space=pltpu.SMEM)


def iota(shape, dim):
    return lax.broadcasted_iota(I32, shape, dim)


def call(kernel, outs, in_specs, scratch=(), cost=None):
    one = not isinstance(outs, (list, tuple))
    shapes = [outs] if one else list(outs)
    return pl.pallas_call(
        kernel,
        out_shape=shapes[0] if one else shapes,
        in_specs=in_specs,
        out_specs=VMEM if one else [VMEM] * len(shapes),
        scratch_shapes=list(scratch),
        cost_estimate=cost,
        compiler_params=pltpu.CompilerParams(vmem_limit_bytes=32 << 20),
    )


def thirds(table):
    first = table.astype(BF16)
    rest = table - first.astype(F32)
    second = rest.astype(BF16)
    third = (rest - second.astype(F32)).astype(BF16)
    return first, second, third


def pack_kernel(temp_ref, rock_ref, misfit_ref, map_ref, zone_ref, pack_ref, spread_ref):
    pack_ref[0] = rock_ref[...]
    pack_ref[1] = misfit_ref[...]
    pack_ref[2] = temp_ref[...]
    east, north = rock_ref.shape[0], rock_ref.shape[1]
    diagonal = iota((north, north), 0) == iota((north, north), 1)
    for x in range(east):
        row = jnp.broadcast_to(map_ref[x].astype(F32), (north, north))
        column = jnp.sum(jnp.where(diagonal, row, 0.0), axis=1, keepdims=True)
        pack_ref[3, x] = jnp.broadcast_to(column, (north, LANES))
    shard = zone_ref[...]
    for other in range(spread_ref.shape[0]):
        spread_ref[other] = shard


def extend_kernel(own_ref, south_ref, north_ref, table_ref, ext_ref, low_ref, high_ref):
    east = own_ref.shape[1]

    def window(field):
        return jnp.concatenate([south_ref[field], own_ref[field], north_ref[field]], axis=1)

    ids = window(3).reshape(east * 24, LANES).astype(I32)
    rows = ids >> 7
    lane = iota((east * 24, LANES), 1)
    hot = jnp.concatenate(
        [jnp.where(rows == lane + LANES * part, 1.0, 0.0).astype(BF16) for part in range(table_ref.shape[0] // LANES)],
        axis=1,
    )
    found = sum(jnp.dot(hot, piece, preferred_element_type=F32) for piece in thirds(table_ref[...]))
    log = jnp.sum(jnp.where(lane == (ids & 127), found, 0.0), axis=1, keepdims=True)
    conduct = window(0) * jnp.exp(jnp.broadcast_to(log, (east * 24, LANES))).reshape(east, 24, LANES)
    inner = conduct[:, 4:20]
    misfit, temp = window(1)[:, 4:20], window(2)[:, 4:20]
    ext_ref[0] = inner
    ext_ref[1] = conduct[:, 3:19] + conduct[:, 5:21]
    ext_ref[2] = misfit
    ext_ref[3] = temp
    low_ref[0:5] = inner[0:5]
    low_ref[5:9] = misfit[0:4]
    low_ref[9:10] = temp[0:1]
    high_ref[0:5] = inner[3:8]
    high_ref[5:9] = misfit[4:8]
    high_ref[9:10] = temp[7:8]


def smooth_kernel(gx_ref, adjacency_ref, zone_ref, table_ref, after_ref, out_ref):
    rows = out_ref.shape[0]
    count = rows * LANES
    high_size = table_ref.shape[0]
    pieces = jnp.concatenate(thirds(jnp.transpose(table_ref[...])), axis=0)
    offset = pl.multiple_of(gx_ref[0] * count, count)
    high_row = iota((high_size, count), 0)
    low_row = iota((LANES, count), 0)
    total = jnp.zeros((LANES, count), F32)
    for k in range(NBRS):
        ids = adjacency_ref[k : k + 1, pl.ds(offset, count)]
        hot = jnp.where(high_row == (ids >> 7), 1.0, 0.0).astype(BF16)
        found = jnp.dot(pieces, hot, preferred_element_type=F32)
        found = found[0:LANES] + found[LANES : 2 * LANES] + found[2 * LANES :]
        total = total + jnp.where(low_row == (ids & 127), found, 0.0)
    near = jnp.sum(total, axis=0, keepdims=True)
    own = zone_ref[pl.ds(gx_ref[0] * rows, rows), :]
    for row in range(rows):
        out_ref[row : row + 1] = SMOOTHING * (
            NBRS * own[row : row + 1] - near[:, row * LANES : (row + 1) * LANES]
        )


def sweep_kernel(ext_ref, west_ref, east_ref, ids_ref, smooth_ref, out_ref):
    shape = (16, LANES)
    lane = iota(shape, 1)
    first, last = lane == 0, lane == LANES - 1

    def depth_sides(v):
        up = jnp.where(first, 0.0, pltpu.roll(v, 1, 1))
        down = jnp.where(last, 0.0, pltpu.roll(v, LANES - 1, 1))
        return up, down

    def north_sides(v):
        return pltpu.roll(v, 1, 0), pltpu.roll(v, 15, 0)

    def around(rows, x):
        v = rows[x]
        up, down = depth_sides(v)
        south, north = north_sides(v)
        return ((rows[x - 1] + rows[x + 1]) + (south + north)) + (up + down)

    conduct = {x: ext_ref[0, x] for x in range(8)}
    source = {x: ext_ref[2, x] for x in range(8)}
    heat = {x: ext_ref[3, x] for x in range(8)}
    for step in range(5):
        conduct[step - 5] = west_ref[step]
        conduct[step + 8] = east_ref[step]
    for step in range(4):
        source[step - 4] = west_ref[5 + step]
        source[step + 8] = east_ref[5 + step]
    heat[-1] = west_ref[9]
    heat[8] = east_ref[9]

    inverse, dual, flux = {}, {}, {}
    for x in range(-4, 12):
        v = conduct[x]
        if 0 <= x < 8:
            across = ext_ref[1, x]
        else:
            south, north = north_sides(v)
            across = south + north
        up, down = depth_sides(v)
        twice = 6.0 * v + (((conduct[x - 1] + conduct[x + 1]) + across) + (up + down))
        inverse[x] = jnp.where(v > 0.0, 2.0 / twice, 0.0)
        dual[x] = source[x] * inverse[x]
    for sweep in range(ITERS):
        reach = 3 - sweep
        flux = {x: conduct[x] * dual[x] for x in dual}
        fresh = {}
        for x in range(-reach, 8 + reach):
            coupled = 0.5 * (conduct[x] * around(dual, x) + around(flux, x))
            fresh[x] = (1.0 - RELAXATION) * dual[x] + (RELAXATION * inverse[x]) * (source[x] + coupled)
        dual = fresh
    blocks = []
    for x in range(8):
        t, v = heat[x], dual[x]
        total = (t - heat[x + 1]) * (v - dual[x + 1]) + (t - heat[x - 1]) * (v - dual[x - 1])
        for near_t, near_v in zip(north_sides(t) + depth_sides(t), north_sides(v) + depth_sides(v)):
            total = total + (t - near_t) * (v - near_v)
        blocks.append(((-0.5 * SENS_SCALE) * total * conduct[x])[4:12])
    stacked = jnp.concatenate(blocks + [ids_ref[3, x] for x in range(8)], axis=0)
    turned = jnp.transpose(stacked)
    sums = jnp.sum(turned, axis=0, keepdims=True)
    row = jnp.where(iota((1, LANES), 1) < 64, sums, turned[0:1])
    tile = jnp.concatenate([smooth_ref[...], row, jnp.zeros((3, LANES), F32)], axis=0)
    for other in range(out_ref.shape[0]):
        out_ref[other] = tile


def place_kernel(gy_ref, tally_ref, all_ref, out_ref, smooth_ref, hot_ref, low_ref):
    me = gy_ref[0]
    start = jnp.int32(0)
    for other in range(tally_ref.shape[0]):
        start = start + jnp.where(other < me, tally_ref[other], 0)
    held = tally_ref[me]
    sources = all_ref.shape[0]
    half = sources // 2
    both = all_ref[:, 4, :]
    turned = pltpu.roll(both, 64, 1)
    left = iota((half, LANES), 1) < 64
    values = jnp.where(left, both[:half], turned[half:])
    slots = jnp.where(left, turned[:half], both[half:]).astype(I32) - start
    pieces = [piece.astype(F32) for piece in thirds(values)]
    high, low = slots >> 7, slots & 127
    slot_rows = out_ref.shape[0]
    high_row = iota((slot_rows, LANES), 0)
    low_row = iota((LANES, LANES), 0)
    for row in range(half):
        match = high_row == high[row : row + 1]
        for number in range(3):
            hot_ref[number * slot_rows : (number + 1) * slot_rows, row * LANES : (row + 1) * LANES] = jnp.where(
                match, pieces[number][row : row + 1], 0.0
            ).astype(BF16)
        low_ref[:, row * LANES : (row + 1) * LANES] = jnp.where(low_row == low[row : row + 1], 1.0, 0.0).astype(BF16)
    sums = lax.dot_general(hot_ref[...], low_ref[...], (((1,), (1,)), ((), ())), preferred_element_type=F32)
    sums = sums[0:slot_rows] + sums[slot_rows : 2 * slot_rows] + sums[2 * slot_rows :]

    top, shift = start >> 7, start & 127
    for row in range(slot_rows + 1):
        zone_row = jnp.minimum(top + row, sources * 4 - 1)
        smooth_ref[row : row + 1, :] = all_ref[zone_row >> 2, pl.ds(zone_row & 3, 1), :]
    moved = pltpu.roll(smooth_ref[...], LANES - shift, 1)
    lane = iota((slot_rows, LANES), 1)
    smooth = jnp.where(lane < LANES - shift, moved[0:slot_rows], moved[1 : slot_rows + 1])
    within = iota((slot_rows, LANES), 0) * LANES + lane
    out_ref[...] = jnp.where(within < held, sums + smooth, 0.0)


def body(temp, rock, misfit, zone_map, zone_log, tally, adjacency):
    east, north, depth = temp.shape
    across, along = lax.axis_size("gx"), lax.axis_size("gy")
    shard_rows = zone_log.shape[0] // LANES
    zone = zone_log.reshape(shard_rows, LANES)
    gx = lax.axis_index("gx").astype(I32).reshape(1)
    gy = lax.axis_index("gy").astype(I32).reshape(1)

    def move(array, axis, by):
        count = lax.axis_size(axis)
        return lax.ppermute(array, axis, [(i, i + by) for i in range(count) if 0 <= i + by < count])

    shape = jax.ShapeDtypeStruct
    pack, spread = call(
        pack_kernel,
        [shape((4, east, north, depth), F32), shape((along, shard_rows, LANES), F32)],
        [VMEM] * 5,
    )(temp, rock, misfit, jnp.transpose(zone_map, (0, 2, 1)), zone)
    from_south, from_north = move(pack, "gy", 1), move(pack, "gy", -1)
    table = lax.all_to_all(spread, "gy", 0, 0, tiled=True).reshape(along * shard_rows, LANES)
    ext, low, high = call(
        extend_kernel,
        [shape((4, 8, 16, LANES), F32), shape((10, 16, LANES), F32), shape((10, 16, LANES), F32)],
        [VMEM] * 4,
    )(pack, from_south, from_north, table)
    from_west, from_east = move(high, "gx", 1), move(low, "gx", -1)
    smooth = call(
        smooth_kernel,
        shape((shard_rows // across, LANES), F32),
        [SMEM] + [VMEM] * 3 + [pl.BlockSpec(memory_space=pl.ANY)],
        cost=pl.CostEstimate(flops=1 << 32, bytes_accessed=1 << 20, transcendentals=0),
    )(gx, jnp.transpose(adjacency), zone, table, ext)
    tile = call(sweep_kernel, shape((across * along, 8, LANES), F32), [VMEM] * 5)(
        ext, from_west, from_east, pack, smooth
    )
    gathered = lax.all_to_all(tile, ("gy", "gx"), 0, 0, tiled=True)
    slot_rows = 2 * shard_rows
    out = call(
        place_kernel,
        shape((slot_rows, LANES), F32),
        [SMEM, SMEM, VMEM],
        [
            pltpu.VMEM((slot_rows + 8, LANES), F32),
            pltpu.VMEM((3 * slot_rows, across * along * 64), BF16),
            pltpu.VMEM((LANES, across * along * 64), BF16),
        ],
    )(gy, tally, gathered)
    return out.reshape(slot_rows * LANES)


def solution(mesh):
    placed = (
        P("gx", "gy", None),
        P("gx", "gy", None),
        P("gx", "gy", None),
        P("gx", "gy", None),
        P("gy"),
        P(),
        P("gy", None),
    )
    return jax.shard_map(body, mesh=mesh, in_specs=placed, out_specs=P("gy"), check_vma=False)
```

time: 345 us -> 62.6 us (0.18); the launches traced: 341 us -> 62 us
  waiting for transfers between devices: 123 us -> 19.8 us
  local copies, waits for them, and re-layouts: 77.4 us -> 3.67 us
  blocking collectives: 40.8 us -> 0 us
  starting transfers between devices: 59.5 us -> 31.4 us
  other arithmetic: 25.4 us -> 0 us
  between operations: 14.8 us -> 0.12 us
  Pallas kernels: 0 us -> 7.11 us
    unnamed x2 -> x0, waiting for transfers between devices: 115 us -> none
    gather x3 -> x0, local copies, waits for them, and re-layouts: 69.8 us -> none  [the longest x2 69.1 us: body(): neighbour_sum = jnp.sum(zone_all[region_adjacency_table], axis=-1)]
    ppermute x20 -> x4, starting transfers between devices: 59.5 us -> 9.97 us  [move(): lax.ppermute(array, axis, [(i, i + by) for i in range(count) if 0 <= i +...]
    all_gather x1 -> x0, blocking collectives: 27.7 us -> none  [body(): lax.all_gather(region_logarithmic_thermal, 'gy', axis=0, tiled=True)]
    all_to_all x0 -> x2, starting transfers between devices: none -> 21.4 us  [the longest x1 11.8 us: body(): gathered = lax.all_to_all(tile, ('gy', 'gx'), 0, 0, tiled=True)]
    scatter-add x1 -> x0, other arithmetic: 16.9 us -> none  [body(): jax.ops.segment_sum(values, targets, num_segments=owners * capacity)]
    all_to_all x0 -> x2, waiting for transfers between devices: none -> 15 us  [the longest x1 14.1 us: body(): gathered = lax.all_to_all(tile, ('gy', 'gx'), 0, 0, tiled=True)]
    psum x1 -> x0, blocking collectives: 13.1 us -> none  [body(): column = lax.psum(partial_sums, 'gx')]
  transfers between devices with their start and end apart: 21 -> 6, of which waited for: 10 -> 4; matrix products, arithmetic and copies ran while one was open for 21% -> 0% of each run, Pallas kernels for 0% -> 3%
where the time goes in v1:
time: 62.6 us; the launch traced here: 62 us
  starting transfers between devices  31.4 us (50%)
  waiting for transfers between devices  19.8 us (32%)
  Pallas kernels  7.11 us (11%)
  local copies, waits for them, and re-layouts  3.67 us (6%)
    all_to_all x1, waiting for transfers between devices, body(): gathered = lax.all_to_all(tile, ('gy', 'gx'), 0, 0, tiled=True)  14.1 us
    all_to_all x1, starting transfers between devices, body(): gathered = lax.all_to_all(tile, ('gy', 'gx'), 0, 0, tiled=True)  11.8 us
    ppermute x4, starting transfers between devices, move(): lax.ppermute(array, axis, [(i, i + by) for i in range(count) if 0 <= i +...  9.97 us
    all_to_all x1, starting transfers between devices, body(): lax.all_to_all(spread, 'gy', 0, 0, tiled=True)  9.6 us
    ppermute x4, waiting for transfers between devices, move(): lax.ppermute(array, axis, [(i, i + by) for i in range(count) if 0 <= i +...  4.72 us
    unnamed x16, local copies, waits for them, and re-layouts  3.67 us
    pallas_call x1, Pallas kernels, body(): call(place_kernel, shape((slot_rows, LANES), F32), [SMEM, SMEM, VMEM], [p...  2.89 us
    pallas_call x1, Pallas kernels, body(): call(smooth_kernel, shape((shard_rows // across, LANES), F32), [SMEM] + [...  1.61 us
  transfers between devices with their start and end apart: 6, of which 4 were waited for; matrix products, arithmetic and copies ran while one was open for 0% of the time, Pallas kernels for 3%

profile of v1, /device:TPU:1, one launch (start us, length us, event | category | flops | bytes accessed | tf_op | source)
XLA Modules:
  0.0 62.0 jit_solution(7819926954639945201)
XLA Ops:
  0.0 0.0 copy-start
  0.0 0.8 %copy-done = f32[8,8,128]{2,1,0:T(8,128)S(1)} copy-done((f32[8,8,128]{2,1,0:T(8,128)S(1)}, f32[8,8,128]{2,1,0:T(8,128)}, u32[]{:S(2)}) %copy-start) | copy-done | bytes 32792
  0.8 0.0 copy-start.1
  0.8 0.8 %copy-done.1 = f32[8,8,128]{2,1,0:T(8,128)S(1)} copy-done((f32[8,8,128]{2,1,0:T(8,128)S(1)}, f32[8,8,128]{2,1,0:T(8,128)}, u32[]{:S(2)}) %copy-start.1) | copy-done | bytes 32792
  1.5 0.0 copy-start.2
  1.5 0.8 %copy-done.2 = f32[8,8,128]{2,1,0:T(8,128)S(1)} copy-done((f32[8,8,128]{2,1,0:T(8,128)S(1)}, f32[8,8,128]{2,1,0:T(8,128)}, u32[]{:S(2)}) %copy-start.2) | copy-done | bytes 32792
  2.3 0.0 copy-start.3
  2.3 0.7 %copy-done.3 = f32[2048]{0:T(1024)S(1)} copy-done((f32[2048]{0:T(1024)S(1)}, f32[2048]{0:T(1024)}, u32[]{:S(2)}) %copy-start.3) | copy-done | bytes 8216
  3.0 0.0 copy-start.5
  3.0 0.7 %copy-done.5 = s32[8,8,1]{1,2,0:T(1,128)S(1)} copy-done((s32[8,8,1]{1,2,0:T(1,128)S(1)}, s32[8,8,1]{1,2,0:T(1,128)}, u32[]{:S(2)}) %copy-start.5) | copy-done | bytes 280
  3.7 0.7 %shard_map.73 = (f32[4,8,8,128]{3,2,1,0:T(8,128)S(1)}, f32[32,16,128]{2,1,0:T(8,128)}) custom-call(f32[8,8,128]{2,1,0:T(8,128)S(1)} %copy-done, f32[8,8,128]{2,1,0:T(8,128)S(1)} %copy-done.1, f32[8,8,128]{2,1,0:T(8,128)S(1)} %copy-done.2, s32[8,1,8]{2,1,0:T(1,128)S(1)} %bitcast.13, f32[16,128]{1,0:T(8,128)S(1)} %bitcast.11), custom_call_target="tpu_custom_call" | custom-call | tf_op jit(solution)/shard_map/pallas_call | solution.py:235
  4.4 9.6 %all-to-all-start = ((f32[32,16,128]{2,1,0:T(8,128)}), f32[32,16,128]{2,1,0:T(8,128)S(1)}, u32[]{:S(2)}, u32[]{:S(2)}) async-start(f32[32,16,128]{2,1,0:T(8,128)} %get-tuple-element.11), calls=%async_computation | async-start | bytes 524288 | tf_op jit(solution)/shard_map/all_to_all | solution.py:241
  14.0 2.1 %collective-permute-start.1 = (f32[4,8,8,128]{3,2,1,0:T(8,128)S(1)}, f32[4,8,8,128]{3,2,1,0:T(8,128)S(1)}, u32[]{:S(2)}, u32[]{:S(2)}) collective-permute-start(f32[4,8,8,128]{3,2,1,0:T(8,128)S(1)} %get-tuple-element.10.own_ref.ids_ref), channel_id=1, source_target_pairs={{1,0},{2,1},{3,2},{4,3},{5,4},{6,5},{7,6},{8,7},{9,8},{10,9},{11,1... | collective-permute-start | bytes 393224 | tf_op jit(solution)/shard_map/ppermute | solution.py:232
  16.1 3.4 %collective-permute-start = (f32[4,8,8,128]{3,2,1,0:T(8,128)S(1)}, f32[4,8,8,128]{3,2,1,0:T(8,128)S(1)}, u32[]{:S(2)}, u32[]{:S(2)}) collective-permute-start(f32[4,8,8,128]{3,2,1,0:T(8,128)S(1)} %get-tuple-element.10.own_ref.ids_ref), channel_id=1, source_target_pairs={{0,1},{1,2},{2,3},{3,4},{4,5},{5,6},{6,7},{7,8},{8,9},{9,10},{10,1... | collective-permute-start | bytes 393224 | tf_op jit(solution)/shard_map/ppermute | solution.py:232
  19.6 2.5 %collective-permute-done.1.north_ref = f32[4,8,8,128]{3,2,1,0:T(8,128)S(1)} collective-permute-done((f32[4,8,8,128]{3,2,1,0:T(8,128)S(1)}, f32[4,8,8,128]{3,2,1,0:T(8,128)S(1)}, u32[]{:S(2)}, u32[]{:S(2)}) %collective-permute-start.1) | collective-permute-done | bytes 131104 | tf_op jit(solution)/shard_map/ppermute | solution.py:232
  22.0 0.0 collective-permute-done.south_ref
  22.1 0.9 %all-to-all-done = f32[32,16,128]{2,1,0:T(8,128)S(1)} async-done(((f32[32,16,128]{2,1,0:T(8,128)}), f32[32,16,128]{2,1,0:T(8,128)S(1)}, u32[]{:S(2)}, u32[]{:S(2)}) %all-to-all-start) | async-done | bytes 262176 | tf_op jit(solution)/shard_map/all_to_all | solution.py:241
  23.0 0.4 shard_map.74
  23.4 0.0 copy-start.4
  23.4 3.1 %collective-permute-start.2 = (f32[10,16,128]{2,1,0:T(8,128)S(1)}, f32[10,16,128]{2,1,0:T(8,128)S(1)}, u32[]{:S(2)}, u32[]{:S(2)}) collective-permute-start(f32[10,16,128]{2,1,0:T(8,128)S(1)} %get-tuple-element.13), channel_id=1, source_target_pairs={{0,32},{32,64},{64,96},{1,33},{33,65},{65,97},{2,34},{34,66},{66,9... | collective-permute-start | bytes 245768 | tf_op jit(solution)/shard_map/ppermute | solution.py:232
  26.5 1.3 %collective-permute-start.3 = (f32[10,16,128]{2,1,0:T(8,128)S(1)}, f32[10,16,128]{2,1,0:T(8,128)S(1)}, u32[]{:S(2)}, u32[]{:S(2)}) collective-permute-start(f32[10,16,128]{2,1,0:T(8,128)S(1)} %get-tuple-element.14), channel_id=1, source_target_pairs={{32,0},{64,32},{96,64},{33,1},{65,33},{97,65},{34,2},{66,34},{98,6... | collective-permute-start | bytes 245768 | tf_op jit(solution)/shard_map/ppermute | solution.py:232
  27.8 0.0 copy-done.7
  27.9 0.0 copy-done.4
  27.9 1.6 %shard_map.75.smooth_ref = f32[4,128]{1,0:T(4,128)S(1)} custom-call(s32[1]{0:T(128)} %bitcast.5.gx_ref, s32[6,2048]{1,0:T(8,128)S(1)} %bitcast.14, f32[16,128]{1,0:T(8,128)S(1)} %bitcast.12, f32[512,128]{1,0:T(8,128)S(1)} %bitcast.10, f32[4,8,16,128]{3,2,1,0:T(8,128)S(1)} %get-tuple-element.12.after_ref.ext_ref), custom_call_target="tpu_custom_call" | custom-call | flops 4294967296 | bytes 1048576 | tf_op jit(solution)/shard_map/pallas_call | solution.py:248
  29.5 0.0 collective-permute-done.2.west_ref
  29.5 2.2 %collective-permute-done.3.east_ref = f32[10,16,128]{2,1,0:T(8,128)S(1)} collective-permute-done((f32[10,16,128]{2,1,0:T(8,128)S(1)}, f32[10,16,128]{2,1,0:T(8,128)S(1)}, u32[]{:S(2)}, u32[]{:S(2)}) %collective-permute-start.3) | collective-permute-done | bytes 81952 | tf_op jit(solution)/shard_map/ppermute | solution.py:232
  31.7 1.5 %shard_map.76 = f32[128,8,128]{2,1,0:T(8,128)} custom-call(f32[4,8,16,128]{3,2,1,0:T(8,128)S(1)} %get-tuple-element.12.after_ref.ext_ref, f32[10,16,128]{2,1,0:T(8,128)S(1)} %collective-permute-done.2.west_ref, f32[10,16,128]{2,1,0:T(8,128)S(1)} %collective-permute-done.3.east_ref, f32[4,8,8,128]{3,2,1,0:T(8,128)S(1)} %get-tuple-element.10.own_ref.ids_ref, ...), custom_call_target="tpu_custom_call" | custom-call | tf_op jit(solution)/shard_map/pallas_call | solution.py:254
  33.2 11.8 %all-to-all-start.1 = ((f32[128,8,128]{2,1,0:T(8,128)}), f32[128,8,128]{2,1,0:T(8,128)S(1)}, u32[]{:S(2)}, u32[]{:S(2)}) async-start(f32[128,8,128]{2,1,0:T(8,128)} %shard_map.76), calls=%async_computation.1 | async-start | bytes 1048576 | tf_op jit(solution)/shard_map/all_to_all | solution.py:257
  45.0 0.0 copy-start.6
  45.0 14.1 %all-to-all-done.1.all_ref = f32[128,8,128]{2,1,0:T(8,128)S(1)} async-done(((f32[128,8,128]{2,1,0:T(8,128)}), f32[128,8,128]{2,1,0:T(8,128)S(1)}, u32[]{:S(2)}, u32[]{:S(2)}) %all-to-all-start.1) | async-done | bytes 524320 | tf_op jit(solution)/shard_map/all_to_all | solution.py:257
  59.1 0.0 copy-done.6
  59.1 2.9 %shard_map.77 = f32[32,128]{1,0:T(8,128)} custom-call(s32[1]{0:T(128)} %bitcast.gy_ref, s32[32]{0:T(128)S(1)} %copy-done.6, f32[128,8,128]{2,1,0:T(8,128)S(1)} %all-to-all-done.1.all_ref), custom_call_target="tpu_custom_call" | custom-call | tf_op jit(solution)/shard_map/pallas_call | solution.py:259
  (1 shorter events, 0.0 us)
Async XLA Ops:
  0.0 0.8 %copy-start = (f32[8,8,128]{2,1,0:T(8,128)S(1)}, f32[8,8,128]{2,1,0:T(8,128)}, u32[]{:S(2)}) copy-start(f32[8,8,128]{2,1,0:T(8,128)} %temp_ref.1) | copy-start | bytes 98308
  0.8 0.8 %copy-start.1 = (f32[8,8,128]{2,1,0:T(8,128)S(1)}, f32[8,8,128]{2,1,0:T(8,128)}, u32[]{:S(2)}) copy-start(f32[8,8,128]{2,1,0:T(8,128)} %rock_ref.1) | copy-start | bytes 98308
  1.5 0.8 %copy-start.2 = (f32[8,8,128]{2,1,0:T(8,128)S(1)}, f32[8,8,128]{2,1,0:T(8,128)}, u32[]{:S(2)}) copy-start(f32[8,8,128]{2,1,0:T(8,128)} %misfit_ref.1) | copy-start | bytes 98308
  2.3 0.7 %copy-start.3 = (f32[2048]{0:T(1024)S(1)}, f32[2048]{0:T(1024)}, u32[]{:S(2)}) copy-start(f32[2048]{0:T(1024)} %param.11) | copy-start | bytes 24580
  3.0 0.7 %copy-start.5 = (s32[8,8,1]{1,2,0:T(1,128)S(1)}, s32[8,8,1]{1,2,0:T(1,128)}, u32[]{:S(2)}) copy-start(s32[8,8,1]{1,2,0:T(1,128)} %param.10) | copy-start | bytes 772
  4.4 18.6 %all-to-all-start = ((f32[32,16,128]{2,1,0:T(8,128)}), f32[32,16,128]{2,1,0:T(8,128)S(1)}, u32[]{:S(2)}, u32[]{:S(2)}) async-start(f32[32,16,128]{2,1,0:T(8,128)} %get-tuple-element.11), calls=%async_computation | async-start | bytes 524288 | tf_op jit(solution)/shard_map/all_to_all | solution.py:241
  14.0 8.1 %collective-permute-start.1 = (f32[4,8,8,128]{3,2,1,0:T(8,128)S(1)}, f32[4,8,8,128]{3,2,1,0:T(8,128)S(1)}, u32[]{:S(2)}, u32[]{:S(2)}) collective-permute-start(f32[4,8,8,128]{3,2,1,0:T(8,128)S(1)} %get-tuple-element.10.own_ref.ids_ref), channel_id=1, source_target_pairs={{1,0},{2,1},{3,2},{4,3},{5,4},{6,5},{7,6},{8,7},{9,8},{10,9},{11,1... | collective-permute-start | bytes 393224 | tf_op jit(solution)/shard_map/ppermute | solution.py:232
  16.1 5.9 %collective-permute-start = (f32[4,8,8,128]{3,2,1,0:T(8,128)S(1)}, f32[4,8,8,128]{3,2,1,0:T(8,128)S(1)}, u32[]{:S(2)}, u32[]{:S(2)}) collective-permute-start(f32[4,8,8,128]{3,2,1,0:T(8,128)S(1)} %get-tuple-element.10.own_ref.ids_ref), channel_id=1, source_target_pairs={{0,1},{1,2},{2,3},{3,4},{4,5},{5,6},{6,7},{7,8},{8,9},{9,10},{10,1... | collective-permute-start | bytes 393224 | tf_op jit(solution)/shard_map/ppermute | solution.py:232
  23.0 4.9 %copy-start.7 = (s32[2048,6]{0,1:T(8,128)S(1)}, s32[2048,6]{0,1:T(8,128)}, u32[]{:S(2)}) copy-start(s32[2048,6]{0,1:T(8,128)} %param.13) | copy-start | bytes 147460
  23.4 4.4 %copy-start.4 = (f32[2048]{0:T(1024)S(1)}, f32[2048]{0:T(1024)}, u32[]{:S(2)}) copy-start(f32[2048]{0:T(1024)} %param.11) | copy-start | bytes 24580
  23.4 6.1 %collective-permute-start.2 = (f32[10,16,128]{2,1,0:T(8,128)S(1)}, f32[10,16,128]{2,1,0:T(8,128)S(1)}, u32[]{:S(2)}, u32[]{:S(2)}) collective-permute-start(f32[10,16,128]{2,1,0:T(8,128)S(1)} %get-tuple-element.13), channel_id=1, source_target_pairs={{0,32},{32,64},{64,96},{1,33},{33,65},{65,97},{2,34},{34,66},{66,9... | collective-permute-start | bytes 245768 | tf_op jit(solution)/shard_map/ppermute | solution.py:232
  26.5 5.2 %collective-permute-start.3 = (f32[10,16,128]{2,1,0:T(8,128)S(1)}, f32[10,16,128]{2,1,0:T(8,128)S(1)}, u32[]{:S(2)}, u32[]{:S(2)}) collective-permute-start(f32[10,16,128]{2,1,0:T(8,128)S(1)} %get-tuple-element.14), channel_id=1, source_target_pairs={{32,0},{64,32},{96,64},{33,1},{65,33},{97,65},{34,2},{66,34},{98,6... | collective-permute-start | bytes 245768 | tf_op jit(solution)/shard_map/ppermute | solution.py:232
  33.2 25.9 %all-to-all-start.1 = ((f32[128,8,128]{2,1,0:T(8,128)}), f32[128,8,128]{2,1,0:T(8,128)S(1)}, u32[]{:S(2)}, u32[]{:S(2)}) async-start(f32[128,8,128]{2,1,0:T(8,128)} %shard_map.76), calls=%async_computation.1 | async-start | bytes 1048576 | tf_op jit(solution)/shard_map/all_to_all | solution.py:257
  45.0 14.1 %copy-start.6 = (s32[32]{0:T(128)S(1)}, s32[32]{0:T(128)}, u32[]{:S(2)}) copy-start(s32[32]{0:T(128)} %tally_ref.1) | copy-start | bytes 388

commit v2 on v1

v2 whole, which is shorter than its diff:
```python
import jax
import jax.numpy as jnp
from jax import lax
from jax.experimental import pallas as pl
from jax.experimental.pallas import tpu as pltpu
from jax.sharding import PartitionSpec as P

NBRS = 6
ITERS = 3
RELAXATION = 0.8
SMOOTHING = 0.5
SENS_SCALE = 0.03125
LANES = 128
F32 = jnp.float32
BF16 = jnp.bfloat16
I32 = jnp.int32

VMEM = pl.BlockSpec(memory_space=pltpu.VMEM)
HBM = pl.BlockSpec(memory_space=pltpu.HBM)


def iota(shape, dim):
    return lax.broadcasted_iota(I32, shape, dim)


def in_hbm(array):
    return pltpu.with_memory_space_constraint(array, pltpu.HBM)


def call(kernel, outs, in_specs, scratch=(), cost=None):
    one = not isinstance(outs, (list, tuple))
    shapes = [outs] if one else list(outs)
    return pl.pallas_call(
        kernel,
        out_shape=shapes[0] if one else shapes,
        in_specs=in_specs,
        out_specs=VMEM if one else [VMEM] * len(shapes),
        scratch_shapes=list(scratch),
        cost_estimate=cost,
        compiler_params=pltpu.CompilerParams(vmem_limit_bytes=32 << 20),
    )


def thirds(table):
    first = table.astype(BF16)
    rest = table - first.astype(F32)
    second = rest.astype(BF16)
    third = (rest - second.astype(F32)).astype(BF16)
    return first, second, third


def column(tile, lane):
    picked = jnp.where(iota(tile.shape, 1) == lane, tile, 0.0)
    return jnp.broadcast_to(jnp.sum(picked, axis=1, keepdims=True), tile.shape)


def pack_kernel(temp_ref, rock_ref, misfit_ref, map_ref, zone_ref, pack_ref, spread_ref, map_buf, zone_buf, sems):
    east, north = rock_ref.shape[0], rock_ref.shape[1]
    copies = [
        pltpu.make_async_copy(source, target, sems.at[number])
        for number, (source, target) in enumerate(
            [
                (map_ref, map_buf),
                (zone_ref, zone_buf),
                (rock_ref, pack_ref.at[pl.ds(0, east)]),
                (misfit_ref, pack_ref.at[pl.ds(east, east)]),
                (temp_ref, pack_ref.at[pl.ds(2 * east, east)]),
            ]
        )
    ]
    for copy in copies:
        copy.start()
    copies[0].wait()
    diagonal = iota((north, north), 0) == iota((north, north), 1)
    lane = iota((north, LANES), 1)
    ids = jnp.zeros((north, LANES), F32)
    for x in range(east):
        row = jnp.broadcast_to(map_buf[x].astype(F32), (north, north))
        one = jnp.sum(jnp.where(diagonal, row, 0.0), axis=1, keepdims=True)
        ids = jnp.where(lane == x, one, ids)
    pack_ref[3 * east] = ids
    copies[1].wait()
    shard = zone_buf[...]
    for other in range(spread_ref.shape[0]):
        spread_ref[other] = shard
    for copy in copies[2:]:
        copy.wait()


def extend_kernel(own_ref, first_ref, second_ref, ext_ref, slab_a_ref, slab_b_ref):
    gx, gy = lax.axis_index("gx"), lax.axis_index("gy")
    even = gy % 2 == 0

    def window(begin, count):
        one, two = first_ref[begin : begin + count], second_ref[begin : begin + count]
        south, north = jnp.where(even, two, one), jnp.where(even, one, two)
        return jnp.concatenate([south, own_ref[begin : begin + count], north], axis=1)

    rock, ids = window(0, 8), window(24, 1)
    misfit, temp = window(8, 8)[:, 4:20], window(16, 8)[:, 4:20]
    ext_ref[0:8] = rock
    ext_ref[8:9] = ids
    ext_ref[9:17, 0:16] = misfit
    ext_ref[17:25, 0:16] = temp
    inner, ids = rock[:, 4:20], ids[:, 4:20]
    low = (inner[0:5], misfit[0:4], temp[0:1], ids)
    moved = pltpu.roll(ids[0], LANES - 3, 1).reshape(1, 16, LANES)
    high = (inner[3:8], misfit[4:8], temp[7:8], moved)
    east_first = gx % 2 == 0
    begin = 0
    for lower, upper in zip(low, high):
        end = begin + lower.shape[0]
        slab_a_ref[begin:end] = jnp.where(east_first, upper, lower)
        slab_b_ref[begin:end] = jnp.where(east_first, lower, upper)
        begin = end


def smooth_kernel(adjacency_ref, zone_ref, tally_ref, table_ref, out_ref, meta_ref, tally_buf, sem):
    copy = pltpu.make_async_copy(tally_ref, tally_buf, sem)
    copy.start()
    rows = out_ref.shape[0]
    count = rows * LANES
    high_size = table_ref.shape[0]
    gx = lax.axis_index("gx")
    pieces = jnp.concatenate(thirds(jnp.transpose(table_ref[...])), axis=0)
    offset = pl.multiple_of(gx * count, count)
    high_row = iota((high_size, count), 0)
    low_row = iota((LANES, count), 0)
    total = jnp.zeros((LANES, count), F32)
    for k in range(NBRS):
        ids = adjacency_ref[k : k + 1, pl.ds(offset, count)]
        hot = jnp.where(high_row == (ids >> 7), 1.0, 0.0).astype(BF16)
        found = jnp.dot(pieces, hot, preferred_element_type=F32)
        found = found[0:LANES] + found[LANES : 2 * LANES] + found[2 * LANES :]
        total = total + jnp.where(low_row == (ids & 127), found, 0.0)
    near = jnp.sum(total, axis=0, keepdims=True)
    own = zone_ref[pl.ds(gx * rows, rows), :]
    for row in range(rows):
        out_ref[row : row + 1] = SMOOTHING * (
            NBRS * own[row : row + 1] - near[:, row * LANES : (row + 1) * LANES]
        )
    copy.wait()
    tally = tally_buf[...].astype(F32)
    rank, gy = iota(tally.shape, 1), lax.axis_index("gy")
    start = jnp.sum(jnp.where(rank < gy, tally, 0.0), axis=1, keepdims=True)
    held = jnp.sum(jnp.where(rank == gy, tally, 0.0), axis=1, keepdims=True)
    meta_ref[...] = jnp.where(iota((8, LANES), 0) == 0, start, held).astype(I32)


def sweep_kernel(ext_ref, first_ref, second_ref, table_ref, smooth_ref, out_ref):
    shape = (16, LANES)
    lane = iota(shape, 1)
    first, last = lane == 0, lane == LANES - 1
    even = lax.axis_index("gx") % 2 == 0
    one, two = first_ref[...], second_ref[...]
    west, east = jnp.where(even, two, one), jnp.where(even, one, two)

    own_ids = ext_ref[8]
    ids = [column(own_ids, x) for x in range(8)]
    ids += [column(west[10], step) for step in range(5)]
    ids += [column(east[10], step) for step in range(5)]
    own_columns = ids[:8]
    ids = jnp.concatenate(ids, axis=0).astype(I32)
    places = ids.shape[0]
    rows = ids >> 7
    lanes = iota((places, LANES), 1)
    hot = jnp.concatenate(
        [jnp.where(rows == lanes + LANES * part, 1.0, 0.0).astype(BF16) for part in range(table_ref.shape[0] // LANES)],
        axis=1,
    )
    found = sum(jnp.dot(hot, piece, preferred_element_type=F32) for piece in thirds(table_ref[...]))
    log = jnp.sum(jnp.where(lanes == (ids & 127), found, 0.0), axis=1, keepdims=True)
    gain = jnp.exp(jnp.broadcast_to(log, (places, LANES)))

    conduct, source, heat, own_sides = {}, {}, {}, {}
    for x in range(8):
        wide = ext_ref[x] * gain[24 * x : 24 * x + 24]
        conduct[x] = wide[4:20]
        own_sides[x] = wide[3:19] + wide[5:21]
        source[x] = ext_ref[9 + x, 0:16]
        heat[x] = ext_ref[17 + x, 0:16]
    for step in range(5):
        conduct[step - 5] = west[step] * gain[192 + 16 * step : 208 + 16 * step]
        conduct[step + 8] = east[step] * gain[272 + 16 * step : 288 + 16 * step]
    for step in range(4):
        source[step - 4] = west[5 + step]
        source[step + 8] = east[5 + step]
    heat[-1] = west[9]
    heat[8] = east[9]

    def depth_sides(v):
        up = jnp.where(first, 0.0, pltpu.roll(v, 1, 1))
        down = jnp.where(last, 0.0, pltpu.roll(v, LANES - 1, 1))
        return up, down

    def north_sides(v):
        return pltpu.roll(v, 1, 0), pltpu.roll(v, 15, 0)

    def around(rows, x):
        v = rows[x]
        up, down = depth_sides(v)
        south, north = north_sides(v)
        return ((rows[x - 1] + rows[x + 1]) + (south + north)) + (up + down)

    inverse, dual = {}, {}
    for x in range(-4, 12):
        v = conduct[x]
        if 0 <= x < 8:
            across = own_sides[x]
        else:
            south, north = north_sides(v)
            across = south + north
        up, down = depth_sides(v)
        twice = 6.0 * v + (((conduct[x - 1] + conduct[x + 1]) + across) + (up + down))
        inverse[x] = jnp.where(v > 0.0, 2.0 / twice, 0.0)
        dual[x] = source[x] * inverse[x]
    for sweep in range(ITERS):
        reach = 3 - sweep
        flux = {x: conduct[x] * dual[x] for x in dual}
        fresh = {}
        for x in range(-reach, 8 + reach):
            coupled = 0.5 * (conduct[x] * around(dual, x) + around(flux, x))
            fresh[x] = (1.0 - RELAXATION) * dual[x] + (RELAXATION * inverse[x]) * (source[x] + coupled)
        dual = fresh
    blocks = []
    for x in range(8):
        t, v = heat[x], dual[x]
        total = (t - heat[x + 1]) * (v - dual[x + 1]) + (t - heat[x - 1]) * (v - dual[x - 1])
        for near_t, near_v in zip(north_sides(t) + depth_sides(t), north_sides(v) + depth_sides(v)):
            total = total + (t - near_t) * (v - near_v)
        blocks.append(((-0.5 * SENS_SCALE) * total * conduct[x])[4:12])
    stacked = jnp.concatenate(blocks + [own[8:16] for own in own_columns], axis=0)
    turned = jnp.transpose(stacked)
    sums = jnp.sum(turned, axis=0, keepdims=True)
    row = jnp.where(iota((1, LANES), 1) < 64, sums, turned[0:1])
    tile = jnp.concatenate([smooth_ref[...], row], axis=0)
    for eight in range(out_ref.shape[0] // 40):
        out_ref[40 * eight : 40 * eight + 40] = jnp.concatenate([tile] * 8, axis=0)


def place_kernel(meta_ref, all_ref, out_ref, smooth_ref, hot_ref, low_ref):
    start, held = meta_ref[0, 0], meta_ref[1, 0]
    sources = all_ref.shape[0] // 5
    half = sources // 2
    both = all_ref[pl.ds(4, sources, stride=5), :]
    turned = pltpu.roll(both, 64, 1)
    left = iota((half, LANES), 1) < 64
    values = jnp.where(left, both[:half], turned[half:])
    slots = jnp.where(left, turned[:half], both[half:]).astype(I32) - start
    pieces = [piece.astype(F32) for piece in thirds(values)]
    high, low = slots >> 7, slots & 127
    slot_rows = out_ref.shape[0]
    high_row = iota((slot_rows, LANES), 0)
    low_row = iota((LANES, LANES), 0)
    for row in range(half):
        match = high_row == high[row : row + 1]
        for number in range(3):
            hot_ref[number * slot_rows : (number + 1) * slot_rows, row * LANES : (row + 1) * LANES] = jnp.where(
                match, pieces[number][row : row + 1], 0.0
            ).astype(BF16)
        low_ref[:, row * LANES : (row + 1) * LANES] = jnp.where(low_row == low[row : row + 1], 1.0, 0.0).astype(BF16)
    sums = lax.dot_general(hot_ref[...], low_ref[...], (((1,), (1,)), ((), ())), preferred_element_type=F32)
    sums = sums[0:slot_rows] + sums[slot_rows : 2 * slot_rows] + sums[2 * slot_rows :]

    top, shift = start >> 7, start & 127
    for row in range(slot_rows + 1):
        zone_row = jnp.minimum(top + row, sources * 4 - 1)
        smooth_ref[row : row + 1, :] = all_ref[pl.ds((zone_row >> 2) * 5 + (zone_row & 3), 1), :]
    moved = pltpu.roll(smooth_ref[...], LANES - shift, 1)
    lane = iota((slot_rows, LANES), 1)
    smooth = jnp.where(lane < LANES - shift, moved[0:slot_rows], moved[1 : slot_rows + 1])
    within = iota((slot_rows, LANES), 0) * LANES + lane
    out_ref[...] = jnp.where(within < held, sums + smooth, 0.0)


def swap(array, axis, begin):
    pairs = [(i, i + 1) for i in range(begin, lax.axis_size(axis) - 1, 2)]
    return lax.ppermute(array, axis, pairs + [(b, a) for a, b in pairs])


def body(temp, rock, misfit, zone_map, zone_log, tally, adjacency):
    east, north, depth = temp.shape
    across, along = lax.axis_size("gx"), lax.axis_size("gy")
    devices = across * along
    shard_rows = zone_log.shape[0] // LANES
    zone = zone_log.reshape(shard_rows, LANES)
    shape = jax.ShapeDtypeStruct
    pack, spread = call(
        pack_kernel,
        [shape((3 * east + 1, north, depth), F32), shape((along, shard_rows, LANES), F32)],
        [HBM] * 5,
        [pltpu.VMEM((east, 1, north), I32), pltpu.VMEM((shard_rows, LANES), F32), pltpu.SemaphoreType.DMA((5,))],
    )(*map(in_hbm, (temp, rock, misfit, jnp.transpose(zone_map, (0, 2, 1)), zone)))
    y_first, y_second = swap(pack, "gy", 0), swap(pack, "gy", 1)
    table = lax.all_to_all(spread, "gy", 0, 0, tiled=True).reshape(along * shard_rows, LANES)
    ext, slab_a, slab_b = call(
        extend_kernel,
        [shape((25, 24, LANES), F32), shape((11, 16, LANES), F32), shape((11, 16, LANES), F32)],
        [VMEM] * 3,
    )(pack, y_first, y_second)
    x_first, x_second = swap(slab_a, "gx", 0), swap(slab_b, "gx", 1)
    smooth, meta = call(
        smooth_kernel,
        [shape((shard_rows // across, LANES), F32), shape((8, LANES), I32)],
        [VMEM, VMEM, HBM, VMEM],
        [pltpu.VMEM((1, along), I32), pltpu.SemaphoreType.DMA],
        cost=pl.CostEstimate(flops=1 << 32, bytes_accessed=1 << 20, transcendentals=0),
    )(jnp.transpose(adjacency), zone, in_hbm(tally.reshape(1, along)), table)
    rows = call(sweep_kernel, shape((devices * 5, LANES), F32), [VMEM] * 5)(ext, x_first, x_second, table, smooth)
    gathered = lax.all_to_all(rows.reshape(devices, 1, 5 * LANES), ("gy", "gx"), 0, 0, tiled=True)
    slot_rows = 2 * shard_rows
    out = call(
        place_kernel,
        shape((slot_rows, LANES), F32),
        [VMEM, VMEM],
        [
            pltpu.VMEM((slot_rows + 8, LANES), F32),
            pltpu.VMEM((3 * slot_rows, devices * 64), BF16),
            pltpu.VMEM((LANES, devices * 64), BF16),
        ],
    )(meta, gathered.reshape(devices * 5, LANES))
    return out.reshape(slot_rows * LANES)


def solution(mesh):
    placed = (
        P("gx", "gy", None),
        P("gx", "gy", None),
        P("gx", "gy", None),
        P("gx", "gy", None),
        P("gy"),
        P(),
        P("gy", None),
    )
    return jax.shard_map(body, mesh=mesh, in_specs=placed, out_specs=P("gy"), check_vma=False)
```

time: 62.6 us -> 50.5 us (0.81)
  blocking collectives: 0 us -> 23.8 us
  starting transfers between devices: 31.4 us -> 15.3 us
  waiting for transfers between devices: 19.8 us -> 3.95 us
  local copies, waits for them, and re-layouts: 3.67 us -> 0.01 us
    all_to_all x0 -> x1, blocking collectives: none -> 23.8 us  [body(): lax.all_to_all(rows.reshape(devices, 1, 5 * LANES), ('gy', 'gx'), 0, 0, t...]
    all_to_all x1 -> x0, waiting for transfers between devices: 14.1 us -> none  [body(): gathered = lax.all_to_all(tile, ('gy', 'gx'), 0, 0, tiled=True)]
    all_to_all x1 -> x0, starting transfers between devices: 11.8 us -> none  [body(): gathered = lax.all_to_all(tile, ('gy', 'gx'), 0, 0, tiled=True)]
    ppermute x4, starting transfers between devices: 9.97 us -> 5.68 us  [swap(): return lax.ppermute(array, axis, pairs + [(b, a) for a, b in pairs])]
    unnamed x16 -> x4, local copies, waits for them, and re-layouts: 3.67 us -> 0.01 us
    all_to_all x1, waiting for transfers between devices: 0.92 us -> 0.01 us  [body(): lax.all_to_all(spread, 'gy', 0, 0, tiled=True)]
    ppermute x4, waiting for transfers between devices: 4.72 us -> 3.95 us  [swap(): return lax.ppermute(array, axis, pairs + [(b, a) for a, b in pairs])]
  transfers between devices with their start and end apart: 6 -> 5, of which waited for: 4 -> 1; matrix products, arithmetic and copies ran while one was open for 0% -> 0% of each run, Pallas kernels for 3% -> 4%
where the time goes in v2:
time: 50.5 us; the launch traced here: 50.1 us
  blocking collectives  23.8 us (47%)
  starting transfers between devices  15.3 us (30%)
  Pallas kernels  6.99 us (14%)
  waiting for transfers between devices  3.95 us (8%)
    all_to_all x1, blocking collectives, body(): lax.all_to_all(rows.reshape(devices, 1, 5 * LANES), ('gy', 'gx'), 0, 0, t...  23.8 us
    all_to_all x1, starting transfers between devices, body(): lax.all_to_all(spread, 'gy', 0, 0, tiled=True)  9.61 us
    ppermute x4, starting transfers between devices, swap(): return lax.ppermute(array, axis, pairs + [(b, a) for a, b in pairs])  5.68 us
    ppermute x4, waiting for transfers between devices, swap(): return lax.ppermute(array, axis, pairs + [(b, a) for a, b in pairs])  3.95 us
    pallas_call x1, Pallas kernels, body(): call(place_kernel, shape((slot_rows, LANES), F32), [VMEM, VMEM], [pltpu.V...  2.31 us
    pallas_call x1, Pallas kernels, body(): call(smooth_kernel, [shape((shard_rows // across, LANES), F32), shape((8,...  1.7 us
    pallas_call x1, Pallas kernels, body(): call(pack_kernel, [shape((3 * east + 1, north, depth), F32), shape((along...  1.58 us
    pallas_call x1, Pallas kernels, body(): call(sweep_kernel, shape((devices * 5, LANES), F32), [VMEM] * 5)  1.31 us
  transfers between devices with their start and end apart: 5, of which 1 were waited for; matrix products, arithmetic and copies ran while one was open for 0% of the time, Pallas kernels for 4%

profile of v2, /device:TPU:1, one launch (start us, length us, event | category | flops | bytes accessed | tf_op | source)
XLA Modules:
  0.0 50.1 jit_solution(3194441524301281085)
XLA Ops:
  0.0 1.6 %shard_map.73 = (f32[25,8,128]{2,1,0:T(8,128)S(1)}, f32[32,16,128]{2,1,0:T(8,128)}) custom-call(f32[8,8,128]{2,1,0:T(8,128)} %temp_ref.1, f32[8,8,128]{2,1,0:T(8,128)} %rock_ref.1, f32[8,8,128]{2,1,0:T(8,128)} %misfit_ref.1, s32[8,1,8]{2,1,0:T(1,128)} %bitcast.17, f32[16,128]{1,0:T(8,128)} %bitcast.14), custom_call_target="tpu_custom_call" | custom-call | tf_op jit(solution)/shard_map/pallas_call | solution.py:288
  1.6 9.6 %all-to-all-start = ((f32[32,16,128]{2,1,0:T(8,128)}), f32[32,16,128]{2,1,0:T(8,128)S(1)}, u32[]{:S(2)}, u32[]{:S(2)}) async-start(f32[32,16,128]{2,1,0:T(8,128)} %get-tuple-element.12), calls=%async_computation | async-start | bytes 524288 | tf_op jit(solution)/shard_map/all_to_all | solution.py:295
  11.2 0.0 copy-start.1
  11.2 3.7 %collective-permute-start.1 = (f32[25,8,128]{2,1,0:T(8,128)S(1)}, f32[25,8,128]{2,1,0:T(8,128)S(1)}, u32[]{:S(2)}, u32[]{:S(2)}) collective-permute-start(f32[25,8,128]{2,1,0:T(8,128)S(1)} %get-tuple-element.14.own_ref), channel_id=1, source_target_pairs={{1,2},{3,4},{5,6},{7,8},{9,10},{11,12},{13,14},{15,16},{17,18},{19... | collective-permute-start | bytes 307208 | tf_op jit(solution)/shard_map/ppermute | solution.py:278
  14.9 0.1 collective-permute-start
  15.0 3.9 %collective-permute-done.1.second_ref = f32[25,8,128]{2,1,0:T(8,128)S(1)} collective-permute-done((f32[25,8,128]{2,1,0:T(8,128)S(1)}, f32[25,8,128]{2,1,0:T(8,128)S(1)}, u32[]{:S(2)}, u32[]{:S(2)}) %collective-permute-start.1) | collective-permute-done | bytes 102432 | tf_op jit(solution)/shard_map/ppermute | solution.py:278
  18.9 0.0 collective-permute-done.first_ref
  18.9 0.1 shard_map.75
  19.0 0.0 copy-start
  19.0 1.3 %collective-permute-start.2 = (f32[11,16,128]{2,1,0:T(8,128)S(1)}, f32[11,16,128]{2,1,0:T(8,128)S(1)}, u32[]{:S(2)}, u32[]{:S(2)}) collective-permute-start(f32[11,16,128]{2,1,0:T(8,128)S(1)} %get-tuple-element.16), channel_id=1, source_target_pairs={{0,32},{64,96},{32,0},{96,64},{1,33},{65,97},{33,1},{97,65},{2,34}... | collective-permute-start | bytes 270344 | tf_op jit(solution)/shard_map/ppermute | solution.py:278
  20.3 0.7 %collective-permute-start.3 = (f32[11,16,128]{2,1,0:T(8,128)S(1)}, f32[11,16,128]{2,1,0:T(8,128)S(1)}, u32[]{:S(2)}, u32[]{:S(2)}) collective-permute-start(f32[11,16,128]{2,1,0:T(8,128)S(1)} %get-tuple-element.17), channel_id=1, source_target_pairs={{32,64},{64,32},{33,65},{65,33},{34,66},{66,34},{35,67},{67,35},{3... | collective-permute-start | bytes 270344 | tf_op jit(solution)/shard_map/ppermute | solution.py:278
  21.0 0.0 all-to-all-done
  21.0 0.0 copy-done.1
  21.0 0.0 copy-done
  21.0 1.7 %shard_map.74 = (f32[4,128]{1,0:T(4,128)S(1)}, s32[8,128]{1,0:T(8,128)S(1)}) custom-call(s32[6,2048]{1,0:T(8,128)S(1)} %bitcast.16, f32[16,128]{1,0:T(8,128)S(1)} %bitcast.15, s32[1,32]{1,0:T(1,128)} %bitcast.18, f32[512,128]{1,0:T(8,128)S(1)} %bitcast.12), custom_call_target="tpu_custom_call" | custom-call | flops 4294967296 | bytes 1048576 | tf_op jit(solution)/shard_map/pallas_call | solution.py:302
  22.7 0.0 collective-permute-done.2.first_ref
  22.7 0.0 collective-permute-done.3.second_ref
  22.7 1.3 %shard_map.76 = f32[640,128]{1,0:T(8,128)S(1)} custom-call(f32[25,24,128]{2,1,0:T(8,128)S(1)} %get-tuple-element.15.ext_ref, f32[11,16,128]{2,1,0:T(8,128)S(1)} %collective-permute-done.2.first_ref, f32[11,16,128]{2,1,0:T(8,128)S(1)} %collective-permute-done.3.second_ref, f32[512,128]{1,0:T(8,128)S(1)} %bitcast.13, f32[4,128]{1,0:T(4,128)S(1)} %get-tuple-element.18.smooth_ref), custom_call_target="tpu_custom_call" | custom-call | tf_op jit(solution)/shard_map/pallas_call | solution.py:309
  24.0 23.8 %all_to_all.10 = f32[128,1,640]{2,1,0:T(1,128)S(1)} all-to-all(f32[128,1,640]{2,1,0:T(1,128)S(1)} %bitcast.10), channel_id=1, replica_groups=mesh['gx'=4,'gy'=32] {'gy','gx'}, dimensions={0} | all-to-all | bytes 655360 | tf_op jit(solution)/shard_map/all_to_all | solution.py:310
  47.8 2.3 %shard_map.77 = f32[32,128]{1,0:T(8,128)} custom-call(s32[8,128]{1,0:T(8,128)S(1)} %get-tuple-element.13.meta_ref, f32[640,128]{1,0:T(8,128)S(1)} %bitcast.11), custom_call_target="tpu_custom_call" | custom-call | tf_op jit(solution)/shard_map/pallas_call | solution.py:312
Async XLA Ops:
  1.6 19.4 %all-to-all-start = ((f32[32,16,128]{2,1,0:T(8,128)}), f32[32,16,128]{2,1,0:T(8,128)S(1)}, u32[]{:S(2)}, u32[]{:S(2)}) async-start(f32[32,16,128]{2,1,0:T(8,128)} %get-tuple-element.12), calls=%async_computation | async-start | bytes 524288 | tf_op jit(solution)/shard_map/all_to_all | solution.py:295
  11.2 9.8 %copy-start.1 = (s32[2048,6]{0,1:T(8,128)S(1)}, s32[2048,6]{0,1:T(8,128)}, u32[]{:S(2)}) copy-start(s32[2048,6]{0,1:T(8,128)} %param.13) | copy-start | bytes 147460
  11.2 7.7 %collective-permute-start.1 = (f32[25,8,128]{2,1,0:T(8,128)S(1)}, f32[25,8,128]{2,1,0:T(8,128)S(1)}, u32[]{:S(2)}, u32[]{:S(2)}) collective-permute-start(f32[25,8,128]{2,1,0:T(8,128)S(1)} %get-tuple-element.14.own_ref), channel_id=1, source_target_pairs={{1,2},{3,4},{5,6},{7,8},{9,10},{11,12},{13,14},{15,16},{17,18},{19... | collective-permute-start | bytes 307208 | tf_op jit(solution)/shard_map/ppermute | solution.py:278
  14.9 4.0 %collective-permute-start = (f32[25,8,128]{2,1,0:T(8,128)S(1)}, f32[25,8,128]{2,1,0:T(8,128)S(1)}, u32[]{:S(2)}, u32[]{:S(2)}) collective-permute-start(f32[25,8,128]{2,1,0:T(8,128)S(1)} %get-tuple-element.14.own_ref), channel_id=1, source_target_pairs={{0,1},{2,3},{4,5},{6,7},{8,9},{10,11},{12,13},{14,15},{16,17},{18,... | collective-permute-start | bytes 307208 | tf_op jit(solution)/shard_map/ppermute | solution.py:278
  19.0 2.0 %copy-start = (f32[2048]{0:T(1024)S(1)}, f32[2048]{0:T(1024)}, u32[]{:S(2)}) copy-start(f32[2048]{0:T(1024)} %param.11) | copy-start | bytes 24580
  19.0 3.7 %collective-permute-start.2 = (f32[11,16,128]{2,1,0:T(8,128)S(1)}, f32[11,16,128]{2,1,0:T(8,128)S(1)}, u32[]{:S(2)}, u32[]{:S(2)}) collective-permute-start(f32[11,16,128]{2,1,0:T(8,128)S(1)} %get-tuple-element.16), channel_id=1, source_target_pairs={{0,32},{64,96},{32,0},{96,64},{1,33},{65,97},{33,1},{97,65},{2,34}... | collective-permute-start | bytes 270344 | tf_op jit(solution)/shard_map/ppermute | solution.py:278
  20.3 2.4 %collective-permute-start.3 = (f32[11,16,128]{2,1,0:T(8,128)S(1)}, f32[11,16,128]{2,1,0:T(8,128)S(1)}, u32[]{:S(2)}, u32[]{:S(2)}) collective-permute-start(f32[11,16,128]{2,1,0:T(8,128)S(1)} %get-tuple-element.17), channel_id=1, source_target_pairs={{32,64},{64,32},{33,65},{65,33},{34,66},{66,34},{35,67},{67,35},{3... | collective-permute-start | bytes 270344 | tf_op jit(solution)/shard_map/ppermute | solution.py:278

commit v3 on v2

--- a/solution.py
+++ b/solution.py
@@ -54,14 +54,14 @@
     return jnp.broadcast_to(jnp.sum(picked, axis=1, keepdims=True), tile.shape)
 
 
-def pack_kernel(temp_ref, rock_ref, misfit_ref, map_ref, zone_ref, pack_ref, spread_ref, map_buf, zone_buf, sems):
+def pack_kernel(temp_ref, rock_ref, misfit_ref, map_ref, zone_ref, pack_ref, shard_ref, map_buf, sems):
     east, north = rock_ref.shape[0], rock_ref.shape[1]
     copies = [
         pltpu.make_async_copy(source, target, sems.at[number])
         for number, (source, target) in enumerate(
             [
                 (map_ref, map_buf),
-                (zone_ref, zone_buf),
+                (zone_ref, shard_ref),
                 (rock_ref, pack_ref.at[pl.ds(0, east)]),
                 (misfit_ref, pack_ref.at[pl.ds(east, east)]),
                 (temp_ref, pack_ref.at[pl.ds(2 * east, east)]),
@@ -79,12 +79,14 @@
         one = jnp.sum(jnp.where(diagonal, row, 0.0), axis=1, keepdims=True)
         ids = jnp.where(lane == x, one, ids)
     pack_ref[3 * east] = ids
-    copies[1].wait()
-    shard = zone_buf[...]
+    for copy in copies[1:]:
+        copy.wait()
+
+
+def spread_kernel(shard_ref, spread_ref):
+    shard = shard_ref[...]
     for other in range(spread_ref.shape[0]):
         spread_ref[other] = shard
-    for copy in copies[2:]:
-        copy.wait()
 
 
 def extend_kernel(own_ref, first_ref, second_ref, ext_ref, slab_a_ref, slab_b_ref):
@@ -285,18 +287,25 @@
     shard_rows = zone_log.shape[0] // LANES
     zone = zone_log.reshape(shard_rows, LANES)
     shape = jax.ShapeDtypeStruct
-    pack, spread = call(
+    pack, shard = call(
         pack_kernel,
-        [shape((3 * east + 1, north, depth), F32), shape((along, shard_rows, LANES), F32)],
+        [shape((3 * east + 1, north, depth), F32), shape((shard_rows, LANES), F32)],
         [HBM] * 5,
-        [pltpu.VMEM((east, 1, north), I32), pltpu.VMEM((shard_rows, LANES), F32), pltpu.SemaphoreType.DMA((5,))],
+        [pltpu.VMEM((east, 1, north), I32), pltpu.SemaphoreType.DMA((5,))],
     )(*map(in_hbm, (temp, rock, misfit, jnp.transpose(zone_map, (0, 2, 1)), zone)))
     y_first, y_second = swap(pack, "gy", 0), swap(pack, "gy", 1)
+    spread = call(
+        spread_kernel,
+        shape((along, shard_rows, LANES), F32),
+        [VMEM],
+        cost=pl.CostEstimate(flops=1 << 35, bytes_accessed=1 << 20, transcendentals=0),
+    )(shard)
     table = lax.all_to_all(spread, "gy", 0, 0, tiled=True).reshape(along * shard_rows, LANES)
     ext, slab_a, slab_b = call(
         extend_kernel,
         [shape((25, 24, LANES), F32), shape((11, 16, LANES), F32), shape((11, 16, LANES), F32)],
         [VMEM] * 3,
+        cost=pl.CostEstimate(flops=1 << 37, bytes_accessed=1 << 20, transcendentals=0),
     )(pack, y_first, y_second)
     x_first, x_second = swap(slab_a, "gx", 0), swap(slab_b, "gx", 1)
     smooth, meta = call(
@@ -305,7 +314,7 @@
         [VMEM, VMEM, HBM, VMEM],
         [pltpu.VMEM((1, along), I32), pltpu.SemaphoreType.DMA],
         cost=pl.CostEstimate(flops=1 << 32, bytes_accessed=1 << 20, transcendentals=0),
-    )(jnp.transpose(adjacency), zone, in_hbm(tally.reshape(1, along)), table)
+    )(jnp.transpose(adjacency), shard, in_hbm(tally.reshape(1, along)), table)
     rows = call(sweep_kernel, shape((devices * 5, LANES), F32), [VMEM] * 5)(ext, x_first, x_second, table, smooth)
     gathered = lax.all_to_all(rows.reshape(devices, 1, 5 * LANES), ("gy", "gx"), 0, 0, tiled=True)
     slot_rows = 2 * shard_rows

time: 50.5 us -> 47.2 us (0.935)
  blocking collectives: 23.8 us -> 18.2 us
  waiting for transfers between devices: 3.95 us -> 6.95 us
  starting transfers between devices: 15.3 us -> 14.7 us
    all_to_all x1, waiting for transfers between devices: 0.01 us -> 6.94 us  [body(): lax.all_to_all(spread, 'gy', 0, 0, tiled=True)]
    all_to_all x1, blocking collectives: 23.8 us -> 18.2 us  [body(): lax.all_to_all(rows.reshape(devices, 1, 5 * LANES), ('gy', 'gx'), 0, 0, t...]
    ppermute x4, waiting for transfers between devices: 3.95 us -> 0.01 us  [swap(): return lax.ppermute(array, axis, pairs + [(b, a) for a, b in pairs])]
    all_to_all x1, starting transfers between devices: 9.61 us -> 7.76 us  [body(): lax.all_to_all(spread, 'gy', 0, 0, tiled=True)]
    ppermute x4, starting transfers between devices: 5.68 us -> 6.95 us  [swap(): return lax.ppermute(array, axis, pairs + [(b, a) for a, b in pairs])]
    pallas_call x1 -> x2, Pallas kernels: 1.58 us -> 1.58 us  [the longest x1 0.86 us: body(): call(pack_kernel, [shape((3 * east + 1, north, depth), F32), shape((shard...]
  transfers between devices with their start and end apart: 5 -> 5, of which waited for: 1 -> 1; matrix products, arithmetic and copies ran while one was open for 0% -> 0% of each run, Pallas kernels for 4% -> 5%
where the time goes in v3:
time: 47.2 us; the launch traced here: 46.9 us
  blocking collectives  18.2 us (39%)
  starting transfers between devices  14.7 us (31%)
  Pallas kernels  7 us (15%)
  waiting for transfers between devices  6.95 us (15%)
    all_to_all x1, blocking collectives, body(): lax.all_to_all(rows.reshape(devices, 1, 5 * LANES), ('gy', 'gx'), 0, 0, t...  18.2 us
    all_to_all x1, starting transfers between devices, body(): lax.all_to_all(spread, 'gy', 0, 0, tiled=True)  7.76 us
    ppermute x4, starting transfers between devices, swap(): return lax.ppermute(array, axis, pairs + [(b, a) for a, b in pairs])  6.95 us
    all_to_all x1, waiting for transfers between devices, body(): lax.all_to_all(spread, 'gy', 0, 0, tiled=True)  6.94 us
    pallas_call x1, Pallas kernels, body(): call(place_kernel, shape((slot_rows, LANES), F32), [VMEM, VMEM], [pltpu.V...  2.31 us
    pallas_call x1, Pallas kernels, body(): call(smooth_kernel, [shape((shard_rows // across, LANES), F32), shape((8,...  1.7 us
    pallas_call x1, Pallas kernels, body(): call(sweep_kernel, shape((devices * 5, LANES), F32), [VMEM] * 5)  1.31 us
  transfers between devices with their start and end apart: 5, of which 1 were waited for; matrix products, arithmetic and copies ran while one was open for 0% of the time, Pallas kernels for 5%

profile of v3, /device:TPU:1, one launch (start us, length us, event | category | flops | bytes accessed | tf_op | source)
XLA Modules:
  0.0 46.9 jit_solution(10837869314516377817)
XLA Ops:
  0.0 0.9 %shard_map.73 = (f32[25,8,128]{2,1,0:T(8,128)S(1)}, f32[16,128]{1,0:T(8,128)S(1)}) custom-call(f32[8,8,128]{2,1,0:T(8,128)} %temp_ref.1, f32[8,8,128]{2,1,0:T(8,128)} %rock_ref.1, f32[8,8,128]{2,1,0:T(8,128)} %misfit_ref.1, s32[8,1,8]{2,1,0:T(1,128)} %bitcast.16, f32[16,128]{1,0:T(8,128)} %bitcast.15), custom_call_target="tpu_custom_call" | custom-call | tf_op jit(solution)/shard_map/pallas_call | solution.py:290
  0.9 1.5 %collective-permute-start = (f32[25,8,128]{2,1,0:T(8,128)S(1)}, f32[25,8,128]{2,1,0:T(8,128)S(1)}, u32[]{:S(2)}, u32[]{:S(2)}) collective-permute-start(f32[25,8,128]{2,1,0:T(8,128)S(1)} %get-tuple-element.14.own_ref), channel_id=1, source_target_pairs={{0,1},{2,3},{4,5},{6,7},{8,9},{10,11},{12,13},{14,15},{16,17},{18,... | collective-permute-start | bytes 307208 | tf_op jit(solution)/shard_map/ppermute | solution.py:280
  2.4 3.5 %collective-permute-start.1 = (f32[25,8,128]{2,1,0:T(8,128)S(1)}, f32[25,8,128]{2,1,0:T(8,128)S(1)}, u32[]{:S(2)}, u32[]{:S(2)}) collective-permute-start(f32[25,8,128]{2,1,0:T(8,128)S(1)} %get-tuple-element.14.own_ref), channel_id=1, source_target_pairs={{1,2},{3,4},{5,6},{7,8},{9,10},{11,12},{13,14},{15,16},{17,18},{19... | collective-permute-start | bytes 307208 | tf_op jit(solution)/shard_map/ppermute | solution.py:280
  5.9 0.7 %shard_map.74 = f32[32,16,128]{2,1,0:T(8,128)} custom-call(f32[16,128]{1,0:T(8,128)S(1)} %get-tuple-element.12.shard_ref.zone_ref), custom_call_target="tpu_custom_call" | custom-call | flops 34359738368 | bytes 1048576 | tf_op jit(solution)/shard_map/pallas_call | solution.py:297
  6.6 7.8 %all-to-all-start = ((f32[32,16,128]{2,1,0:T(8,128)}), f32[32,16,128]{2,1,0:T(8,128)S(1)}, u32[]{:S(2)}, u32[]{:S(2)}) async-start(f32[32,16,128]{2,1,0:T(8,128)} %shard_map.74), calls=%async_computation | async-start | bytes 524288 | tf_op jit(solution)/shard_map/all_to_all | solution.py:303
  14.4 0.0 copy-start
  14.4 0.0 collective-permute-done.first_ref
  14.4 0.0 collective-permute-done.1.second_ref
  14.4 0.1 shard_map.76
  14.5 1.3 %collective-permute-start.2 = (f32[11,16,128]{2,1,0:T(8,128)S(1)}, f32[11,16,128]{2,1,0:T(8,128)S(1)}, u32[]{:S(2)}, u32[]{:S(2)}) collective-permute-start(f32[11,16,128]{2,1,0:T(8,128)S(1)} %get-tuple-element.16), channel_id=1, source_target_pairs={{0,32},{64,96},{32,0},{96,64},{1,33},{65,97},{33,1},{97,65},{2,34}... | collective-permute-start | bytes 270344 | tf_op jit(solution)/shard_map/ppermute | solution.py:280
  15.8 0.7 %collective-permute-start.3 = (f32[11,16,128]{2,1,0:T(8,128)S(1)}, f32[11,16,128]{2,1,0:T(8,128)S(1)}, u32[]{:S(2)}, u32[]{:S(2)}) collective-permute-start(f32[11,16,128]{2,1,0:T(8,128)S(1)} %get-tuple-element.17), channel_id=1, source_target_pairs={{32,64},{64,32},{33,65},{65,33},{34,66},{66,34},{35,67},{67,35},{3... | collective-permute-start | bytes 270344 | tf_op jit(solution)/shard_map/ppermute | solution.py:280
  16.4 6.9 %all-to-all-done = f32[32,16,128]{2,1,0:T(8,128)S(1)} async-done(((f32[32,16,128]{2,1,0:T(8,128)}), f32[32,16,128]{2,1,0:T(8,128)S(1)}, u32[]{:S(2)}, u32[]{:S(2)}) %all-to-all-start) | async-done | bytes 262176 | tf_op jit(solution)/shard_map/all_to_all | solution.py:303
  23.4 0.0 copy-done
  23.4 1.7 %shard_map.75 = (f32[4,128]{1,0:T(4,128)S(1)}, s32[8,128]{1,0:T(8,128)S(1)}) custom-call(s32[6,2048]{1,0:T(8,128)S(1)} %bitcast.14, f32[16,128]{1,0:T(8,128)S(1)} %get-tuple-element.12.shard_ref.zone_ref, s32[1,32]{1,0:T(1,128)} %bitcast.17, f32[512,128]{1,0:T(8,128)S(1)} %bitcast.12), custom_call_target="tpu_custom_call" | custom-call | flops 4294967296 | bytes 1048576 | tf_op jit(solution)/shard_map/pallas_call | solution.py:311
  25.1 0.0 collective-permute-done.2.first_ref
  25.1 0.0 collective-permute-done.3.second_ref
  25.1 1.3 %shard_map.77 = f32[640,128]{1,0:T(8,128)S(1)} custom-call(f32[25,24,128]{2,1,0:T(8,128)S(1)} %get-tuple-element.15.ext_ref, f32[11,16,128]{2,1,0:T(8,128)S(1)} %collective-permute-done.2.first_ref, f32[11,16,128]{2,1,0:T(8,128)S(1)} %collective-permute-done.3.second_ref, f32[512,128]{1,0:T(8,128)S(1)} %bitcast.13, f32[4,128]{1,0:T(4,128)S(1)} %get-tuple-element.18.smooth_ref), custom_call_target="tpu_custom_call" | custom-call | tf_op jit(solution)/shard_map/pallas_call | solution.py:318
  26.4 18.2 %all_to_all.10 = f32[128,1,640]{2,1,0:T(1,128)S(1)} all-to-all(f32[128,1,640]{2,1,0:T(1,128)S(1)} %bitcast.10), channel_id=1, replica_groups=mesh['gx'=4,'gy'=32] {'gy','gx'}, dimensions={0} | all-to-all | bytes 655360 | tf_op jit(solution)/shard_map/all_to_all | solution.py:319
  44.6 2.3 %shard_map.78 = f32[32,128]{1,0:T(8,128)} custom-call(s32[8,128]{1,0:T(8,128)S(1)} %get-tuple-element.13.meta_ref, f32[640,128]{1,0:T(8,128)S(1)} %bitcast.11), custom_call_target="tpu_custom_call" | custom-call | tf_op jit(solution)/shard_map/pallas_call | solution.py:321
Async XLA Ops:
  0.9 13.5 %collective-permute-start = (f32[25,8,128]{2,1,0:T(8,128)S(1)}, f32[25,8,128]{2,1,0:T(8,128)S(1)}, u32[]{:S(2)}, u32[]{:S(2)}) collective-permute-start(f32[25,8,128]{2,1,0:T(8,128)S(1)} %get-tuple-element.14.own_ref), channel_id=1, source_target_pairs={{0,1},{2,3},{4,5},{6,7},{8,9},{10,11},{12,13},{14,15},{16,17},{18,... | collective-permute-start | bytes 307208 | tf_op jit(solution)/shard_map/ppermute | solution.py:280
  2.4 12.0 %collective-permute-start.1 = (f32[25,8,128]{2,1,0:T(8,128)S(1)}, f32[25,8,128]{2,1,0:T(8,128)S(1)}, u32[]{:S(2)}, u32[]{:S(2)}) collective-permute-start(f32[25,8,128]{2,1,0:T(8,128)S(1)} %get-tuple-element.14.own_ref), channel_id=1, source_target_pairs={{1,2},{3,4},{5,6},{7,8},{9,10},{11,12},{13,14},{15,16},{17,18},{19... | collective-permute-start | bytes 307208 | tf_op jit(solution)/shard_map/ppermute | solution.py:280
  6.6 16.8 %all-to-all-start = ((f32[32,16,128]{2,1,0:T(8,128)}), f32[32,16,128]{2,1,0:T(8,128)S(1)}, u32[]{:S(2)}, u32[]{:S(2)}) async-start(f32[32,16,128]{2,1,0:T(8,128)} %shard_map.74), calls=%async_computation | async-start | bytes 524288 | tf_op jit(solution)/shard_map/all_to_all | solution.py:303
  14.4 9.0 %copy-start = (s32[2048,6]{0,1:T(8,128)S(1)}, s32[2048,6]{0,1:T(8,128)}, u32[]{:S(2)}) copy-start(s32[2048,6]{0,1:T(8,128)} %param.13) | copy-start | bytes 147460
  14.5 10.6 %collective-permute-start.2 = (f32[11,16,128]{2,1,0:T(8,128)S(1)}, f32[11,16,128]{2,1,0:T(8,128)S(1)}, u32[]{:S(2)}, u32[]{:S(2)}) collective-permute-start(f32[11,16,128]{2,1,0:T(8,128)S(1)} %get-tuple-element.16), channel_id=1, source_target_pairs={{0,32},{64,96},{32,0},{96,64},{1,33},{65,97},{33,1},{97,65},{2,34}... | collective-permute-start | bytes 270344 | tf_op jit(solution)/shard_map/ppermute | solution.py:280
  15.8 9.3 %collective-permute-start.3 = (f32[11,16,128]{2,1,0:T(8,128)S(1)}, f32[11,16,128]{2,1,0:T(8,128)S(1)}, u32[]{:S(2)}, u32[]{:S(2)}) collective-permute-start(f32[11,16,128]{2,1,0:T(8,128)S(1)} %get-tuple-element.17), channel_id=1, source_target_pairs={{32,64},{64,32},{33,65},{65,33},{34,66},{66,34},{35,67},{67,35},{3... | collective-permute-start | bytes 270344 | tf_op jit(solution)/shard_map/ppermute | solution.py:280

commit v4 on v3

--- a/solution.py
+++ b/solution.py
@@ -240,7 +240,7 @@
         out_ref[40 * eight : 40 * eight + 40] = jnp.concatenate([tile] * 8, axis=0)
 
 
-def place_kernel(meta_ref, all_ref, out_ref, smooth_ref, hot_ref, low_ref):
+def place_kernel(meta_ref, all_ref, out_ref, smooth_ref):
     start, held = meta_ref[0, 0], meta_ref[1, 0]
     sources = all_ref.shape[0] // 5
     half = sources // 2
@@ -250,18 +250,26 @@
     values = jnp.where(left, both[:half], turned[half:])
     slots = jnp.where(left, turned[:half], both[half:]).astype(I32) - start
     pieces = [piece.astype(F32) for piece in thirds(values)]
-    high, low = slots >> 7, slots & 127
     slot_rows = out_ref.shape[0]
-    high_row = iota((slot_rows, LANES), 0)
-    low_row = iota((LANES, LANES), 0)
-    for row in range(half):
-        match = high_row == high[row : row + 1]
-        for number in range(3):
-            hot_ref[number * slot_rows : (number + 1) * slot_rows, row * LANES : (row + 1) * LANES] = jnp.where(
-                match, pieces[number][row : row + 1], 0.0
-            ).astype(BF16)
-        low_ref[:, row * LANES : (row + 1) * LANES] = jnp.where(low_row == low[row : row + 1], 1.0, 0.0).astype(BF16)
-    sums = lax.dot_general(hot_ref[...], low_ref[...], (((1,), (1,)), ((), ())), preferred_element_type=F32)
+    high = jnp.clip(slots >> 7, -1, slot_rows).astype(F32)
+    low = (slots & 127).astype(F32)
+    high_row = iota((slot_rows, LANES), 0).astype(F32).astype(BF16)
+    low_row = iota((LANES, LANES), 0).astype(F32).astype(BF16)
+    one, zero = jnp.ones((), BF16), jnp.zeros((), BF16)
+
+    def spread(rows, row, count):
+        sixteen = jnp.broadcast_to(rows[row : row + 1], (16, LANES)).astype(BF16)
+        return jnp.concatenate([sixteen] * (count // 16), axis=0)
+
+    sums = jnp.zeros((3 * slot_rows, LANES), F32)
+    for pair in range(half // 2):
+        hot, place = [], []
+        for row in (2 * pair, 2 * pair + 1):
+            match = high_row == spread(high, row, slot_rows)
+            hot.append(jnp.concatenate([jnp.where(match, spread(piece, row, slot_rows), zero) for piece in pieces], axis=0))
+            place.append(jnp.where(low_row == spread(low, row, LANES), one, zero))
+        hot, place = jnp.concatenate(hot, axis=1), jnp.concatenate(place, axis=1)
+        sums = sums + lax.dot_general(hot, place, (((1,), (1,)), ((), ())), preferred_element_type=F32)
     sums = sums[0:slot_rows] + sums[slot_rows : 2 * slot_rows] + sums[2 * slot_rows :]
 
     top, shift = start >> 7, start & 127
@@ -322,11 +330,7 @@
         place_kernel,
         shape((slot_rows, LANES), F32),
         [VMEM, VMEM],
-        [
-            pltpu.VMEM((slot_rows + 8, LANES), F32),
-            pltpu.VMEM((3 * slot_rows, devices * 64), BF16),
-            pltpu.VMEM((LANES, devices * 64), BF16),
-        ],
+        [pltpu.VMEM((slot_rows + 8, LANES), F32)],
     )(meta, gathered.reshape(devices * 5, LANES))
     return out.reshape(slot_rows * LANES)
 

time: 47.2 us -> 46.4 us (0.983)
  Pallas kernels: 7 us -> 6.18 us
    pallas_call x1, Pallas kernels: 2.31 us -> 1.5 us  [body(): call(place_kernel, shape((slot_rows, LANES), F32), [VMEM, VMEM], [pltpu.V...]
where the time goes in v4:
time: 46.4 us; the launch traced here: 46.1 us
  blocking collectives  18.2 us (39%)
  starting transfers between devices  14.7 us (32%)
  waiting for transfers between devices  6.95 us (15%)
  Pallas kernels  6.18 us (13%)
    all_to_all x1, blocking collectives, body(): lax.all_to_all(rows.reshape(devices, 1, 5 * LANES), ('gy', 'gx'), 0, 0, t...  18.2 us
    all_to_all x1, starting transfers between devices, body(): lax.all_to_all(spread, 'gy', 0, 0, tiled=True)  7.76 us
    ppermute x4, starting transfers between devices, swap(): return lax.ppermute(array, axis, pairs + [(b, a) for a, b in pairs])  6.95 us
    all_to_all x1, waiting for transfers between devices, body(): lax.all_to_all(spread, 'gy', 0, 0, tiled=True)  6.94 us
    pallas_call x1, Pallas kernels, body(): call(smooth_kernel, [shape((shard_rows // across, LANES), F32), shape((8,...  1.7 us
    pallas_call x1, Pallas kernels, body(): call(place_kernel, shape((slot_rows, LANES), F32), [VMEM, VMEM], [pltpu.V...  1.5 us
    pallas_call x1, Pallas kernels, body(): call(sweep_kernel, shape((devices * 5, LANES), F32), [VMEM] * 5)  1.31 us
  transfers between devices with their start and end apart: 5, of which 1 were waited for; matrix products, arithmetic and copies ran while one was open for 0% of the time, Pallas kernels for 5%

profile of v4, /device:TPU:1, one launch (start us, length us, event | category | flops | bytes accessed | tf_op | source)
XLA Modules:
  0.0 46.1 jit_solution(15152552587046734689)
XLA Ops:
  0.0 0.9 %shard_map.73 = (f32[25,8,128]{2,1,0:T(8,128)S(1)}, f32[16,128]{1,0:T(8,128)S(1)}) custom-call(f32[8,8,128]{2,1,0:T(8,128)} %temp_ref.1, f32[8,8,128]{2,1,0:T(8,128)} %rock_ref.1, f32[8,8,128]{2,1,0:T(8,128)} %misfit_ref.1, s32[8,1,8]{2,1,0:T(1,128)} %bitcast.16, f32[16,128]{1,0:T(8,128)} %bitcast.15), custom_call_target="tpu_custom_call" | custom-call | tf_op jit(solution)/shard_map/pallas_call | solution.py:298
  0.9 1.5 %collective-permute-start = (f32[25,8,128]{2,1,0:T(8,128)S(1)}, f32[25,8,128]{2,1,0:T(8,128)S(1)}, u32[]{:S(2)}, u32[]{:S(2)}) collective-permute-start(f32[25,8,128]{2,1,0:T(8,128)S(1)} %get-tuple-element.14.own_ref), channel_id=1, source_target_pairs={{0,1},{2,3},{4,5},{6,7},{8,9},{10,11},{12,13},{14,15},{16,17},{18,... | collective-permute-start | bytes 307208 | tf_op jit(solution)/shard_map/ppermute | solution.py:288
  2.4 3.5 %collective-permute-start.1 = (f32[25,8,128]{2,1,0:T(8,128)S(1)}, f32[25,8,128]{2,1,0:T(8,128)S(1)}, u32[]{:S(2)}, u32[]{:S(2)}) collective-permute-start(f32[25,8,128]{2,1,0:T(8,128)S(1)} %get-tuple-element.14.own_ref), channel_id=1, source_target_pairs={{1,2},{3,4},{5,6},{7,8},{9,10},{11,12},{13,14},{15,16},{17,18},{19... | collective-permute-start | bytes 307208 | tf_op jit(solution)/shard_map/ppermute | solution.py:288
  5.9 0.7 %shard_map.74 = f32[32,16,128]{2,1,0:T(8,128)} custom-call(f32[16,128]{1,0:T(8,128)S(1)} %get-tuple-element.12.shard_ref.zone_ref), custom_call_target="tpu_custom_call" | custom-call | flops 34359738368 | bytes 1048576 | tf_op jit(solution)/shard_map/pallas_call | solution.py:305
  6.6 7.8 %all-to-all-start = ((f32[32,16,128]{2,1,0:T(8,128)}), f32[32,16,128]{2,1,0:T(8,128)S(1)}, u32[]{:S(2)}, u32[]{:S(2)}) async-start(f32[32,16,128]{2,1,0:T(8,128)} %shard_map.74), calls=%async_computation | async-start | bytes 524288 | tf_op jit(solution)/shard_map/all_to_all | solution.py:311
  14.4 0.0 copy-start
  14.4 0.0 collective-permute-done.first_ref
  14.4 0.0 collective-permute-done.1.second_ref
  14.4 0.1 shard_map.76
  14.5 1.3 %collective-permute-start.2 = (f32[11,16,128]{2,1,0:T(8,128)S(1)}, f32[11,16,128]{2,1,0:T(8,128)S(1)}, u32[]{:S(2)}, u32[]{:S(2)}) collective-permute-start(f32[11,16,128]{2,1,0:T(8,128)S(1)} %get-tuple-element.16), channel_id=1, source_target_pairs={{0,32},{64,96},{32,0},{96,64},{1,33},{65,97},{33,1},{97,65},{2,34}... | collective-permute-start | bytes 270344 | tf_op jit(solution)/shard_map/ppermute | solution.py:288
  15.8 0.7 %collective-permute-start.3 = (f32[11,16,128]{2,1,0:T(8,128)S(1)}, f32[11,16,128]{2,1,0:T(8,128)S(1)}, u32[]{:S(2)}, u32[]{:S(2)}) collective-permute-start(f32[11,16,128]{2,1,0:T(8,128)S(1)} %get-tuple-element.17), channel_id=1, source_target_pairs={{32,64},{64,32},{33,65},{65,33},{34,66},{66,34},{35,67},{67,35},{3... | collective-permute-start | bytes 270344 | tf_op jit(solution)/shard_map/ppermute | solution.py:288
  16.4 6.9 %all-to-all-done = f32[32,16,128]{2,1,0:T(8,128)S(1)} async-done(((f32[32,16,128]{2,1,0:T(8,128)}), f32[32,16,128]{2,1,0:T(8,128)S(1)}, u32[]{:S(2)}, u32[]{:S(2)}) %all-to-all-start) | async-done | bytes 262176 | tf_op jit(solution)/shard_map/all_to_all | solution.py:311
  23.4 0.0 copy-done
  23.4 1.7 %shard_map.75 = (f32[4,128]{1,0:T(4,128)S(1)}, s32[8,128]{1,0:T(8,128)S(1)}) custom-call(s32[6,2048]{1,0:T(8,128)S(1)} %bitcast.14, f32[16,128]{1,0:T(8,128)S(1)} %get-tuple-element.12.shard_ref.zone_ref, s32[1,32]{1,0:T(1,128)} %bitcast.17, f32[512,128]{1,0:T(8,128)S(1)} %bitcast.12), custom_call_target="tpu_custom_call" | custom-call | flops 4294967296 | bytes 1048576 | tf_op jit(solution)/shard_map/pallas_call | solution.py:319
  25.1 0.0 collective-permute-done.2.first_ref
  25.1 0.0 collective-permute-done.3.second_ref
  25.1 1.3 %shard_map.77 = f32[640,128]{1,0:T(8,128)S(1)} custom-call(f32[25,24,128]{2,1,0:T(8,128)S(1)} %get-tuple-element.15.ext_ref, f32[11,16,128]{2,1,0:T(8,128)S(1)} %collective-permute-done.2.first_ref, f32[11,16,128]{2,1,0:T(8,128)S(1)} %collective-permute-done.3.second_ref, f32[512,128]{1,0:T(8,128)S(1)} %bitcast.13, f32[4,128]{1,0:T(4,128)S(1)} %get-tuple-element.18.smooth_ref), custom_call_target="tpu_custom_call" | custom-call | tf_op jit(solution)/shard_map/pallas_call | solution.py:326
  26.4 18.2 %all_to_all.10 = f32[128,1,640]{2,1,0:T(1,128)S(1)} all-to-all(f32[128,1,640]{2,1,0:T(1,128)S(1)} %bitcast.10), channel_id=1, replica_groups=mesh['gx'=4,'gy'=32] {'gy','gx'}, dimensions={0} | all-to-all | bytes 655360 | tf_op jit(solution)/shard_map/all_to_all | solution.py:327
  44.6 1.5 %shard_map.78 = f32[32,128]{1,0:T(8,128)} custom-call(s32[8,128]{1,0:T(8,128)S(1)} %get-tuple-element.13.meta_ref, f32[640,128]{1,0:T(8,128)S(1)} %bitcast.11), custom_call_target="tpu_custom_call" | custom-call | tf_op jit(solution)/shard_map/pallas_call | solution.py:329
Async XLA Ops:
  0.9 13.5 %collective-permute-start = (f32[25,8,128]{2,1,0:T(8,128)S(1)}, f32[25,8,128]{2,1,0:T(8,128)S(1)}, u32[]{:S(2)}, u32[]{:S(2)}) collective-permute-start(f32[25,8,128]{2,1,0:T(8,128)S(1)} %get-tuple-element.14.own_ref), channel_id=1, source_target_pairs={{0,1},{2,3},{4,5},{6,7},{8,9},{10,11},{12,13},{14,15},{16,17},{18,... | collective-permute-start | bytes 307208 | tf_op jit(solution)/shard_map/ppermute | solution.py:288
  2.4 12.0 %collective-permute-start.1 = (f32[25,8,128]{2,1,0:T(8,128)S(1)}, f32[25,8,128]{2,1,0:T(8,128)S(1)}, u32[]{:S(2)}, u32[]{:S(2)}) collective-permute-start(f32[25,8,128]{2,1,0:T(8,128)S(1)} %get-tuple-element.14.own_ref), channel_id=1, source_target_pairs={{1,2},{3,4},{5,6},{7,8},{9,10},{11,12},{13,14},{15,16},{17,18},{19... | collective-permute-start | bytes 307208 | tf_op jit(solution)/shard_map/ppermute | solution.py:288
  6.6 16.8 %all-to-all-start = ((f32[32,16,128]{2,1,0:T(8,128)}), f32[32,16,128]{2,1,0:T(8,128)S(1)}, u32[]{:S(2)}, u32[]{:S(2)}) async-start(f32[32,16,128]{2,1,0:T(8,128)} %shard_map.74), calls=%async_computation | async-start | bytes 524288 | tf_op jit(solution)/shard_map/all_to_all | solution.py:311
  14.4 9.0 %copy-start = (s32[2048,6]{0,1:T(8,128)S(1)}, s32[2048,6]{0,1:T(8,128)}, u32[]{:S(2)}) copy-start(s32[2048,6]{0,1:T(8,128)} %param.13) | copy-start | bytes 147460
  14.5 10.6 %collective-permute-start.2 = (f32[11,16,128]{2,1,0:T(8,128)S(1)}, f32[11,16,128]{2,1,0:T(8,128)S(1)}, u32[]{:S(2)}, u32[]{:S(2)}) collective-permute-start(f32[11,16,128]{2,1,0:T(8,128)S(1)} %get-tuple-element.16), channel_id=1, source_target_pairs={{0,32},{64,96},{32,0},{96,64},{1,33},{65,97},{33,1},{97,65},{2,34}... | collective-permute-start | bytes 270344 | tf_op jit(solution)/shard_map/ppermute | solution.py:288
  15.8 9.3 %collective-permute-start.3 = (f32[11,16,128]{2,1,0:T(8,128)S(1)}, f32[11,16,128]{2,1,0:T(8,128)S(1)}, u32[]{:S(2)}, u32[]{:S(2)}) collective-permute-start(f32[11,16,128]{2,1,0:T(8,128)S(1)} %get-tuple-element.17), channel_id=1, source_target_pairs={{32,64},{64,32},{33,65},{65,33},{34,66},{66,34},{35,67},{67,35},{3... | collective-permute-start | bytes 270344 | tf_op jit(solution)/shard_map/ppermute | solution.py:288

commit v5 on v4

--- a/solution.py
+++ b/solution.py
@@ -11,6 +11,7 @@
 SMOOTHING = 0.5
 SENS_SCALE = 0.03125
 LANES = 128
+ROWS = 17
 F32 = jnp.float32
 BF16 = jnp.bfloat16
 I32 = jnp.int32
@@ -54,7 +55,7 @@
     return jnp.broadcast_to(jnp.sum(picked, axis=1, keepdims=True), tile.shape)
 
 
-def pack_kernel(temp_ref, rock_ref, misfit_ref, map_ref, zone_ref, pack_ref, shard_ref, map_buf, sems):
+def pack_kernel(temp_ref, rock_ref, misfit_ref, map_ref, zone_ref, near_ref, tally_ref, pack_ref, shard_ref, table_ref, counts_ref, map_buf, sems):
     east, north = rock_ref.shape[0], rock_ref.shape[1]
     copies = [
         pltpu.make_async_copy(source, target, sems.at[number])
@@ -65,6 +66,8 @@
                 (rock_ref, pack_ref.at[pl.ds(0, east)]),
                 (misfit_ref, pack_ref.at[pl.ds(east, east)]),
                 (temp_ref, pack_ref.at[pl.ds(2 * east, east)]),
+                (near_ref, table_ref),
+                (tally_ref, counts_ref),
             ]
         )
     ]
@@ -83,10 +86,23 @@
         copy.wait()
 
 
-def spread_kernel(shard_ref, spread_ref):
+def spread_kernel(shard_ref, near_ref, spread_ref, lists_ref):
     shard = shard_ref[...]
-    for other in range(spread_ref.shape[0]):
-        spread_ref[other] = shard
+    tiles = near_ref.shape[1] // LANES
+    for tile in range(tiles):
+        lists_ref[8 * tile : 8 * tile + NBRS] = near_ref[:, tile * LANES : (tile + 1) * LANES].astype(F32)
+    for other in range(2 * tiles):
+        spread_ref[other * ROWS : other * ROWS + 16] = shard
+    group = iota((tiles, LANES), 1) >> 4
+    first = lax.axis_index("gx") * 16
+    for odd in range(2):
+        ids = jnp.zeros((tiles, LANES), F32)
+        for number in range(NBRS):
+            moved = pltpu.roll(
+                lists_ref[pl.ds(number, tiles, stride=8), :], (2 * LANES + 16 * number - 64 * odd - first) & 127, 1
+            )
+            ids = jnp.where(group == number, moved, ids)
+        spread_ref[pl.ds(16 + odd * ROWS, tiles, stride=2 * ROWS), :] = ids
 
 
 def extend_kernel(own_ref, first_ref, second_ref, ext_ref, slab_a_ref, slab_b_ref):
@@ -117,73 +133,107 @@
         begin = end
 
 
-def smooth_kernel(adjacency_ref, zone_ref, tally_ref, table_ref, out_ref, meta_ref, tally_buf, sem):
-    copy = pltpu.make_async_copy(tally_ref, tally_buf, sem)
-    copy.start()
-    rows = out_ref.shape[0]
-    count = rows * LANES
-    high_size = table_ref.shape[0]
-    gx = lax.axis_index("gx")
-    pieces = jnp.concatenate(thirds(jnp.transpose(table_ref[...])), axis=0)
-    offset = pl.multiple_of(gx * count, count)
-    high_row = iota((high_size, count), 0)
-    low_row = iota((LANES, count), 0)
-    total = jnp.zeros((LANES, count), F32)
-    for k in range(NBRS):
-        ids = adjacency_ref[k : k + 1, pl.ds(offset, count)]
-        hot = jnp.where(high_row == (ids >> 7), 1.0, 0.0).astype(BF16)
+def gains(ids, pieces):
+    ids = ids.astype(I32)
+    rows, lanes = ids >> 7, iota(ids.shape, 1)
+    hot = jnp.concatenate(
+        [jnp.where(rows == lanes + LANES * part, 1.0, 0.0).astype(BF16) for part in range(pieces.shape[1] // LANES)], axis=1
+    )
+    found = lax.dot_general(hot, pieces, (((1,), (1,)), ((), ())), preferred_element_type=F32)
+    found = found[:, 0:LANES] + found[:, LANES : 2 * LANES] + found[:, 2 * LANES :]
+    log = jnp.sum(jnp.where(lanes == (ids & 127), found, 0.0), axis=1, keepdims=True)
+    return jnp.exp(jnp.broadcast_to(log, ids.shape))
+
+
+def smooth_kernel(all_ref, ext_ref, tally_ref, out_ref, meta_ref, pieces_ref, gain_ref, term_ref):
+    gx, gy = lax.axis_index("gx"), lax.axis_index("gy")
+    shards = all_ref.shape[0] // ROWS
+    table = jnp.concatenate([all_ref[ROWS * shard : ROWS * shard + 16] for shard in range(shards)], axis=0)
+    high_size = table.shape[0]
+    pieces = jnp.concatenate(thirds(jnp.transpose(table)), axis=0)
+    pieces_ref[...] = pieces
+
+    lane = iota((24, LANES), 1)
+    ids = all_ref[pl.ds(16, shards, stride=ROWS), :]
+    rest = jnp.concatenate([pltpu.roll(ids[24:], 96 - 32 * part, 1) for part in range(3)], axis=0)
+    ids = jnp.where(lane < 96, ids[:24], rest).astype(I32)
+    high, low = ids >> 7, ids & 127
+    high_row = iota((high_size, LANES), 0)
+    low_row = iota((LANES, LANES), 0)
+    near = []
+    for chunk in range(6):
+        rows = range(4 * chunk, 4 * chunk + 4)
+        hot = jnp.concatenate(
+            [jnp.where(high_row == high[row : row + 1], 1.0, 0.0).astype(BF16) for row in rows], axis=1
+        )
         found = jnp.dot(pieces, hot, preferred_element_type=F32)
         found = found[0:LANES] + found[LANES : 2 * LANES] + found[2 * LANES :]
-        total = total + jnp.where(low_row == (ids & 127), found, 0.0)
-    near = jnp.sum(total, axis=0, keepdims=True)
-    own = zone_ref[pl.ds(gx * rows, rows), :]
-    for row in range(rows):
-        out_ref[row : row + 1] = SMOOTHING * (
-            NBRS * own[row : row + 1] - near[:, row * LANES : (row + 1) * LANES]
-        )
-    copy.wait()
-    tally = tally_buf[...].astype(F32)
-    rank, gy = iota(tally.shape, 1), lax.axis_index("gy")
-    start = jnp.sum(jnp.where(rank < gy, tally, 0.0), axis=1, keepdims=True)
-    held = jnp.sum(jnp.where(rank == gy, tally, 0.0), axis=1, keepdims=True)
-    meta_ref[...] = jnp.where(iota((8, LANES), 0) == 0, start, held).astype(I32)
-
-
-def sweep_kernel(ext_ref, first_ref, second_ref, table_ref, smooth_ref, out_ref):
+        for number, row in enumerate(rows):
+            picked = jnp.where(low_row == low[row : row + 1], found[:, number * LANES : (number + 1) * LANES], 0.0)
+            near.append(jnp.sum(picked, axis=0, keepdims=True))
+    near = jnp.concatenate(near, axis=0)
+    lane = iota((8, LANES), 1)
+    rest = jnp.zeros((8, LANES), F32)
+    for part in range(3):
+        moved = pltpu.roll(near[8 * part : 8 * part + 8], 32 + 32 * part, 1)
+        rest = jnp.where((lane >> 5) == part, moved, rest)
+    near = jnp.concatenate([near, rest], axis=0)
+    total = near
+    for number in range(1, NBRS):
+        total = total + pltpu.roll(near, LANES - 16 * number, 1)
+    own = all_ref[pl.ds(gy >> 1, shards, stride=ROWS), :]
+    own = pltpu.roll(own, (2 * LANES - (gy & 1) * 64 - gx * 16) & 127, 1)
+    term_ref[...] = SMOOTHING * (NBRS * own - total)
+
+    mine = (gy * 4 + gx) & 7
+    lane = iota((16, LANES), 1)
+    first = pltpu.roll(term_ref[pl.ds(0, 16, stride=2), :], mine * 16, 1)
+    second = pltpu.roll(term_ref[pl.ds(1, 16, stride=2), :], (mine * 16 + 64) & 127, 1)
+    terms = jnp.where((lane >> 4) == mine, first, jnp.where((lane >> 4) == ((mine + 4) & 7), second, 0.0))
+
+    owners = tally_ref.shape[1]
+    tally = jnp.broadcast_to(tally_ref[...].astype(F32), (owners, owners))
+    before = iota((owners, owners), 1) < iota((owners, owners), 0)
+    start = jnp.sum(jnp.where(before, tally, 0.0), axis=1, keepdims=True)
+    start = jnp.broadcast_to(start, (owners, LANES)).astype(I32)
+    lane = iota((owners, LANES), 1)
+    slot = jnp.where((lane >> 4) == mine, 0, 2048) + (gy * 4 + gx) * 16 + (lane & 15)
+    wanted = (start >> 12) + jnp.where(slot < (start & 4095), 1, 0)
+    chosen = jnp.zeros((owners, LANES), F32)
+    for number in range(16):
+        chosen = chosen + jnp.where(wanted == number, terms[number : number + 1], 0.0)
+    out_ref[...] = chosen
+
+    row = tally[0:1]
+    rank = iota(row.shape, 1)
+    begin = jnp.sum(jnp.where(rank < gy, row, 0.0), axis=1, keepdims=True)
+    held = jnp.sum(jnp.where(rank == gy, row, 0.0), axis=1, keepdims=True)
+    meta_ref[...] = jnp.where(iota((8, LANES), 0) == 0, begin, held).astype(I32)
+
+    gain_ref[...] = gains(jnp.concatenate([column(ext_ref[8], x) for x in range(8)], axis=0), pieces)
+
+
+def sweep_kernel(ext_ref, first_ref, second_ref, pieces_ref, gain_ref, smooth_ref, out_ref):
     shape = (16, LANES)
     lane = iota(shape, 1)
     first, last = lane == 0, lane == LANES - 1
     even = lax.axis_index("gx") % 2 == 0
     one, two = first_ref[...], second_ref[...]
     west, east = jnp.where(even, two, one), jnp.where(even, one, two)
-
-    own_ids = ext_ref[8]
-    ids = [column(own_ids, x) for x in range(8)]
-    ids += [column(west[10], step) for step in range(5)]
-    ids += [column(east[10], step) for step in range(5)]
-    own_columns = ids[:8]
-    ids = jnp.concatenate(ids, axis=0).astype(I32)
-    places = ids.shape[0]
-    rows = ids >> 7
-    lanes = iota((places, LANES), 1)
-    hot = jnp.concatenate(
-        [jnp.where(rows == lanes + LANES * part, 1.0, 0.0).astype(BF16) for part in range(table_ref.shape[0] // LANES)],
-        axis=1,
-    )
-    found = sum(jnp.dot(hot, piece, preferred_element_type=F32) for piece in thirds(table_ref[...]))
-    log = jnp.sum(jnp.where(lanes == (ids & 127), found, 0.0), axis=1, keepdims=True)
-    gain = jnp.exp(jnp.broadcast_to(log, (places, LANES)))
+    own_columns = [column(ext_ref[8], x) for x in range(8)]
+    ids = [column(west[10], step) for step in range(5)] + [column(east[10], step) for step in range(5)]
+    beside = gains(jnp.concatenate(ids, axis=0), pieces_ref[...])
 
     conduct, source, heat, own_sides = {}, {}, {}, {}
     for x in range(8):
-        wide = ext_ref[x] * gain[24 * x : 24 * x + 24]
+        wide = ext_ref[x] * gain_ref[24 * x : 24 * x + 24]
         conduct[x] = wide[4:20]
         own_sides[x] = wide[3:19] + wide[5:21]
         source[x] = ext_ref[9 + x, 0:16]
         heat[x] = ext_ref[17 + x, 0:16]
     for step in range(5):
-        conduct[step - 5] = west[step] * gain[192 + 16 * step : 208 + 16 * step]
-        conduct[step + 8] = east[step] * gain[272 + 16 * step : 288 + 16 * step]
+        conduct[step - 5] = west[step] * beside[16 * step : 16 * step + 16]
+        conduct[step + 8] = east[step] * beside[80 + 16 * step : 96 + 16 * step]
     for step in range(4):
         source[step - 4] = west[5 + step]
         source[step + 8] = east[5 + step]
@@ -235,16 +285,16 @@
     turned = jnp.transpose(stacked)
     sums = jnp.sum(turned, axis=0, keepdims=True)
     row = jnp.where(iota((1, LANES), 1) < 64, sums, turned[0:1])
-    tile = jnp.concatenate([smooth_ref[...], row], axis=0)
-    for eight in range(out_ref.shape[0] // 40):
-        out_ref[40 * eight : 40 * eight + 40] = jnp.concatenate([tile] * 8, axis=0)
+    odd = (iota((8, LANES), 0) & 1) == 1
+    for owner in range(smooth_ref.shape[0]):
+        out_ref[8 * owner : 8 * owner + 8] = jnp.where(odd, smooth_ref[owner : owner + 1], row)
 
 
 def place_kernel(meta_ref, all_ref, out_ref, smooth_ref):
     start, held = meta_ref[0, 0], meta_ref[1, 0]
-    sources = all_ref.shape[0] // 5
+    sources = all_ref.shape[0] // 2
     half = sources // 2
-    both = all_ref[pl.ds(4, sources, stride=5), :]
+    both = all_ref[pl.ds(0, sources, stride=2), :]
     turned = pltpu.roll(both, 64, 1)
     left = iota((half, LANES), 1) < 64
     values = jnp.where(left, both[:half], turned[half:])
@@ -272,11 +322,16 @@
         sums = sums + lax.dot_general(hot, place, (((1,), (1,)), ((), ())), preferred_element_type=F32)
     sums = sums[0:slot_rows] + sums[slot_rows : 2 * slot_rows] + sums[2 * slot_rows :]
 
-    top, shift = start >> 7, start & 127
-    for row in range(slot_rows + 1):
-        zone_row = jnp.minimum(top + row, sources * 4 - 1)
-        smooth_ref[row : row + 1, :] = all_ref[pl.ds((zone_row >> 2) * 5 + (zone_row & 3), 1), :]
-    moved = pltpu.roll(smooth_ref[...], LANES - shift, 1)
+    terms = all_ref[pl.ds(1, sources, stride=2), :].reshape(sources // 8, 8, LANES)
+    group, source = iota((1, 8, LANES), 2) >> 4, iota((1, 8, LANES), 1)
+    first = jnp.sum(jnp.where(group == source, terms, 0.0), axis=1)
+    second = pltpu.roll(jnp.sum(jnp.where(group == ((source + 4) & 7), terms, 0.0), axis=1), 64, 1)
+    for copy in range(2):
+        smooth_ref[32 * copy : 32 * copy + 16] = first
+        smooth_ref[32 * copy + 16 : 32 * copy + 32] = second
+    smooth_ref[64:72] = first[0:8]
+    top, shift = (start >> 7) & 31, start & 127
+    moved = pltpu.roll(smooth_ref[pl.ds(top, 40), :], LANES - shift, 1)
     lane = iota((slot_rows, LANES), 1)
     smooth = jnp.where(lane < LANES - shift, moved[0:slot_rows], moved[1 : slot_rows + 1])
     within = iota((slot_rows, LANES), 0) * LANES + lane
@@ -295,20 +350,39 @@
     shard_rows = zone_log.shape[0] // LANES
     zone = zone_log.reshape(shard_rows, LANES)
     shape = jax.ShapeDtypeStruct
-    pack, shard = call(
+    pack, shard, near, counts = call(
         pack_kernel,
-        [shape((3 * east + 1, north, depth), F32), shape((shard_rows, LANES), F32)],
-        [HBM] * 5,
-        [pltpu.VMEM((east, 1, north), I32), pltpu.SemaphoreType.DMA((5,))],
-    )(*map(in_hbm, (temp, rock, misfit, jnp.transpose(zone_map, (0, 2, 1)), zone)))
+        [
+            shape((3 * east + 1, north, depth), F32),
+            shape((shard_rows, LANES), F32),
+            shape((NBRS, zone_log.shape[0]), I32),
+            shape((1, along), I32),
+        ],
+        [HBM] * 7,
+        [pltpu.VMEM((east, 1, north), I32), pltpu.SemaphoreType.DMA((7,))],
+    )(
+        *map(
+            in_hbm,
+            (
+                temp,
+                rock,
+                misfit,
+                jnp.transpose(zone_map, (0, 2, 1)),
+                zone,
+                jnp.transpose(adjacency),
+                tally.reshape(1, along),
+            ),
+        )
+    )
     y_first, y_second = swap(pack, "gy", 0), swap(pack, "gy", 1)
     spread = call(
         spread_kernel,
-        shape((along, shard_rows, LANES), F32),
-        [VMEM],
+        shape((along * ROWS, LANES), F32),
+        [VMEM, VMEM],
+        [pltpu.VMEM((8 * shard_rows, LANES), F32)],
         cost=pl.CostEstimate(flops=1 << 35, bytes_accessed=1 << 20, transcendentals=0),
-    )(shard)
-    table = lax.all_to_all(spread, "gy", 0, 0, tiled=True).reshape(along * shard_rows, LANES)
+    )(shard, near)
+    shards = lax.all_to_all(spread.reshape(along, 1, ROWS * LANES), "gy", 0, 0, tiled=True).reshape(along * ROWS, LANES)
     ext, slab_a, slab_b = call(
         extend_kernel,
         [shape((25, 24, LANES), F32), shape((11, 16, LANES), F32), shape((11, 16, LANES), F32)],
@@ -316,22 +390,27 @@
         cost=pl.CostEstimate(flops=1 << 37, bytes_accessed=1 << 20, transcendentals=0),
     )(pack, y_first, y_second)
     x_first, x_second = swap(slab_a, "gx", 0), swap(slab_b, "gx", 1)
-    smooth, meta = call(
+    smooth, meta, pieces, gain = call(
         smooth_kernel,
-        [shape((shard_rows // across, LANES), F32), shape((8, LANES), I32)],
-        [VMEM, VMEM, HBM, VMEM],
-        [pltpu.VMEM((1, along), I32), pltpu.SemaphoreType.DMA],
+        [
+            shape((along, LANES), F32),
+            shape((8, LANES), I32),
+            shape((3 * LANES, along * shard_rows), BF16),
+            shape((east * 24, LANES), F32),
+        ],
+        [VMEM] * 3,
+        [pltpu.VMEM((along, LANES), F32)],
         cost=pl.CostEstimate(flops=1 << 32, bytes_accessed=1 << 20, transcendentals=0),
-    )(jnp.transpose(adjacency), shard, in_hbm(tally.reshape(1, along)), table)
-    rows = call(sweep_kernel, shape((devices * 5, LANES), F32), [VMEM] * 5)(ext, x_first, x_second, table, smooth)
-    gathered = lax.all_to_all(rows.reshape(devices, 1, 5 * LANES), ("gy", "gx"), 0, 0, tiled=True)
+    )(shards, ext, counts)
+    rows = call(sweep_kernel, shape((devices * 2, LANES), F32), [VMEM] * 6)(ext, x_first, x_second, pieces, gain, smooth)
+    gathered = lax.all_to_all(rows.reshape(devices, 1, 2 * LANES), ("gy", "gx"), 0, 0, tiled=True)
     slot_rows = 2 * shard_rows
     out = call(
         place_kernel,
         shape((slot_rows, LANES), F32),
         [VMEM, VMEM],
-        [pltpu.VMEM((slot_rows + 8, LANES), F32)],
-    )(meta, gathered.reshape(devices * 5, LANES))
+        [pltpu.VMEM((72, LANES), F32)],
+    )(meta, gathered.reshape(devices * 2, LANES))
     return out.reshape(slot_rows * LANES)
 
 

time: 46.4 us -> 45.1 us (0.972)
  blocking collectives: 18.2 us -> 16 us
    all_to_all x1, blocking collectives: 18.2 us -> 16 us  [body(): lax.all_to_all(rows.reshape(devices, 1, 2 * LANES), ('gy', 'gx'), 0, 0, t...]
  transfers between devices with their start and end apart: 5 -> 5, of which waited for: 1 -> 1; matrix products, arithmetic and copies ran while one was open for 0% -> 0% of each run, Pallas kernels for 5% -> 6%
where the time goes in v5:
time: 45.1 us; the launch traced here: 44.8 us
  blocking collectives  16 us (35%)
  starting transfers between devices  15.1 us (33%)
  waiting for transfers between devices  7.12 us (16%)
  Pallas kernels  6.49 us (14%)
    all_to_all x1, blocking collectives, body(): lax.all_to_all(rows.reshape(devices, 1, 2 * LANES), ('gy', 'gx'), 0, 0, t...  16 us
    all_to_all x1, starting transfers between devices, body(): lax.all_to_all(spread.reshape(along, 1, ROWS * LANES), 'gy', 0, 0, tiled=...  8.14 us
    all_to_all x1, waiting for transfers between devices, body(): lax.all_to_all(spread.reshape(along, 1, ROWS * LANES), 'gy', 0, 0, tiled=...  7.11 us
    ppermute x4, starting transfers between devices, swap(): return lax.ppermute(array, axis, pairs + [(b, a) for a, b in pairs])  6.94 us
    pallas_call x1, Pallas kernels, body(): call(smooth_kernel, [shape((along, LANES), F32), shape((8, LANES), I32),...  1.94 us
    pallas_call x1, Pallas kernels, body(): call(place_kernel, shape((slot_rows, LANES), F32), [VMEM, VMEM], [pltpu.V...  1.51 us
    pallas_call x1, Pallas kernels, body(): call(sweep_kernel, shape((devices * 2, LANES), F32), [VMEM] * 6)  1.15 us
    pallas_call x1, Pallas kernels, body(): call(pack_kernel, [shape((3 * east + 1, north, depth), F32), shape((shard...  0.99 us
  transfers between devices with their start and end apart: 5, of which 1 were waited for; matrix products, arithmetic and copies ran while one was open for 0% of the time, Pallas kernels for 6%

profile of v5, /device:TPU:1, one launch (start us, length us, event | category | flops | bytes accessed | tf_op | source)
XLA Modules:
  0.0 44.8 jit_solution(12128498675324552188)
XLA Ops:
  0.0 1.0 %shard_map.73 = (f32[25,8,128]{2,1,0:T(8,128)S(1)}, f32[16,128]{1,0:T(8,128)S(1)}, s32[6,2048]{1,0:T(8,128)S(1)}, s32[1,32]{1,0:T(1,128)S(1)}) custom-call(f32[8,8,128]{2,1,0:T(8,128)} %temp_ref.1, f32[8,8,128]{2,1,0:T(8,128)} %rock_ref.1, f32[8,8,128]{2,1,0:T(8,128)} %misfit_ref.1, s32[8,1,8]{2,1,0:T(1,128)} %bitcast.16, f32[16,128]{1,0:T(8,128)} %bitcast.15, ...), custom_call_target="tpu_custom_call" | custom-call | tf_op jit(solution)/shard_map/pallas_call | solution.py:353
  1.0 4.9 %collective-permute-start.1 = (f32[25,8,128]{2,1,0:T(8,128)S(1)}, f32[25,8,128]{2,1,0:T(8,128)S(1)}, u32[]{:S(2)}, u32[]{:S(2)}) collective-permute-start(f32[25,8,128]{2,1,0:T(8,128)S(1)} %get-tuple-element.18.own_ref), channel_id=1, source_target_pairs={{1,2},{3,4},{5,6},{7,8},{9,10},{11,12},{13,14},{15,16},{17,18},{19... | collective-permute-start | bytes 307208 | tf_op jit(solution)/shard_map/ppermute | solution.py:343
  5.9 0.1 collective-permute-start
  6.0 0.8 %shard_map.74 = f32[544,128]{1,0:T(8,128)} custom-call(f32[16,128]{1,0:T(8,128)S(1)} %get-tuple-element.16.shard_ref, s32[6,2048]{1,0:T(8,128)S(1)} %get-tuple-element.17.near_ref), custom_call_target="tpu_custom_call" | custom-call | flops 34359738368 | bytes 1048576 | tf_op jit(solution)/shard_map/pallas_call | solution.py:378
  6.8 8.1 %all-to-all-start = ((f32[32,1,2176]{2,1,0:T(1,128)}), f32[32,1,2176]{2,1,0:T(1,128)S(1)}, u32[]{:S(2)}, u32[]{:S(2)}) async-start(f32[32,1,2176]{2,1,0:T(1,128)} %bitcast.5), calls=%async_computation | async-start | bytes 557056 | tf_op jit(solution)/shard_map/all_to_all | solution.py:385
  15.0 0.0 collective-permute-done.1.second_ref
  15.0 0.0 collective-permute-done.first_ref
  15.0 0.1 shard_map.75
  15.1 1.3 %collective-permute-start.2 = (f32[11,16,128]{2,1,0:T(8,128)S(1)}, f32[11,16,128]{2,1,0:T(8,128)S(1)}, u32[]{:S(2)}, u32[]{:S(2)}) collective-permute-start(f32[11,16,128]{2,1,0:T(8,128)S(1)} %get-tuple-element.22), channel_id=1, source_target_pairs={{0,32},{64,96},{32,0},{96,64},{1,33},{65,97},{33,1},{97,65},{2,34}... | collective-permute-start | bytes 270344 | tf_op jit(solution)/shard_map/ppermute | solution.py:343
  16.4 0.7 %collective-permute-start.3 = (f32[11,16,128]{2,1,0:T(8,128)S(1)}, f32[11,16,128]{2,1,0:T(8,128)S(1)}, u32[]{:S(2)}, u32[]{:S(2)}) collective-permute-start(f32[11,16,128]{2,1,0:T(8,128)S(1)} %get-tuple-element.23), channel_id=1, source_target_pairs={{32,64},{64,32},{33,65},{65,33},{34,66},{66,34},{35,67},{67,35},{3... | collective-permute-start | bytes 270344 | tf_op jit(solution)/shard_map/ppermute | solution.py:343
  17.0 7.1 %all-to-all-done = f32[32,1,2176]{2,1,0:T(1,128)S(1)} async-done(((f32[32,1,2176]{2,1,0:T(1,128)}), f32[32,1,2176]{2,1,0:T(1,128)S(1)}, u32[]{:S(2)}, u32[]{:S(2)}) %all-to-all-start) | async-done | bytes 278560 | tf_op jit(solution)/shard_map/all_to_all | solution.py:385
  24.1 1.9 %shard_map.76 = (f32[32,128]{1,0:T(8,128)S(1)}, s32[8,128]{1,0:T(8,128)S(1)}, bf16[384,512]{1,0:T(8,128)(2,1)S(1)}, f32[192,128]{1,0:T(8,128)S(1)}) custom-call(f32[544,128]{1,0:T(8,128)S(1)} %bitcast.13, f32[25,24,128]{2,1,0:T(8,128)S(1)} %get-tuple-element.19.ext_ref, s32[1,32]{1,0:T(1,128)S(1)} %get-tuple-element.20.tally_ref), custom_call_target="tpu_custom_call" | custom-call | flops 4294967296 | bytes 1048576 | tf_op jit(solution)/shard_map/pallas_call | solution.py:393
  26.1 0.0 collective-permute-done.2.first_ref
  26.1 0.0 collective-permute-done.3.second_ref
  26.1 1.1 %shard_map.77 = f32[256,128]{1,0:T(8,128)S(1)} custom-call(f32[25,24,128]{2,1,0:T(8,128)S(1)} %get-tuple-element.19.ext_ref, f32[11,16,128]{2,1,0:T(8,128)S(1)} %collective-permute-done.2.first_ref, f32[11,16,128]{2,1,0:T(8,128)S(1)} %collective-permute-done.3.second_ref, bf16[384,512]{1,0:T(8,128)(2,1)S(1)} %get-tuple-element.24.pieces_ref, ...), custom_call_target="tpu_custom_call" | custom-call | tf_op jit(solution)/shard_map/pallas_call | solution.py:405
  27.3 16.0 %all_to_all.10 = f32[128,1,256]{2,1,0:T(1,128)S(1)} all-to-all(f32[128,1,256]{2,1,0:T(1,128)S(1)} %bitcast.11), channel_id=1, replica_groups=mesh['gx'=4,'gy'=32] {'gy','gx'}, dimensions={0} | all-to-all | bytes 262144 | tf_op jit(solution)/shard_map/all_to_all | solution.py:406
  43.3 1.5 %shard_map.78 = f32[32,128]{1,0:T(8,128)} custom-call(s32[8,128]{1,0:T(8,128)S(1)} %get-tuple-element.21.meta_ref, f32[256,128]{1,0:T(8,128)S(1)} %bitcast.12), custom_call_target="tpu_custom_call" | custom-call | tf_op jit(solution)/shard_map/pallas_call | solution.py:408
Async XLA Ops:
  1.0 14.0 %collective-permute-start.1 = (f32[25,8,128]{2,1,0:T(8,128)S(1)}, f32[25,8,128]{2,1,0:T(8,128)S(1)}, u32[]{:S(2)}, u32[]{:S(2)}) collective-permute-start(f32[25,8,128]{2,1,0:T(8,128)S(1)} %get-tuple-element.18.own_ref), channel_id=1, source_target_pairs={{1,2},{3,4},{5,6},{7,8},{9,10},{11,12},{13,14},{15,16},{17,18},{19... | collective-permute-start | bytes 307208 | tf_op jit(solution)/shard_map/ppermute | solution.py:343
  5.9 9.1 %collective-permute-start = (f32[25,8,128]{2,1,0:T(8,128)S(1)}, f32[25,8,128]{2,1,0:T(8,128)S(1)}, u32[]{:S(2)}, u32[]{:S(2)}) collective-permute-start(f32[25,8,128]{2,1,0:T(8,128)S(1)} %get-tuple-element.18.own_ref), channel_id=1, source_target_pairs={{0,1},{2,3},{4,5},{6,7},{8,9},{10,11},{12,13},{14,15},{16,17},{18,... | collective-permute-start | bytes 307208 | tf_op jit(solution)/shard_map/ppermute | solution.py:343
  6.8 17.3 %all-to-all-start = ((f32[32,1,2176]{2,1,0:T(1,128)}), f32[32,1,2176]{2,1,0:T(1,128)S(1)}, u32[]{:S(2)}, u32[]{:S(2)}) async-start(f32[32,1,2176]{2,1,0:T(1,128)} %bitcast.5), calls=%async_computation | async-start | bytes 557056 | tf_op jit(solution)/shard_map/all_to_all | solution.py:385
  15.1 11.0 %collective-permute-start.2 = (f32[11,16,128]{2,1,0:T(8,128)S(1)}, f32[11,16,128]{2,1,0:T(8,128)S(1)}, u32[]{:S(2)}, u32[]{:S(2)}) collective-permute-start(f32[11,16,128]{2,1,0:T(8,128)S(1)} %get-tuple-element.22), channel_id=1, source_target_pairs={{0,32},{64,96},{32,0},{96,64},{1,33},{65,97},{33,1},{97,65},{2,34}... | collective-permute-start | bytes 270344 | tf_op jit(solution)/shard_map/ppermute | solution.py:343
  16.4 9.7 %collective-permute-start.3 = (f32[11,16,128]{2,1,0:T(8,128)S(1)}, f32[11,16,128]{2,1,0:T(8,128)S(1)}, u32[]{:S(2)}, u32[]{:S(2)}) collective-permute-start(f32[11,16,128]{2,1,0:T(8,128)S(1)} %get-tuple-element.23), channel_id=1, source_target_pairs={{32,64},{64,32},{33,65},{65,33},{34,66},{66,34},{35,67},{67,35},{3... | collective-permute-start | bytes 270344 | tf_op jit(solution)/shard_map/ppermute | solution.py:343

commit v6 on v5

--- a/solution.py
+++ b/solution.py
@@ -28,14 +28,14 @@
     return pltpu.with_memory_space_constraint(array, pltpu.HBM)
 
 
-def call(kernel, outs, in_specs, scratch=(), cost=None):
+def call(kernel, outs, in_specs, scratch=(), cost=None, out_specs=None):
     one = not isinstance(outs, (list, tuple))
     shapes = [outs] if one else list(outs)
     return pl.pallas_call(
         kernel,
         out_shape=shapes[0] if one else shapes,
         in_specs=in_specs,
-        out_specs=VMEM if one else [VMEM] * len(shapes),
+        out_specs=out_specs or (VMEM if one else [VMEM] * len(shapes)),
         scratch_shapes=list(scratch),
         cost_estimate=cost,
         compiler_params=pltpu.CompilerParams(vmem_limit_bytes=32 << 20),
@@ -55,44 +55,32 @@
     return jnp.broadcast_to(jnp.sum(picked, axis=1, keepdims=True), tile.shape)
 
 
-def pack_kernel(temp_ref, rock_ref, misfit_ref, map_ref, zone_ref, near_ref, tally_ref, pack_ref, shard_ref, table_ref, counts_ref, map_buf, sems):
+def pack_kernel(
+    temp_ref, rock_ref, misfit_ref, map_ref, zone_ref, near_ref, tally_ref,
+    pack_ref, counts_ref, spread_ref, map_buf, shard_ref, table_ref, lists_ref, many_ref, sems,
+):
     east, north = rock_ref.shape[0], rock_ref.shape[1]
     copies = [
         pltpu.make_async_copy(source, target, sems.at[number])
         for number, (source, target) in enumerate(
             [
+                (near_ref, table_ref),
+                (zone_ref, shard_ref),
                 (map_ref, map_buf),
-                (zone_ref, shard_ref),
                 (rock_ref, pack_ref.at[pl.ds(0, east)]),
                 (misfit_ref, pack_ref.at[pl.ds(east, east)]),
                 (temp_ref, pack_ref.at[pl.ds(2 * east, east)]),
-                (near_ref, table_ref),
                 (tally_ref, counts_ref),
+                (many_ref, spread_ref),
             ]
         )
     ]
-    for copy in copies:
+    for copy in copies[:-1]:
         copy.start()
     copies[0].wait()
-    diagonal = iota((north, north), 0) == iota((north, north), 1)
-    lane = iota((north, LANES), 1)
-    ids = jnp.zeros((north, LANES), F32)
-    for x in range(east):
-        row = jnp.broadcast_to(map_buf[x].astype(F32), (north, north))
-        one = jnp.sum(jnp.where(diagonal, row, 0.0), axis=1, keepdims=True)
-        ids = jnp.where(lane == x, one, ids)
-    pack_ref[3 * east] = ids
-    for copy in copies[1:]:
-        copy.wait()
-
-
-def spread_kernel(shard_ref, near_ref, spread_ref, lists_ref):
-    shard = shard_ref[...]
-    tiles = near_ref.shape[1] // LANES
+    tiles = table_ref.shape[1] // LANES
     for tile in range(tiles):
-        lists_ref[8 * tile : 8 * tile + NBRS] = near_ref[:, tile * LANES : (tile + 1) * LANES].astype(F32)
-    for other in range(2 * tiles):
-        spread_ref[other * ROWS : other * ROWS + 16] = shard
+        lists_ref[8 * tile : 8 * tile + NBRS] = table_ref[:, tile * LANES : (tile + 1) * LANES].astype(F32)
     group = iota((tiles, LANES), 1) >> 4
     first = lax.axis_index("gx") * 16
     for odd in range(2):
@@ -102,7 +90,23 @@
                 lists_ref[pl.ds(number, tiles, stride=8), :], (2 * LANES + 16 * number - 64 * odd - first) & 127, 1
             )
             ids = jnp.where(group == number, moved, ids)
-        spread_ref[pl.ds(16 + odd * ROWS, tiles, stride=2 * ROWS), :] = ids
+        many_ref[pl.ds(16 + odd * ROWS, tiles, stride=2 * ROWS), :] = ids
+    copies[1].wait()
+    shard = shard_ref[...]
+    for other in range(2 * tiles):
+        many_ref[other * ROWS : other * ROWS + 16] = shard
+    copies[-1].start()
+    copies[2].wait()
+    diagonal = iota((north, north), 0) == iota((north, north), 1)
+    lane = iota((north, LANES), 1)
+    ids = jnp.zeros((north, LANES), F32)
+    for x in range(east):
+        row = jnp.broadcast_to(map_buf[x].astype(F32), (north, north))
+        one = jnp.sum(jnp.where(diagonal, row, 0.0), axis=1, keepdims=True)
+        ids = jnp.where(lane == x, one, ids)
+    pack_ref[3 * east] = ids
+    for copy in copies[3:]:
+        copy.wait()
 
 
 def extend_kernel(own_ref, first_ref, second_ref, ext_ref, slab_a_ref, slab_b_ref):
@@ -350,16 +354,23 @@
     shard_rows = zone_log.shape[0] // LANES
     zone = zone_log.reshape(shard_rows, LANES)
     shape = jax.ShapeDtypeStruct
-    pack, shard, near, counts = call(
+    pack, counts, spread = call(
         pack_kernel,
         [
             shape((3 * east + 1, north, depth), F32),
-            shape((shard_rows, LANES), F32),
-            shape((NBRS, zone_log.shape[0]), I32),
             shape((1, along), I32),
+            shape((along * ROWS, LANES), F32),
         ],
         [HBM] * 7,
-        [pltpu.VMEM((east, 1, north), I32), pltpu.SemaphoreType.DMA((7,))],
+        [
+            pltpu.VMEM((east, 1, north), I32),
+            pltpu.VMEM((shard_rows, LANES), F32),
+            pltpu.VMEM((NBRS, zone_log.shape[0]), I32),
+            pltpu.VMEM((8 * shard_rows, LANES), F32),
+            pltpu.VMEM((along * ROWS, LANES), F32),
+            pltpu.SemaphoreType.DMA((8,)),
+        ],
+        out_specs=[VMEM, VMEM, HBM],
     )(
         *map(
             in_hbm,
@@ -375,13 +386,7 @@
         )
     )
     y_first, y_second = swap(pack, "gy", 0), swap(pack, "gy", 1)
-    spread = call(
-        spread_kernel,
-        shape((along * ROWS, LANES), F32),
-        [VMEM, VMEM],
-        [pltpu.VMEM((8 * shard_rows, LANES), F32)],
-        cost=pl.CostEstimate(flops=1 << 35, bytes_accessed=1 << 20, transcendentals=0),
-    )(shard, near)
+    spread, y_first = lax.optimization_barrier((spread, y_first))
     shards = lax.all_to_all(spread.reshape(along, 1, ROWS * LANES), "gy", 0, 0, tiled=True).reshape(along * ROWS, LANES)
     ext, slab_a, slab_b = call(
         extend_kernel,

time: 45.1 us -> 44.6 us (0.989)
    pallas_call x2 -> x1, Pallas kernels: 1.8 us -> 1.73 us  [body(): call(pack_kernel, [shape((3 * east + 1, north, depth), F32), shape((1, al...]
  transfers between devices with their start and end apart: 5 -> 5, of which waited for: 1 -> 1; matrix products, arithmetic and copies ran while one was open for 0% -> 0% of each run, Pallas kernels for 6% -> 5%
where the time goes in v6:
time: 44.6 us; the launch traced here: 44.3 us
  blocking collectives  16 us (36%)
  starting transfers between devices  14.7 us (33%)
  waiting for transfers between devices  7.13 us (16%)
  Pallas kernels  6.42 us (14%)
    all_to_all x1, blocking collectives, body(): lax.all_to_all(rows.reshape(devices, 1, 2 * LANES), ('gy', 'gx'), 0, 0, t...  16 us
    all_to_all x1, starting transfers between devices, body(): lax.all_to_all(spread.reshape(along, 1, ROWS * LANES), 'gy', 0, 0, tiled=...  7.77 us
    all_to_all x1, waiting for transfers between devices, body(): lax.all_to_all(spread.reshape(along, 1, ROWS * LANES), 'gy', 0, 0, tiled=...  7.12 us
    ppermute x4, starting transfers between devices, swap(): return lax.ppermute(array, axis, pairs + [(b, a) for a, b in pairs])  6.95 us
    pallas_call x1, Pallas kernels, body(): call(smooth_kernel, [shape((along, LANES), F32), shape((8, LANES), I32),...  1.93 us
    pallas_call x1, Pallas kernels, body(): call(pack_kernel, [shape((3 * east + 1, north, depth), F32), shape((1, al...  1.73 us
    pallas_call x1, Pallas kernels, body(): call(place_kernel, shape((slot_rows, LANES), F32), [VMEM, VMEM], [pltpu.V...  1.51 us
    pallas_call x1, Pallas kernels, body(): call(sweep_kernel, shape((devices * 2, LANES), F32), [VMEM] * 6)  1.15 us
  transfers between devices with their start and end apart: 5, of which 1 were waited for; matrix products, arithmetic and copies ran while one was open for 0% of the time, Pallas kernels for 5%

profile of v6, /device:TPU:1, one launch (start us, length us, event | category | flops | bytes accessed | tf_op | source)
XLA Modules:
  0.0 44.3 jit_solution(8007301041429134340)
XLA Ops:
  0.0 1.7 %shard_map.73 = (f32[25,8,128]{2,1,0:T(8,128)S(1)}, s32[1,32]{1,0:T(1,128)S(1)}, f32[544,128]{1,0:T(8,128)}) custom-call(f32[8,8,128]{2,1,0:T(8,128)} %temp_ref.1, f32[8,8,128]{2,1,0:T(8,128)} %rock_ref.1, f32[8,8,128]{2,1,0:T(8,128)} %misfit_ref.1, s32[8,1,8]{2,1,0:T(1,128)} %bitcast.16, f32[16,128]{1,0:T(8,128)} %bitcast.15, s32[6,2048]{1,0:T(8,128)} %bitcast.14, ...), custom_call_target="tpu_custom_call" | custom-call | tf_op jit(solution)/shard_map/pallas_call | solution.py:357
  1.7 1.5 %collective-permute-start = (f32[25,8,128]{2,1,0:T(8,128)S(1)}, f32[25,8,128]{2,1,0:T(8,128)S(1)}, u32[]{:S(2)}, u32[]{:S(2)}) collective-permute-start(f32[25,8,128]{2,1,0:T(8,128)S(1)} %get-tuple-element.18.own_ref), channel_id=1, source_target_pairs={{0,1},{2,3},{4,5},{6,7},{8,9},{10,11},{12,13},{14,15},{16,17},{18,... | collective-permute-start | bytes 307208 | tf_op jit(solution)/shard_map/ppermute | solution.py:347
  3.2 3.5 %collective-permute-start.1 = (f32[25,8,128]{2,1,0:T(8,128)S(1)}, f32[25,8,128]{2,1,0:T(8,128)S(1)}, u32[]{:S(2)}, u32[]{:S(2)}) collective-permute-start(f32[25,8,128]{2,1,0:T(8,128)S(1)} %get-tuple-element.18.own_ref), channel_id=1, source_target_pairs={{1,2},{3,4},{5,6},{7,8},{9,10},{11,12},{13,14},{15,16},{17,18},{19... | collective-permute-start | bytes 307208 | tf_op jit(solution)/shard_map/ppermute | solution.py:347
  6.8 0.0 collective-permute-done.first_ref
  6.8 7.8 %all-to-all-start = ((f32[32,1,2176]{2,1,0:T(1,128)}), f32[32,1,2176]{2,1,0:T(1,128)S(1)}, u32[]{:S(2)}, u32[]{:S(2)}) async-start(f32[32,1,2176]{2,1,0:T(1,128)} %bitcast.5), calls=%async_computation | async-start | bytes 557056 | tf_op jit(solution)/shard_map/all_to_all | solution.py:390
  14.6 0.0 collective-permute-done.1.second_ref
  14.6 0.1 shard_map.74
  14.7 1.3 %collective-permute-start.2 = (f32[11,16,128]{2,1,0:T(8,128)S(1)}, f32[11,16,128]{2,1,0:T(8,128)S(1)}, u32[]{:S(2)}, u32[]{:S(2)}) collective-permute-start(f32[11,16,128]{2,1,0:T(8,128)S(1)} %get-tuple-element.24), channel_id=1, source_target_pairs={{0,32},{64,96},{32,0},{96,64},{1,33},{65,97},{33,1},{97,65},{2,34}... | collective-permute-start | bytes 270344 | tf_op jit(solution)/shard_map/ppermute | solution.py:347
  15.9 0.7 %collective-permute-start.3 = (f32[11,16,128]{2,1,0:T(8,128)S(1)}, f32[11,16,128]{2,1,0:T(8,128)S(1)}, u32[]{:S(2)}, u32[]{:S(2)}) collective-permute-start(f32[11,16,128]{2,1,0:T(8,128)S(1)} %get-tuple-element.25), channel_id=1, source_target_pairs={{32,64},{64,32},{33,65},{65,33},{34,66},{66,34},{35,67},{67,35},{3... | collective-permute-start | bytes 270344 | tf_op jit(solution)/shard_map/ppermute | solution.py:347
  16.6 7.1 %all-to-all-done = f32[32,1,2176]{2,1,0:T(1,128)S(1)} async-done(((f32[32,1,2176]{2,1,0:T(1,128)}), f32[32,1,2176]{2,1,0:T(1,128)S(1)}, u32[]{:S(2)}, u32[]{:S(2)}) %all-to-all-start) | async-done | bytes 278560 | tf_op jit(solution)/shard_map/all_to_all | solution.py:390
  23.7 1.9 %shard_map.75 = (f32[32,128]{1,0:T(8,128)S(1)}, s32[8,128]{1,0:T(8,128)S(1)}, bf16[384,512]{1,0:T(8,128)(2,1)S(1)}, f32[192,128]{1,0:T(8,128)S(1)}) custom-call(f32[544,128]{1,0:T(8,128)S(1)} %bitcast.13, f32[25,24,128]{2,1,0:T(8,128)S(1)} %get-tuple-element.21.ext_ref, s32[1,32]{1,0:T(1,128)S(1)} %get-tuple-element.22.tally_ref), custom_call_target="tpu_custom_call" | custom-call | flops 4294967296 | bytes 1048576 | tf_op jit(solution)/shard_map/pallas_call | solution.py:398
  25.7 0.0 collective-permute-done.2.first_ref
  25.7 0.0 collective-permute-done.3.second_ref
  25.7 1.1 %shard_map.76 = f32[256,128]{1,0:T(8,128)S(1)} custom-call(f32[25,24,128]{2,1,0:T(8,128)S(1)} %get-tuple-element.21.ext_ref, f32[11,16,128]{2,1,0:T(8,128)S(1)} %collective-permute-done.2.first_ref, f32[11,16,128]{2,1,0:T(8,128)S(1)} %collective-permute-done.3.second_ref, bf16[384,512]{1,0:T(8,128)(2,1)S(1)} %get-tuple-element.26.pieces_ref, ...), custom_call_target="tpu_custom_call" | custom-call | tf_op jit(solution)/shard_map/pallas_call | solution.py:410
  26.8 16.0 %all_to_all.10 = f32[128,1,256]{2,1,0:T(1,128)S(1)} all-to-all(f32[128,1,256]{2,1,0:T(1,128)S(1)} %bitcast.11), channel_id=1, replica_groups=mesh['gx'=4,'gy'=32] {'gy','gx'}, dimensions={0} | all-to-all | bytes 262144 | tf_op jit(solution)/shard_map/all_to_all | solution.py:411
  42.8 1.5 %shard_map.77 = f32[32,128]{1,0:T(8,128)} custom-call(s32[8,128]{1,0:T(8,128)S(1)} %get-tuple-element.23.meta_ref, f32[256,128]{1,0:T(8,128)S(1)} %bitcast.12), custom_call_target="tpu_custom_call" | custom-call | tf_op jit(solution)/shard_map/pallas_call | solution.py:413
Async XLA Ops:
  1.7 5.0 %collective-permute-start = (f32[25,8,128]{2,1,0:T(8,128)S(1)}, f32[25,8,128]{2,1,0:T(8,128)S(1)}, u32[]{:S(2)}, u32[]{:S(2)}) collective-permute-start(f32[25,8,128]{2,1,0:T(8,128)S(1)} %get-tuple-element.18.own_ref), channel_id=1, source_target_pairs={{0,1},{2,3},{4,5},{6,7},{8,9},{10,11},{12,13},{14,15},{16,17},{18,... | collective-permute-start | bytes 307208 | tf_op jit(solution)/shard_map/ppermute | solution.py:347
  3.2 11.3 %collective-permute-start.1 = (f32[25,8,128]{2,1,0:T(8,128)S(1)}, f32[25,8,128]{2,1,0:T(8,128)S(1)}, u32[]{:S(2)}, u32[]{:S(2)}) collective-permute-start(f32[25,8,128]{2,1,0:T(8,128)S(1)} %get-tuple-element.18.own_ref), channel_id=1, source_target_pairs={{1,2},{3,4},{5,6},{7,8},{9,10},{11,12},{13,14},{15,16},{17,18},{19... | collective-permute-start | bytes 307208 | tf_op jit(solution)/shard_map/ppermute | solution.py:347
  6.8 16.9 %all-to-all-start = ((f32[32,1,2176]{2,1,0:T(1,128)}), f32[32,1,2176]{2,1,0:T(1,128)S(1)}, u32[]{:S(2)}, u32[]{:S(2)}) async-start(f32[32,1,2176]{2,1,0:T(1,128)} %bitcast.5), calls=%async_computation | async-start | bytes 557056 | tf_op jit(solution)/shard_map/all_to_all | solution.py:390
  14.7 11.0 %collective-permute-start.2 = (f32[11,16,128]{2,1,0:T(8,128)S(1)}, f32[11,16,128]{2,1,0:T(8,128)S(1)}, u32[]{:S(2)}, u32[]{:S(2)}) collective-permute-start(f32[11,16,128]{2,1,0:T(8,128)S(1)} %get-tuple-element.24), channel_id=1, source_target_pairs={{0,32},{64,96},{32,0},{96,64},{1,33},{65,97},{33,1},{97,65},{2,34}... | collective-permute-start | bytes 270344 | tf_op jit(solution)/shard_map/ppermute | solution.py:347
  15.9 9.7 %collective-permute-start.3 = (f32[11,16,128]{2,1,0:T(8,128)S(1)}, f32[11,16,128]{2,1,0:T(8,128)S(1)}, u32[]{:S(2)}, u32[]{:S(2)}) collective-permute-start(f32[11,16,128]{2,1,0:T(8,128)S(1)} %get-tuple-element.25), channel_id=1, source_target_pairs={{32,64},{64,32},{33,65},{65,33},{34,66},{66,34},{35,67},{67,35},{3... | collective-permute-start | bytes 270344 | tf_op jit(solution)/shard_map/ppermute | solution.py:347

commit v7 on v6

--- a/solution.py
+++ b/solution.py
@@ -11,6 +11,7 @@
 SMOOTHING = 0.5
 SENS_SCALE = 0.03125
 LANES = 128
+X, Y, ALL = "x", ("y", "z", "core"), ("core", "z", "y", "x")
 ROWS = 17
 F32 = jnp.float32
 BF16 = jnp.bfloat16
@@ -53,6 +54,11 @@
 def column(tile, lane):
     picked = jnp.where(iota(tile.shape, 1) == lane, tile, 0.0)
     return jnp.broadcast_to(jnp.sum(picked, axis=1, keepdims=True), tile.shape)
+
+
+def owner_of(number):
+    core, z, y = number // 16, number // 4 % 4, number % 4
+    return (y * 4 + z) * 2 + core
 
 
 def pack_kernel(
@@ -82,7 +88,7 @@
     for tile in range(tiles):
         lists_ref[8 * tile : 8 * tile + NBRS] = table_ref[:, tile * LANES : (tile + 1) * LANES].astype(F32)
     group = iota((tiles, LANES), 1) >> 4
-    first = lax.axis_index("gx") * 16
+    first = lax.axis_index(X) * 16
     for odd in range(2):
         ids = jnp.zeros((tiles, LANES), F32)
         for number in range(NBRS):
@@ -90,7 +96,9 @@
                 lists_ref[pl.ds(number, tiles, stride=8), :], (2 * LANES + 16 * number - 64 * odd - first) & 127, 1
             )
             ids = jnp.where(group == number, moved, ids)
-        many_ref[pl.ds(16 + odd * ROWS, tiles, stride=2 * ROWS), :] = ids
+        for tile in range(tiles):
+            place = ROWS * owner_of(2 * tile + odd) + 16
+            many_ref[place : place + 1] = ids[tile : tile + 1]
     copies[1].wait()
     shard = shard_ref[...]
     for other in range(2 * tiles):
@@ -110,7 +118,7 @@
 
 
 def extend_kernel(own_ref, first_ref, second_ref, ext_ref, slab_a_ref, slab_b_ref):
-    gx, gy = lax.axis_index("gx"), lax.axis_index("gy")
+    gx, gy = lax.axis_index(X), lax.axis_index(Y)
     even = gy % 2 == 0
 
     def window(begin, count):
@@ -150,7 +158,7 @@
 
 
 def smooth_kernel(all_ref, ext_ref, tally_ref, out_ref, meta_ref, pieces_ref, gain_ref, term_ref):
-    gx, gy = lax.axis_index("gx"), lax.axis_index("gy")
+    gy, number = lax.axis_index(Y), lax.axis_index(ALL)
     shards = all_ref.shape[0] // ROWS
     table = jnp.concatenate([all_ref[ROWS * shard : ROWS * shard + 16] for shard in range(shards)], axis=0)
     high_size = table.shape[0]
@@ -172,8 +180,8 @@
         )
         found = jnp.dot(pieces, hot, preferred_element_type=F32)
         found = found[0:LANES] + found[LANES : 2 * LANES] + found[2 * LANES :]
-        for number, row in enumerate(rows):
-            picked = jnp.where(low_row == low[row : row + 1], found[:, number * LANES : (number + 1) * LANES], 0.0)
+        for block, row in enumerate(rows):
+            picked = jnp.where(low_row == low[row : row + 1], found[:, block * LANES : (block + 1) * LANES], 0.0)
             near.append(jnp.sum(picked, axis=0, keepdims=True))
     near = jnp.concatenate(near, axis=0)
     lane = iota((8, LANES), 1)
@@ -183,13 +191,13 @@
         rest = jnp.where((lane >> 5) == part, moved, rest)
     near = jnp.concatenate([near, rest], axis=0)
     total = near
-    for number in range(1, NBRS):
-        total = total + pltpu.roll(near, LANES - 16 * number, 1)
-    own = all_ref[pl.ds(gy >> 1, shards, stride=ROWS), :]
-    own = pltpu.roll(own, (2 * LANES - (gy & 1) * 64 - gx * 16) & 127, 1)
+    for entry in range(1, NBRS):
+        total = total + pltpu.roll(near, LANES - 16 * entry, 1)
+    mine = number & 7
+    own = all_ref[pl.ds(number >> 3, shards, stride=ROWS), :]
+    own = pltpu.roll(own, (LANES - mine * 16) & 127, 1)
     term_ref[...] = SMOOTHING * (NBRS * own - total)
 
-    mine = (gy * 4 + gx) & 7
     lane = iota((16, LANES), 1)
     first = pltpu.roll(term_ref[pl.ds(0, 16, stride=2), :], mine * 16, 1)
     second = pltpu.roll(term_ref[pl.ds(1, 16, stride=2), :], (mine * 16 + 64) & 127, 1)
@@ -201,11 +209,11 @@
     start = jnp.sum(jnp.where(before, tally, 0.0), axis=1, keepdims=True)
     start = jnp.broadcast_to(start, (owners, LANES)).astype(I32)
     lane = iota((owners, LANES), 1)
-    slot = jnp.where((lane >> 4) == mine, 0, 2048) + (gy * 4 + gx) * 16 + (lane & 15)
+    slot = jnp.where((lane >> 4) == mine, 0, 2048) + number * 16 + (lane & 15)
     wanted = (start >> 12) + jnp.where(slot < (start & 4095), 1, 0)
     chosen = jnp.zeros((owners, LANES), F32)
-    for number in range(16):
-        chosen = chosen + jnp.where(wanted == number, terms[number : number + 1], 0.0)
+    for window in range(16):
+        chosen = chosen + jnp.where(wanted == window, terms[window : window + 1], 0.0)
     out_ref[...] = chosen
 
     row = tally[0:1]
@@ -221,7 +229,7 @@
     shape = (16, LANES)
     lane = iota(shape, 1)
     first, last = lane == 0, lane == LANES - 1
-    even = lax.axis_index("gx") % 2 == 0
+    even = lax.axis_index(X) % 2 == 0
     one, two = first_ref[...], second_ref[...]
     west, east = jnp.where(even, two, one), jnp.where(even, one, two)
     own_columns = [column(ext_ref[8], x) for x in range(8)]
@@ -290,8 +298,9 @@
     sums = jnp.sum(turned, axis=0, keepdims=True)
     row = jnp.where(iota((1, LANES), 1) < 64, sums, turned[0:1])
     odd = (iota((8, LANES), 0) & 1) == 1
-    for owner in range(smooth_ref.shape[0]):
-        out_ref[8 * owner : 8 * owner + 8] = jnp.where(odd, smooth_ref[owner : owner + 1], row)
+    for four in range(smooth_ref.shape[0]):
+        owner = owner_of(four)
+        out_ref[8 * four : 8 * four + 8] = jnp.where(odd, smooth_ref[owner : owner + 1], row)
 
 
 def place_kernel(meta_ref, all_ref, out_ref, smooth_ref):
@@ -349,7 +358,7 @@
 
 def body(temp, rock, misfit, zone_map, zone_log, tally, adjacency):
     east, north, depth = temp.shape
-    across, along = lax.axis_size("gx"), lax.axis_size("gy")
+    across, along = lax.axis_size(X), lax.axis_size(Y)
     devices = across * along
     shard_rows = zone_log.shape[0] // LANES
     zone = zone_log.reshape(shard_rows, LANES)
@@ -385,16 +394,16 @@
             ),
         )
     )
-    y_first, y_second = swap(pack, "gy", 0), swap(pack, "gy", 1)
+    y_first, y_second = swap(pack, Y, 0), swap(pack, Y, 1)
     spread, y_first = lax.optimization_barrier((spread, y_first))
-    shards = lax.all_to_all(spread.reshape(along, 1, ROWS * LANES), "gy", 0, 0, tiled=True).reshape(along * ROWS, LANES)
+    shards = lax.all_to_all(spread.reshape(along, 1, ROWS * LANES), Y, 0, 0, tiled=True).reshape(along * ROWS, LANES)
     ext, slab_a, slab_b = call(
         extend_kernel,
         [shape((25, 24, LANES), F32), shape((11, 16, LANES), F32), shape((11, 16, LANES), F32)],
         [VMEM] * 3,
         cost=pl.CostEstimate(flops=1 << 37, bytes_accessed=1 << 20, transcendentals=0),
     )(pack, y_first, y_second)
-    x_first, x_second = swap(slab_a, "gx", 0), swap(slab_b, "gx", 1)
+    x_first, x_second = swap(slab_a, X, 0), swap(slab_b, X, 1)
     smooth, meta, pieces, gain = call(
         smooth_kernel,
         [
@@ -408,7 +417,7 @@
         cost=pl.CostEstimate(flops=1 << 32, bytes_accessed=1 << 20, transcendentals=0),
     )(shards, ext, counts)
     rows = call(sweep_kernel, shape((devices * 2, LANES), F32), [VMEM] * 6)(ext, x_first, x_second, pieces, gain, smooth)
-    gathered = lax.all_to_all(rows.reshape(devices, 1, 2 * LANES), ("gy", "gx"), 0, 0, tiled=True)
+    gathered = lax.all_to_all(rows.reshape(devices, 1, 2 * LANES), ALL, 0, 0, tiled=True)
     slot_rows = 2 * shard_rows
     out = call(
         place_kernel,
@@ -420,13 +429,6 @@
 
 
 def solution(mesh):
-    placed = (
-        P("gx", "gy", None),
-        P("gx", "gy", None),
-        P("gx", "gy", None),
-        P("gx", "gy", None),
-        P("gy"),
-        P(),
-        P("gy", None),
-    )
-    return jax.shard_map(body, mesh=mesh, in_specs=placed, out_specs=P("gy"), check_vma=False)
+    physical = jax.sharding.Mesh(mesh.devices.reshape(4, 4, 4, 2), ("x", "y", "z", "core"))
+    placed = (P(X, Y, None),) * 4 + (P(Y), P(), P(Y, None))
+    return jax.shard_map(body, mesh=physical, in_specs=placed, out_specs=P(Y), check_vma=False)

time: 44.6 us -> 44.4 us (level)
  no operation moved by 1% of the time
where the time goes in v7:
time: 44.4 us; the launch traced here: 44.1 us
  blocking collectives  15.8 us (36%)
  starting transfers between devices  14.7 us (33%)
  waiting for transfers between devices  7.13 us (16%)
  Pallas kernels  6.42 us (14%)
    all_to_all x1, blocking collectives, body(): lax.all_to_all(rows.reshape(devices, 1, 2 * LANES), ALL, 0, 0, tiled=True)  15.8 us
    all_to_all x1, starting transfers between devices, body(): lax.all_to_all(spread.reshape(along, 1, ROWS * LANES), Y, 0, 0, tiled=True)  7.77 us
    all_to_all x1, waiting for transfers between devices, body(): lax.all_to_all(spread.reshape(along, 1, ROWS * LANES), Y, 0, 0, tiled=True)  7.12 us
    ppermute x4, starting transfers between devices, swap(): return lax.ppermute(array, axis, pairs + [(b, a) for a, b in pairs])  6.95 us
    pallas_call x1, Pallas kernels, body(): call(smooth_kernel, [shape((along, LANES), F32), shape((8, LANES), I32),...  1.94 us
    pallas_call x1, Pallas kernels, body(): call(pack_kernel, [shape((3 * east + 1, north, depth), F32), shape((1, al...  1.73 us
    pallas_call x1, Pallas kernels, body(): call(place_kernel, shape((slot_rows, LANES), F32), [VMEM, VMEM], [pltpu.V...  1.51 us
    pallas_call x1, Pallas kernels, body(): call(sweep_kernel, shape((devices * 2, LANES), F32), [VMEM] * 6)  1.15 us
  transfers between devices with their start and end apart: 5, of which 1 were waited for; matrix products, arithmetic and copies ran while one was open for 0% of the time, Pallas kernels for 5%

profile of v7, /device:TPU:1, one launch (start us, length us, event | category | flops | bytes accessed | tf_op | source)
XLA Modules:
  0.0 44.1 jit_solution(12279573545465965957)
XLA Ops:
  0.0 1.7 %shard_map.73 = (f32[25,8,128]{2,1,0:T(8,128)S(1)}, s32[1,32]{1,0:T(1,128)S(1)}, f32[544,128]{1,0:T(8,128)}) custom-call(f32[8,8,128]{2,1,0:T(8,128)} %temp_ref.1, f32[8,8,128]{2,1,0:T(8,128)} %rock_ref.1, f32[8,8,128]{2,1,0:T(8,128)} %misfit_ref.1, s32[8,1,8]{2,1,0:T(1,128)} %bitcast.16, f32[16,128]{1,0:T(8,128)} %bitcast.15, s32[6,2048]{1,0:T(8,128)} %bitcast.14, ...), custom_call_target="tpu_custom_call" | custom-call | tf_op jit(solution)/shard_map/pallas_call | solution.py:366
  1.7 1.5 %collective-permute-start = (f32[25,8,128]{2,1,0:T(8,128)S(1)}, f32[25,8,128]{2,1,0:T(8,128)S(1)}, u32[]{:S(2)}, u32[]{:S(2)}) collective-permute-start(f32[25,8,128]{2,1,0:T(8,128)S(1)} %get-tuple-element.18.own_ref), channel_id=1, source_target_pairs={{0,1},{2,3},{4,5},{6,7},{8,9},{10,11},{12,13},{14,15},{16,17},{18,... | collective-permute-start | bytes 307208 | tf_op jit(solution)/shard_map/ppermute | solution.py:356
  3.2 3.5 %collective-permute-start.1 = (f32[25,8,128]{2,1,0:T(8,128)S(1)}, f32[25,8,128]{2,1,0:T(8,128)S(1)}, u32[]{:S(2)}, u32[]{:S(2)}) collective-permute-start(f32[25,8,128]{2,1,0:T(8,128)S(1)} %get-tuple-element.18.own_ref), channel_id=1, source_target_pairs={{1,2},{3,4},{5,6},{7,8},{9,10},{11,12},{13,14},{15,16},{17,18},{19... | collective-permute-start | bytes 307208 | tf_op jit(solution)/shard_map/ppermute | solution.py:356
  6.8 0.0 collective-permute-done.first_ref
  6.8 7.8 %all-to-all-start = ((f32[32,1,2176]{2,1,0:T(1,128)}), f32[32,1,2176]{2,1,0:T(1,128)S(1)}, u32[]{:S(2)}, u32[]{:S(2)}) async-start(f32[32,1,2176]{2,1,0:T(1,128)} %bitcast.5), calls=%async_computation | async-start | bytes 557056 | tf_op jit(solution)/shard_map/all_to_all | solution.py:399
  14.6 0.0 collective-permute-done.1.second_ref
  14.6 0.1 shard_map.74
  14.7 1.3 %collective-permute-start.2 = (f32[11,16,128]{2,1,0:T(8,128)S(1)}, f32[11,16,128]{2,1,0:T(8,128)S(1)}, u32[]{:S(2)}, u32[]{:S(2)}) collective-permute-start(f32[11,16,128]{2,1,0:T(8,128)S(1)} %get-tuple-element.24), channel_id=1, source_target_pairs={{0,32},{64,96},{32,0},{96,64},{1,33},{65,97},{33,1},{97,65},{2,34}... | collective-permute-start | bytes 270344 | tf_op jit(solution)/shard_map/ppermute | solution.py:356
  15.9 0.7 %collective-permute-start.3 = (f32[11,16,128]{2,1,0:T(8,128)S(1)}, f32[11,16,128]{2,1,0:T(8,128)S(1)}, u32[]{:S(2)}, u32[]{:S(2)}) collective-permute-start(f32[11,16,128]{2,1,0:T(8,128)S(1)} %get-tuple-element.25), channel_id=1, source_target_pairs={{32,64},{64,32},{33,65},{65,33},{34,66},{66,34},{35,67},{67,35},{3... | collective-permute-start | bytes 270344 | tf_op jit(solution)/shard_map/ppermute | solution.py:356
  16.6 7.1 %all-to-all-done = f32[32,1,2176]{2,1,0:T(1,128)S(1)} async-done(((f32[32,1,2176]{2,1,0:T(1,128)}), f32[32,1,2176]{2,1,0:T(1,128)S(1)}, u32[]{:S(2)}, u32[]{:S(2)}) %all-to-all-start) | async-done | bytes 278560 | tf_op jit(solution)/shard_map/all_to_all | solution.py:399
  23.7 1.9 %shard_map.75 = (f32[32,128]{1,0:T(8,128)S(1)}, s32[8,128]{1,0:T(8,128)S(1)}, bf16[384,512]{1,0:T(8,128)(2,1)S(1)}, f32[192,128]{1,0:T(8,128)S(1)}) custom-call(f32[544,128]{1,0:T(8,128)S(1)} %bitcast.13, f32[25,24,128]{2,1,0:T(8,128)S(1)} %get-tuple-element.21.ext_ref, s32[1,32]{1,0:T(1,128)S(1)} %get-tuple-element.22.tally_ref), custom_call_target="tpu_custom_call" | custom-call | flops 4294967296 | bytes 1048576 | tf_op jit(solution)/shard_map/pallas_call | solution.py:407
  25.7 0.0 collective-permute-done.2.first_ref
  25.7 0.0 collective-permute-done.3.second_ref
  25.7 1.1 %shard_map.76 = f32[256,128]{1,0:T(8,128)S(1)} custom-call(f32[25,24,128]{2,1,0:T(8,128)S(1)} %get-tuple-element.21.ext_ref, f32[11,16,128]{2,1,0:T(8,128)S(1)} %collective-permute-done.2.first_ref, f32[11,16,128]{2,1,0:T(8,128)S(1)} %collective-permute-done.3.second_ref, bf16[384,512]{1,0:T(8,128)(2,1)S(1)} %get-tuple-element.26.pieces_ref, ...), custom_call_target="tpu_custom_call" | custom-call | tf_op jit(solution)/shard_map/pallas_call | solution.py:419
  26.8 15.8 %all_to_all.10 = f32[128,1,256]{2,1,0:T(1,128)S(1)} all-to-all(f32[128,1,256]{2,1,0:T(1,128)S(1)} %bitcast.11), channel_id=1, replica_groups=mesh['x'=4,'y'=4,'z'=4,'core'=2] {'core','z','y','x'}, dimensions={0} | all-to-all | bytes 262144 | tf_op jit(solution)/shard_map/all_to_all | solution.py:420
  42.6 1.5 %shard_map.77 = f32[32,128]{1,0:T(8,128)} custom-call(s32[8,128]{1,0:T(8,128)S(1)} %get-tuple-element.23.meta_ref, f32[256,128]{1,0:T(8,128)S(1)} %bitcast.12), custom_call_target="tpu_custom_call" | custom-call | tf_op jit(solution)/shard_map/pallas_call | solution.py:422
Async XLA Ops:
  1.7 5.0 %collective-permute-start = (f32[25,8,128]{2,1,0:T(8,128)S(1)}, f32[25,8,128]{2,1,0:T(8,128)S(1)}, u32[]{:S(2)}, u32[]{:S(2)}) collective-permute-start(f32[25,8,128]{2,1,0:T(8,128)S(1)} %get-tuple-element.18.own_ref), channel_id=1, source_target_pairs={{0,1},{2,3},{4,5},{6,7},{8,9},{10,11},{12,13},{14,15},{16,17},{18,... | collective-permute-start | bytes 307208 | tf_op jit(solution)/shard_map/ppermute | solution.py:356
  3.2 11.3 %collective-permute-start.1 = (f32[25,8,128]{2,1,0:T(8,128)S(1)}, f32[25,8,128]{2,1,0:T(8,128)S(1)}, u32[]{:S(2)}, u32[]{:S(2)}) collective-permute-start(f32[25,8,128]{2,1,0:T(8,128)S(1)} %get-tuple-element.18.own_ref), channel_id=1, source_target_pairs={{1,2},{3,4},{5,6},{7,8},{9,10},{11,12},{13,14},{15,16},{17,18},{19... | collective-permute-start | bytes 307208 | tf_op jit(solution)/shard_map/ppermute | solution.py:356
  6.8 16.9 %all-to-all-start = ((f32[32,1,2176]{2,1,0:T(1,128)}), f32[32,1,2176]{2,1,0:T(1,128)S(1)}, u32[]{:S(2)}, u32[]{:S(2)}) async-start(f32[32,1,2176]{2,1,0:T(1,128)} %bitcast.5), calls=%async_computation | async-start | bytes 557056 | tf_op jit(solution)/shard_map/all_to_all | solution.py:399
  14.7 11.0 %collective-permute-start.2 = (f32[11,16,128]{2,1,0:T(8,128)S(1)}, f32[11,16,128]{2,1,0:T(8,128)S(1)}, u32[]{:S(2)}, u32[]{:S(2)}) collective-permute-start(f32[11,16,128]{2,1,0:T(8,128)S(1)} %get-tuple-element.24), channel_id=1, source_target_pairs={{0,32},{64,96},{32,0},{96,64},{1,33},{65,97},{33,1},{97,65},{2,34}... | collective-permute-start | bytes 270344 | tf_op jit(solution)/shard_map/ppermute | solution.py:356
  15.9 9.7 %collective-permute-start.3 = (f32[11,16,128]{2,1,0:T(8,128)S(1)}, f32[11,16,128]{2,1,0:T(8,128)S(1)}, u32[]{:S(2)}, u32[]{:S(2)}) collective-permute-start(f32[11,16,128]{2,1,0:T(8,128)S(1)} %get-tuple-element.25), channel_id=1, source_target_pairs={{32,64},{64,32},{33,65},{65,33},{34,66},{66,34},{35,67},{67,35},{3... | collective-permute-start | bytes 270344 | tf_op jit(solution)/shard_map/ppermute | solution.py:356

commit v8 on v7

--- a/solution.py
+++ b/solution.py
@@ -162,7 +162,8 @@
     shards = all_ref.shape[0] // ROWS
     table = jnp.concatenate([all_ref[ROWS * shard : ROWS * shard + 16] for shard in range(shards)], axis=0)
     high_size = table.shape[0]
-    pieces = jnp.concatenate(thirds(jnp.transpose(table)), axis=0)
+    parts = thirds(jnp.transpose(table))
+    pieces = jnp.concatenate(parts, axis=0)
     pieces_ref[...] = pieces
 
     lane = iota((24, LANES), 1)
@@ -178,8 +179,7 @@
         hot = jnp.concatenate(
             [jnp.where(high_row == high[row : row + 1], 1.0, 0.0).astype(BF16) for row in rows], axis=1
         )
-        found = jnp.dot(pieces, hot, preferred_element_type=F32)
-        found = found[0:LANES] + found[LANES : 2 * LANES] + found[2 * LANES :]
+        found = sum(jnp.dot(piece, hot, preferred_element_type=F32) for piece in parts)
         for block, row in enumerate(rows):
             picked = jnp.where(low_row == low[row : row + 1], found[:, block * LANES : (block + 1) * LANES], 0.0)
             near.append(jnp.sum(picked, axis=0, keepdims=True))

time: 44.4 us -> 44.4 us (level)
  transfers between devices with their start and end apart: 5 -> 5, of which waited for: 1 -> 1; matrix products, arithmetic and copies ran while one was open for 0% -> 0% of each run, Pallas kernels for 5% -> 4%
where the time goes in v8:
time: 44.4 us; the launch traced here: 44.1 us
  blocking collectives  15.8 us (36%)
  starting transfers between devices  14.7 us (33%)
  waiting for transfers between devices  7.13 us (16%)
  Pallas kernels  6.34 us (14%)
    all_to_all x1, blocking collectives, body(): lax.all_to_all(rows.reshape(devices, 1, 2 * LANES), ALL, 0, 0, tiled=True)  15.8 us
    all_to_all x1, starting transfers between devices, body(): lax.all_to_all(spread.reshape(along, 1, ROWS * LANES), Y, 0, 0, tiled=True)  7.77 us
    all_to_all x1, waiting for transfers between devices, body(): lax.all_to_all(spread.reshape(along, 1, ROWS * LANES), Y, 0, 0, tiled=True)  7.12 us
    ppermute x4, starting transfers between devices, swap(): return lax.ppermute(array, axis, pairs + [(b, a) for a, b in pairs])  6.95 us
    pallas_call x1, Pallas kernels, body(): call(smooth_kernel, [shape((along, LANES), F32), shape((8, LANES), I32),...  1.85 us
    pallas_call x1, Pallas kernels, body(): call(pack_kernel, [shape((3 * east + 1, north, depth), F32), shape((1, al...  1.73 us
    pallas_call x1, Pallas kernels, body(): call(place_kernel, shape((slot_rows, LANES), F32), [VMEM, VMEM], [pltpu.V...  1.51 us
    pallas_call x1, Pallas kernels, body(): call(sweep_kernel, shape((devices * 2, LANES), F32), [VMEM] * 6)  1.15 us
  transfers between devices with their start and end apart: 5, of which 1 were waited for; matrix products, arithmetic and copies ran while one was open for 0% of the time, Pallas kernels for 4%

profile of v8, /device:TPU:1, one launch (start us, length us, event | category | flops | bytes accessed | tf_op | source)
XLA Modules:
  0.0 44.1 jit_solution(7729610201913100640)
XLA Ops:
  0.0 1.7 %shard_map.73 = (f32[25,8,128]{2,1,0:T(8,128)S(1)}, s32[1,32]{1,0:T(1,128)S(1)}, f32[544,128]{1,0:T(8,128)}) custom-call(f32[8,8,128]{2,1,0:T(8,128)} %temp_ref.1, f32[8,8,128]{2,1,0:T(8,128)} %rock_ref.1, f32[8,8,128]{2,1,0:T(8,128)} %misfit_ref.1, s32[8,1,8]{2,1,0:T(1,128)} %bitcast.16, f32[16,128]{1,0:T(8,128)} %bitcast.15, s32[6,2048]{1,0:T(8,128)} %bitcast.14, ...), custom_call_target="tpu_custom_call" | custom-call | tf_op jit(solution)/shard_map/pallas_call | solution.py:366
  1.7 1.5 %collective-permute-start = (f32[25,8,128]{2,1,0:T(8,128)S(1)}, f32[25,8,128]{2,1,0:T(8,128)S(1)}, u32[]{:S(2)}, u32[]{:S(2)}) collective-permute-start(f32[25,8,128]{2,1,0:T(8,128)S(1)} %get-tuple-element.18.own_ref), channel_id=1, source_target_pairs={{0,1},{2,3},{4,5},{6,7},{8,9},{10,11},{12,13},{14,15},{16,17},{18,... | collective-permute-start | bytes 307208 | tf_op jit(solution)/shard_map/ppermute | solution.py:356
  3.2 3.5 %collective-permute-start.1 = (f32[25,8,128]{2,1,0:T(8,128)S(1)}, f32[25,8,128]{2,1,0:T(8,128)S(1)}, u32[]{:S(2)}, u32[]{:S(2)}) collective-permute-start(f32[25,8,128]{2,1,0:T(8,128)S(1)} %get-tuple-element.18.own_ref), channel_id=1, source_target_pairs={{1,2},{3,4},{5,6},{7,8},{9,10},{11,12},{13,14},{15,16},{17,18},{19... | collective-permute-start | bytes 307208 | tf_op jit(solution)/shard_map/ppermute | solution.py:356
  6.8 0.0 collective-permute-done.first_ref
  6.8 7.8 %all-to-all-start = ((f32[32,1,2176]{2,1,0:T(1,128)}), f32[32,1,2176]{2,1,0:T(1,128)S(1)}, u32[]{:S(2)}, u32[]{:S(2)}) async-start(f32[32,1,2176]{2,1,0:T(1,128)} %bitcast.5), calls=%async_computation | async-start | bytes 557056 | tf_op jit(solution)/shard_map/all_to_all | solution.py:399
  14.6 0.0 collective-permute-done.1.second_ref
  14.6 0.1 shard_map.74
  14.7 1.3 %collective-permute-start.2 = (f32[11,16,128]{2,1,0:T(8,128)S(1)}, f32[11,16,128]{2,1,0:T(8,128)S(1)}, u32[]{:S(2)}, u32[]{:S(2)}) collective-permute-start(f32[11,16,128]{2,1,0:T(8,128)S(1)} %get-tuple-element.24), channel_id=1, source_target_pairs={{0,32},{64,96},{32,0},{96,64},{1,33},{65,97},{33,1},{97,65},{2,34}... | collective-permute-start | bytes 270344 | tf_op jit(solution)/shard_map/ppermute | solution.py:356
  15.9 0.7 %collective-permute-start.3 = (f32[11,16,128]{2,1,0:T(8,128)S(1)}, f32[11,16,128]{2,1,0:T(8,128)S(1)}, u32[]{:S(2)}, u32[]{:S(2)}) collective-permute-start(f32[11,16,128]{2,1,0:T(8,128)S(1)} %get-tuple-element.25), channel_id=1, source_target_pairs={{32,64},{64,32},{33,65},{65,33},{34,66},{66,34},{35,67},{67,35},{3... | collective-permute-start | bytes 270344 | tf_op jit(solution)/shard_map/ppermute | solution.py:356
  16.6 7.1 %all-to-all-done = f32[32,1,2176]{2,1,0:T(1,128)S(1)} async-done(((f32[32,1,2176]{2,1,0:T(1,128)}), f32[32,1,2176]{2,1,0:T(1,128)S(1)}, u32[]{:S(2)}, u32[]{:S(2)}) %all-to-all-start) | async-done | bytes 278560 | tf_op jit(solution)/shard_map/all_to_all | solution.py:399
  23.7 1.9 %shard_map.75 = (f32[32,128]{1,0:T(8,128)S(1)}, s32[8,128]{1,0:T(8,128)S(1)}, bf16[384,512]{1,0:T(8,128)(2,1)S(1)}, f32[192,128]{1,0:T(8,128)S(1)}) custom-call(f32[544,128]{1,0:T(8,128)S(1)} %bitcast.13, f32[25,24,128]{2,1,0:T(8,128)S(1)} %get-tuple-element.21.ext_ref, s32[1,32]{1,0:T(1,128)S(1)} %get-tuple-element.22.tally_ref), custom_call_target="tpu_custom_call" | custom-call | flops 4294967296 | bytes 1048576 | tf_op jit(solution)/shard_map/pallas_call | solution.py:407
  25.6 0.0 collective-permute-done.2.first_ref
  25.6 0.0 collective-permute-done.3.second_ref
  25.6 1.1 %shard_map.76 = f32[256,128]{1,0:T(8,128)S(1)} custom-call(f32[25,24,128]{2,1,0:T(8,128)S(1)} %get-tuple-element.21.ext_ref, f32[11,16,128]{2,1,0:T(8,128)S(1)} %collective-permute-done.2.first_ref, f32[11,16,128]{2,1,0:T(8,128)S(1)} %collective-permute-done.3.second_ref, bf16[384,512]{1,0:T(8,128)(2,1)S(1)} %get-tuple-element.26.pieces_ref, ...), custom_call_target="tpu_custom_call" | custom-call | tf_op jit(solution)/shard_map/pallas_call | solution.py:419
  26.7 15.8 %all_to_all.10 = f32[128,1,256]{2,1,0:T(1,128)S(1)} all-to-all(f32[128,1,256]{2,1,0:T(1,128)S(1)} %bitcast.11), channel_id=1, replica_groups=mesh['x'=4,'y'=4,'z'=4,'core'=2] {'core','z','y','x'}, dimensions={0} | all-to-all | bytes 262144 | tf_op jit(solution)/shard_map/all_to_all | solution.py:420
  42.6 1.5 %shard_map.77 = f32[32,128]{1,0:T(8,128)} custom-call(s32[8,128]{1,0:T(8,128)S(1)} %get-tuple-element.23.meta_ref, f32[256,128]{1,0:T(8,128)S(1)} %bitcast.12), custom_call_target="tpu_custom_call" | custom-call | tf_op jit(solution)/shard_map/pallas_call | solution.py:422
Async XLA Ops:
  1.7 5.0 %collective-permute-start = (f32[25,8,128]{2,1,0:T(8,128)S(1)}, f32[25,8,128]{2,1,0:T(8,128)S(1)}, u32[]{:S(2)}, u32[]{:S(2)}) collective-permute-start(f32[25,8,128]{2,1,0:T(8,128)S(1)} %get-tuple-element.18.own_ref), channel_id=1, source_target_pairs={{0,1},{2,3},{4,5},{6,7},{8,9},{10,11},{12,13},{14,15},{16,17},{18,... | collective-permute-start | bytes 307208 | tf_op jit(solution)/shard_map/ppermute | solution.py:356
  3.2 11.3 %collective-permute-start.1 = (f32[25,8,128]{2,1,0:T(8,128)S(1)}, f32[25,8,128]{2,1,0:T(8,128)S(1)}, u32[]{:S(2)}, u32[]{:S(2)}) collective-permute-start(f32[25,8,128]{2,1,0:T(8,128)S(1)} %get-tuple-element.18.own_ref), channel_id=1, source_target_pairs={{1,2},{3,4},{5,6},{7,8},{9,10},{11,12},{13,14},{15,16},{17,18},{19... | collective-permute-start | bytes 307208 | tf_op jit(solution)/shard_map/ppermute | solution.py:356
  6.8 16.9 %all-to-all-start = ((f32[32,1,2176]{2,1,0:T(1,128)}), f32[32,1,2176]{2,1,0:T(1,128)S(1)}, u32[]{:S(2)}, u32[]{:S(2)}) async-start(f32[32,1,2176]{2,1,0:T(1,128)} %bitcast.5), calls=%async_computation | async-start | bytes 557056 | tf_op jit(solution)/shard_map/all_to_all | solution.py:399
  14.7 10.9 %collective-permute-start.2 = (f32[11,16,128]{2,1,0:T(8,128)S(1)}, f32[11,16,128]{2,1,0:T(8,128)S(1)}, u32[]{:S(2)}, u32[]{:S(2)}) collective-permute-start(f32[11,16,128]{2,1,0:T(8,128)S(1)} %get-tuple-element.24), channel_id=1, source_target_pairs={{0,32},{64,96},{32,0},{96,64},{1,33},{65,97},{33,1},{97,65},{2,34}... | collective-permute-start | bytes 270344 | tf_op jit(solution)/shard_map/ppermute | solution.py:356
  15.9 9.6 %collective-permute-start.3 = (f32[11,16,128]{2,1,0:T(8,128)S(1)}, f32[11,16,128]{2,1,0:T(8,128)S(1)}, u32[]{:S(2)}, u32[]{:S(2)}) collective-permute-start(f32[11,16,128]{2,1,0:T(8,128)S(1)} %get-tuple-element.25), channel_id=1, source_target_pairs={{32,64},{64,32},{33,65},{65,33},{34,66},{66,34},{35,67},{67,35},{3... | collective-permute-start | bytes 270344 | tf_op jit(solution)/shard_map/ppermute | solution.py:356
